TPU v7x, 32 devices: a whole 2x2x4 slice. The times are simulated.
32 devices in a mesh: tm: 4 (over z), clip: 8 (over y, x, core).
Axes of the slice: x: 2, y: 2, z: 4, core: 2. Of those that a mesh axis runs over, the one named last changes fastest.
Arguments:
- tokens: bfloat16 [4, 128, 196, 384], P('tm', 'clip'), may hold values from -6 to 6
- cotangent: bfloat16 [4, 128, 196, 384], P('tm', 'clip'), may hold values from -6 to 6
- lane_frames: int32 [128], P('clip'), may hold values from 0 to 32, as said below
- pre_gain: bfloat16 [384], replicated, may hold values from 0.5 to 1.5
- pre_bias: bfloat16 [384], replicated, may hold values from -3 to 3
- w_project: bfloat16 [384, 1152], replicated, may hold values from -0.3125 to 0.3125
- query_bias: bfloat16 [384], replicated, may hold values from -3 to 3
- value_bias: bfloat16 [384], replicated, may hold values from -3 to 3
- w_out: bfloat16 [384, 384], replicated, may hold values from -1.25 to 1.25
- out_bias: bfloat16 [384], replicated, may hold values from -3 to 3
- mid_gain: bfloat16 [384], replicated, may hold values from 0.5 to 1.5
- mid_bias: bfloat16 [384], replicated, may hold values from -3 to 3
- w_up: bfloat16 [384, 1536], replicated, may hold values from -0.3125 to 0.3125
- up_bias: bfloat16 [1536], replicated, may hold values from -3 to 3
- w_down: bfloat16 [1536, 384], replicated, may hold values from -0.15625 to 0.15625
- down_bias: bfloat16 [384], replicated, may hold values from -3 to 3
Outputs:
- layer_output: bfloat16 [4, 128, 196, 384], P('tm', 'clip')
- input_grad: bfloat16 [4, 128, 196, 384], P('tm', 'clip')
- grad_pre_gain: float32 [384], replicated
- grad_pre_bias: float32 [384], replicated
- grad_w_project: float32 [384, 1152], replicated
- grad_query_bias: float32 [384], replicated
- grad_value_bias: float32 [384], replicated
- grad_w_out: float32 [384, 384], replicated
- grad_out_bias: float32 [384], replicated
- grad_mid_gain: float32 [384], replicated
- grad_mid_bias: float32 [384], replicated
- grad_w_up: float32 [384, 1536], replicated
- grad_up_bias: float32 [1536], replicated
- grad_w_down: float32 [1536, 384], replicated
- grad_down_bias: float32 [384], replicated
Inputs may be any that keep to these rules, and one draw needn't show every extreme that they name: `lane_frames`: each value is 0, 8, 16 or 32. A clip of f frames fills f / 8 consecutive lanes of one clip index, starting at a lane that is a multiple of f / 8 within that index's 16 lanes, and each of those lanes holds f; 0 marks an empty lane; the first lane of every clip index holds a clip.
All inputs are finite; a program needn't handle non-finite values.
Results may differ from a plain program's by a relative error of at most 0.012.
Values may be sent and summed in bfloat16 or wider, within the bound.
A program may use at most 320 MiB of HBM per device.

v0:
```python
import functools

import jax
import jax.numpy as jnp
from jax import lax
from jax.sharding import PartitionSpec as P

HEAD_DIM = 64


epsilon = 1e-06
masked_low = -1e30


def extended(value, sides, width):
    for axis, dim in sides:
        size, length = (lax.axis_size(axis), value.shape[dim])
        up = [(i, (i + 1) % size) for i in range(size)]
        down = [(j, i) for i, j in up]
        last = lax.slice_in_dim(value, length - width, length, axis=dim)
        initial = lax.slice_in_dim(value, 0, width, axis=dim)
        before = lax.ppermute(last, axis, up)
        after = lax.ppermute(initial, axis, down)
        value = jnp.concatenate([before, value, after], axis=dim)
    return value


def from_behind(value, axis, steps):
    count = lax.axis_size(axis)
    pairs = [(source, (source + steps) % count) for source in range(count)]
    return lax.ppermute(value, axis, pairs)


def layer_norm(inputs, norm_gain, norm_bias):
    center = inputs - jnp.mean(inputs, -1, keepdims=True)
    spread = jnp.mean(center * center, -1, keepdims=True)
    return center * lax.rsqrt(spread + epsilon) * norm_gain + norm_bias


def from_lower(lane_data, tm_index):
    return jnp.where(tm_index == 0, jnp.roll(lane_data, 1, 0), lane_data)


def from_upper(lane_data, tm_index, tm_count):
    return jnp.where(tm_index == tm_count - 1, jnp.roll(lane_data, -1, 0), lane_data)


def to_lower(lane_data, tm_index):
    return jnp.where(tm_index == 0, jnp.roll(lane_data, -1, 0), lane_data)


def to_upper(lane_data, tm_index, tm_count):
    return jnp.where(tm_index == tm_count - 1, jnp.roll(lane_data, 1, 0), lane_data)


def by_blocks(lane_data):
    return lane_data.reshape((lane_data.shape[0] // 4, 4) + lane_data.shape[1:])


def split_heads(rows):
    return rows.reshape(rows.shape[:2] + (rows.shape[2] // HEAD_DIM, HEAD_DIM))


def block_scores(queries, lower_kv, own_kv, upper_kv, lower_ok, upper_ok):
    features = queries.shape[-1]
    joined = jnp.concatenate([lower_kv, own_kv, upper_kv], 1)
    query_heads = split_heads(queries)
    key_heads = split_heads(joined[..., :features])
    value_heads = split_heads(joined[..., features:])
    scores = jnp.einsum(
        "bqhe,bkhe->bhqk", query_heads, key_heads, preferred_element_type=jnp.float32
    ) * HEAD_DIM ** (-0.5)
    full_rows = jnp.ones(queries.shape[:2], jnp.bool_)
    key_keep = jnp.concatenate(
        [lower_ok[:, None] & full_rows, full_rows, upper_ok[:, None] & full_rows], 1
    )
    scores = jnp.where(key_keep[:, None, None, :], scores, masked_low)
    return (scores, query_heads, key_heads, value_heads)


def attend(pieces):
    queries, lower_kv, own_kv, upper_kv, lower_ok, upper_ok = pieces
    scores, query_heads, key_heads, value_heads = block_scores(
        queries, lower_kv, own_kv, upper_kv, lower_ok, upper_ok
    )
    row_max = jnp.max(scores, -1, keepdims=True)
    log_total = row_max + jnp.log(jnp.sum(jnp.exp(scores - row_max), -1, keepdims=True))
    attn_probs = jnp.exp(scores - log_total).astype(jnp.bfloat16)
    attended = jnp.einsum(
        "bhqk,bkhe->bqhe", attn_probs, value_heads, preferred_element_type=jnp.float32
    )
    return (attended.reshape(queries.shape).astype(jnp.bfloat16), log_total[..., 0])


def attend_back(pieces, full_keys):
    queries, lower_kv, own_kv, upper_kv, lower_ok, upper_ok, log_total, grad_attended = pieces
    scores, query_heads, key_heads, value_heads = block_scores(
        queries, lower_kv, own_kv, upper_kv, lower_ok, upper_ok
    )
    attn_probs = jnp.exp(scores - log_total[..., None])
    grad_heads = split_heads(grad_attended)
    grad_probs = jnp.einsum(
        "bqhe,bkhe->bhqk", grad_heads, value_heads, preferred_element_type=jnp.float32
    )
    row_delta = jnp.sum(grad_probs * attn_probs, -1)
    grad_scores = (attn_probs * (grad_probs - row_delta[..., None])).astype(jnp.bfloat16)
    grad_queries = jnp.einsum(
        "bhqk,bkhe->bqhe", grad_scores, key_heads, preferred_element_type=jnp.float32
    ) * HEAD_DIM ** (-0.5)
    grad_keys = jnp.einsum(
        "bhqk,bqhe->bkhe", grad_scores, query_heads, preferred_element_type=jnp.float32
    ) * HEAD_DIM ** (-0.5)
    grad_values = jnp.einsum(
        "bhqk,bqhe->bkhe",
        attn_probs.astype(jnp.bfloat16),
        grad_heads,
        preferred_element_type=jnp.float32,
    )
    grad_kv = jnp.concatenate(
        [
            grad_keys.reshape(grad_keys.shape[:2] + (-1,)),
            grad_values.reshape(grad_values.shape[:2] + (-1,)),
        ],
        -1,
    )
    return (grad_queries.reshape(queries.shape), grad_kv, row_delta)


def body(
    tokens,
    cotangent,
    lane_frames,
    pre_gain,
    pre_bias,
    w_project,
    query_bias,
    value_bias,
    w_out,
    out_bias,
    mid_gain,
    mid_bias,
    w_up,
    up_bias,
    w_down,
    down_bias,
):
    lane_count, spatial, features = (tokens.shape[1], tokens.shape[2], tokens.shape[3])
    row_count = lane_count * spatial
    tm_count = lax.axis_size("tm")
    tm_index = lax.axis_index("tm")
    lane_span = jnp.maximum(lane_frames // (2 * tm_count), 1)
    lane_offset = jnp.arange(lane_count, dtype=jnp.int32) % lane_span
    occupied = lane_frames > 0
    lower_ok = occupied & ((tm_index > 0) | (lane_offset > 0))
    upper_ok = occupied & ((tm_index < tm_count - 1) | (lane_offset < lane_span - 1))
    row_keep = jnp.repeat(occupied, spatial)[:, None]
    pre_scale = pre_gain.astype(jnp.float32)
    pre_shift = pre_bias.astype(jnp.float32)
    mid_scale = mid_gain.astype(jnp.float32)
    mid_shift = mid_bias.astype(jnp.float32)
    flat_rows = tokens[0].astype(jnp.float32).reshape(row_count, features)
    normed = layer_norm(flat_rows, pre_scale, pre_shift).astype(jnp.bfloat16)
    projected = jnp.dot(normed, w_project, preferred_element_type=jnp.float32)
    queries = (projected[:, :features] + query_bias.astype(jnp.float32)).astype(jnp.bfloat16)
    key_rows = projected[:, features : 2 * features].astype(jnp.bfloat16)
    value_rows = (projected[:, 2 * features :] + value_bias.astype(jnp.float32)).astype(
        jnp.bfloat16
    )
    own_kv = jnp.concatenate([key_rows, value_rows], -1).reshape(lane_count, spatial, 2 * features)
    beside_all = extended(own_kv[None], (("tm", 0),), 1)
    lower_kv = from_lower(beside_all[0], tm_index)
    upper_kv = from_upper(beside_all[2], tm_index, tm_count)
    lane_queries = queries.reshape(lane_count, spatial, features)
    forward_in = (
        by_blocks(lane_queries),
        by_blocks(lower_kv),
        by_blocks(own_kv),
        by_blocks(upper_kv),
        by_blocks(lower_ok),
        by_blocks(upper_ok),
    )
    attended, log_total = lax.map(attend, forward_in)
    attended = attended.reshape(row_count, features)
    residual = (
        flat_rows
        + jnp.dot(attended, w_out, preferred_element_type=jnp.float32)
        + out_bias.astype(jnp.float32)
    )
    normed_two = layer_norm(residual, mid_scale, mid_shift).astype(jnp.bfloat16)
    hidden = jnp.dot(normed_two, w_up, preferred_element_type=jnp.float32) + up_bias.astype(
        jnp.float32
    )
    activated = jax.nn.gelu(hidden, approximate=False).astype(jnp.bfloat16)
    layer_sum = (
        residual
        + jnp.dot(activated, w_down, preferred_element_type=jnp.float32)
        + down_bias.astype(jnp.float32)
    )
    layer_output = (
        jnp.where(row_keep, layer_sum, flat_rows).astype(jnp.bfloat16).reshape(tokens.shape)
    )
    grad_rows = cotangent[0].astype(jnp.float32).reshape(row_count, features)
    grad_layer = jnp.where(row_keep, grad_rows, 0.0)
    grad_down_in = grad_layer.astype(jnp.bfloat16)
    grad_w_down = jnp.einsum(
        "rf,rd->fd", activated, grad_down_in, preferred_element_type=jnp.float32
    )
    grad_down_bias = jnp.sum(grad_down_in.astype(jnp.float32), 0)
    grad_act = jnp.einsum("rd,fd->rf", grad_down_in, w_down, preferred_element_type=jnp.float32)
    _, gelu_back = jax.vjp(functools.partial(jax.nn.gelu, approximate=False), hidden)
    grad_hidden = gelu_back(grad_act)[0].astype(jnp.bfloat16)
    grad_w_up = jnp.einsum("rd,rf->df", normed_two, grad_hidden, preferred_element_type=jnp.float32)
    grad_up_bias = jnp.sum(grad_hidden.astype(jnp.float32), 0)
    grad_normed_two = jnp.einsum("rf,df->rd", grad_hidden, w_up, preferred_element_type=jnp.float32)
    _, mid_back = jax.vjp(layer_norm, residual, mid_scale, mid_shift)
    grad_residual, grad_mid_gain, grad_mid_bias = mid_back(grad_normed_two)
    grad_residual = grad_residual + grad_layer
    grad_attn_out = grad_residual.astype(jnp.bfloat16)
    grad_w_out = jnp.einsum(
        "rd,re->de", attended, grad_attn_out, preferred_element_type=jnp.float32
    )
    grad_out_bias = jnp.sum(grad_attn_out.astype(jnp.float32), 0)
    grad_attended = jnp.einsum(
        "re,de->rd", grad_attn_out, w_out, preferred_element_type=jnp.float32
    ).astype(jnp.bfloat16)
    lane_grads = grad_attended.reshape(lane_count, spatial, features)
    back_in = forward_in + (log_total, by_blocks(lane_grads))
    grad_queries, window_grads, row_delta = lax.map(
        functools.partial(attend_back, full_keys=True), back_in
    )
    window_grads = window_grads.reshape(lane_count, 3 * spatial, 2 * features)
    from_above = from_behind(
        to_lower(window_grads[:, :spatial], tm_index).astype(jnp.bfloat16), "tm", -1
    ).astype(jnp.float32)
    from_below = from_behind(
        to_upper(window_grads[:, 2 * spatial :], tm_index, tm_count).astype(jnp.bfloat16), "tm", 1
    ).astype(jnp.float32)
    kv_grads = (window_grads[:, spatial : 2 * spatial] + from_above + from_below).reshape(
        row_count, 2 * features
    )
    grad_project_in = jnp.concatenate(
        [
            grad_queries.reshape(row_count, features).astype(jnp.bfloat16),
            kv_grads.astype(jnp.bfloat16),
        ],
        -1,
    )
    grad_w_project = jnp.einsum(
        "rd,rc->dc", normed, grad_project_in, preferred_element_type=jnp.float32
    )
    grad_query_bias = jnp.sum(grad_project_in[:, :features].astype(jnp.float32), 0)
    grad_value_bias = jnp.sum(grad_project_in[:, 2 * features :].astype(jnp.float32), 0)
    grad_normed = jnp.einsum(
        "rc,dc->rd", grad_project_in, w_project, preferred_element_type=jnp.float32
    )
    _, pre_back = jax.vjp(layer_norm, flat_rows, pre_scale, pre_shift)
    grad_flat, grad_pre_gain, grad_pre_bias = pre_back(grad_normed)
    input_grad = (grad_flat + grad_residual + jnp.where(row_keep, 0.0, grad_rows)).astype(
        jnp.bfloat16
    )
    input_grad = input_grad.reshape(tokens.shape)
    summed = tuple(
        lax.psum(
            (
                grad_pre_gain,
                grad_pre_bias,
                grad_w_project,
                grad_query_bias,
                grad_value_bias,
                grad_w_out,
                grad_out_bias,
                grad_mid_gain,
                grad_mid_bias,
                grad_w_up,
                grad_up_bias,
                grad_w_down,
                grad_down_bias,
            ),
            ("tm", "clip"),
        )
    )
    return (layer_output, input_grad) + summed


def solution(mesh):
    placed = (
        P("tm", "clip", None, None),
        P("tm", "clip", None, None),
        P("clip"),
        P(),
        P(),
        P(),
        P(),
        P(),
        P(),
        P(),
        P(),
        P(),
        P(),
        P(),
        P(),
        P(),
    )
    return jax.shard_map(
        body,
        mesh=mesh,
        in_specs=placed,
        out_specs=(
            P("tm", "clip", None, None),
            P("tm", "clip", None, None),
            P(),
            P(),
            P(),
            P(),
            P(),
            P(),
            P(),
            P(),
            P(),
            P(),
            P(),
            P(),
            P(),
        ),
        check_vma=False,
    )
```

profile of v0, /device:TPU:0, one launch (start us, length us, event | category | flops | bytes accessed | tf_op | source)
XLA Modules:
  0.0 1166.1 jit_solution(14740012308335085718)
XLA Ops:
  9.8 4.5 copy.115
  16.9 5.3 reshape.255
  22.1 7.1 fusion.41
  34.3 7.2 broadcast_in_dim_reshape.4
  41.5 5.5 copy.119
  47.0 5.1 collective-permute-start.1
  52.4 7.2 reshape_reshape.9
  63.8 4.3 copy.132
  68.1 5.2 reshape.256
  77.4 4.5 copy.130
  81.9 8.1 copy.129
  92.9 63.8 %collective-permute-done.1 = bf16[1,16,196,768]{3,1,2,0:T(8,128)(2,1)} collective-permute-done((bf16[1,16,196,768]{3,1,2,0:T(8,128)(2,1)}, bf16[1,16,196,768]{3,1,2,0:T(8,128)(2,1)}, u32[]{:S(2)}, u32[]{:S(2)}) %collective-permute-start.1) | collective-permute-done | bytes 4816928 | tf_op jit(solution)/shard_map/ppermute | solution.py:23
  159.3 4.9 slice_bitcast_fusion
  167.9 9.4 copy.143
  177.3 82.4 %collective-permute-done = bf16[1,16,196,768]{3,1,2,0:T(8,128)(2,1)} collective-permute-done((bf16[1,16,196,768]{3,1,2,0:T(8,128)(2,1)}, bf16[1,16,196,768]{3,1,2,0:T(8,128)(2,1)}, u32[]{:S(2)}, u32[]{:S(2)}) %collective-permute-start) | collective-permute-done | bytes 4816928 | tf_op jit(solution)/shard_map/ppermute | solution.py:22
  265.2 4.6 pad_maximum_fusion.3
  269.8 9.1 copy.141
  278.9 9.1 copy.144
  288.1 9.1 copy.142
  297.2 10.4 broadcast_select_fusion
  307.6 78.4 %while.24 = (s32[]{:T(128)}, bf16[4,4,196,384]{3,2,1,0:T(8,128)(2,1)}, f32[4,4,6,196]{3,2,1,0:T(8,128)}, bf16[4,4,196,768]{2,3,1,0:T(8,128)(2,1)}, bf16[4,4,196,...) while((s32[]{:T(128)}, ...), condition=%wide.region_5.6_spmd, body=%wide.region_2.5_spmd.sunk | while | flops 749648256 | bytes 63488076 | solution.py:182
  386.0 4.1 reshape.251
  390.1 5.1 fusion.52
  396.5 48.4 %multiply_convert_fusion.1 = (bf16[3136,1536]{1,0:T(8,128)(2,1)}, f32[3136,1536]{1,0:T(8,128)}, f32[3136,1536]{1,0:T(8,128)}) fusion(f32[1536]{0:T(1024)S(1)} %copy-done.43, bf16[384,1536]{1,0:T(8,128)(2,1)S(1)} %copy-done, f32[3136,384]{1,0:T(8,128)S(1)} %get-tuple-element.397, f32[384]{0:T(512)S(1)} %copy-done.49, f32[384]{0:T(512)S(1)} %copy-done.44, ...), kind=kOutput, calls=%fused_computation.54 | convolution fusion | flops 4023312384 | bytes 54199808 | tf_op jit(solution)/shard_map/dot_general | solution.py:190
  444.9 22.9 %convert_reduce_fusion = (f32[1536]{0:T(1024)}, bf16[3136,1536]{1,0:T(8,128)(2,1)}) fusion(f32[3136,1536]{1,0:T(8,128)} %get-tuple-element.368, bf16[1536,384]{1,0:T(8,128)(2,1)S(1)} %copy-done.61, f32[3136,384]{1,0:T(8,128)} %reshape.256, pred[3136]{0:T(1024)(128)(4,1)S(1)} %copy-done.33, f32[3136,1536]{1,0:T(8,128)} %get-tuple-element.398, ...), kind=kOutput, calls=%fused_computation.52 | convolution fusion | flops 3782466048 | bytes 54180928 | tf_op jit(solution)/shard_map/rd,fd->rf/dot_general | solution.py:209
  467.8 11.2 multiply_reduce_fusion.1
  489.1 4.1 reshape_reshape.11
  493.2 168.3 %while.25 = (s32[]{:T(128)}, bf16[4,4,196,384]{2,3,1,0:T(8,128)(2,1)}, f32[4,4,588,768]{2,3,1,0:T(8,128)}, bf16[4,4,196,768]{2,3,1,0:T(8,128)(2,1)}, bf16[4,4,19...) while((s32[]{:T(128)}, ...), condition=%wide.region_12.13_spmd, body=%wide.region_10.12_spmd.sunk | while | flops 1825848192 | bytes 142954880 | solution.py:228
  511.7 8.4 multiply_reduce_fusion.8
  520.1 6.8 multiply_convert_fusion.3
  553.7 8.4 multiply_reduce_fusion.8
  562.1 6.8 multiply_convert_fusion.3
  595.7 8.4 multiply_reduce_fusion.8
  604.1 6.8 multiply_convert_fusion.3
  637.8 8.4 multiply_reduce_fusion.8
  646.2 6.8 multiply_convert_fusion.3
  663.0 14.0 %fusion.49 = (bf16[15,196,768]{1,2,0:T(8,128)(2,1)}, bf16[15,196,768]{1,2,0:T(8,128)(2,1)}) fusion(f32[16,588,768]{1,2,0:T(8,128)} %bitcast.179), kind=kLoop, calls=%fused_computation.144 | loop fusion | bytes 18063360 | tf_op jit(solution)/shard_map/jit(_roll_static)/slice | solution.py:49
  677.0 14.4 %fusion.51 = (bf16[16,196,768]{1,2,0:T(8,128)(2,1)}, bf16[16,196,768]{1,2,0:T(8,128)(2,1)}) fusion(f32[16,588,768]{1,2,0:T(8,128)} %bitcast.180), kind=kLoop, calls=%fused_computation.146 | loop fusion | bytes 19267584 | tf_op jit(solution)/shard_map/slice | solution.py:233
  693.2 8.7 copy.152
  701.9 8.7 copy.156
  710.6 8.7 copy.154
  719.3 8.9 copy.157
  728.2 9.2 fusion.27
  739.1 4.8 fusion.26
  743.9 4.6 collective-permute-start.2
  748.5 10.2 fusion.31
  758.7 14.3 %slice.112 = f32[16,196,768]{1,2,0:T(8,128)} slice(f32[16,588,768]{1,2,0:T(8,128)} %bitcast.181), slice={[0:16], [196:392], [0:768]} | slice | bytes 19267584 | tf_op jit(solution)/shard_map/slice | solution.py:238
  780.5 4.5 copy.136
  789.1 12.5 %copy.151 = f32[16,196,768]{2,0,1:T(8,128)} copy(f32[16,196,768]{1,2,0:T(8,128)} %slice.112) | data formatting | bytes 19267584
  804.3 4.9 fusion.54
  811.0 10.3 fusion.38
  821.4 7.0 fusion.37
  828.3 18.1 %collective-permute-done.3 = bf16[16,196,768]{2,0,1:T(8,128)(2,1)} collective-permute-done((bf16[16,196,768]{2,0,1:T(8,128)(2,1)}, bf16[16,196,768]{2,0,1:T(8,128)(2,1)}, u32[]{:S(2)}, u32[]{:S(2)}) %collective-permute-start.3) | collective-permute-done | bytes 4816928 | tf_op jit(solution)/shard_map/ppermute | solution.py:31
  846.5 101.1 %collective-permute-done.2 = bf16[16,196,768]{2,0,1:T(8,128)(2,1)} collective-permute-done((bf16[16,196,768]{2,0,1:T(8,128)(2,1)}, bf16[16,196,768]{2,0,1:T(8,128)(2,1)}, u32[]{:S(2)}, u32[]{:S(2)}) %collective-permute-start.2) | collective-permute-done | bytes 4816928 | tf_op jit(solution)/shard_map/ppermute | solution.py:31
  947.6 10.9 add_convert_fusion.1
  958.5 6.2 copy.138
  964.7 7.2 convert_element_type.183
  971.9 4.9 constant_dynamic-update-slice_fusion.2
  976.8 9.5 fusion.40
  987.5 11.0 multiply_reduce_fusion.2
  1001.5 7.2 add_convert_fusion.2
  1008.7 4.1 reshape.254
  1018.5 40.1 %all-reduce = (f32[384]{0:T(512)}, f32[384]{0:T(512)}, f32[384]{0:T(512)}, f32[384]{0:T(512)}, f32[384]{0:T(512)}, /*index=5*/f32[384]{0:T(512)}, f32[384]{0:T(512)}, f32[1536]{0:T(1024)}, f32[384]{0:T(512)}) all-reduce(f32[384]{0:T(512)S(1)} %get-tuple-element.302, ...), channel_id=1, replica_groups=mesh['tm'=4,'clip'=8] {'tm','clip'}, use_global_device_ids=true, to_apply=%region_16.17 | all-reduce | flops 4608 | bytes 36864 | tf_op jit(solution)/shard_map/psum | solution.py:263
  1058.5 92.5 %all-reduce.4.cloned.1.call-done = (f32[384,1152]{1,0:T(8,128)}, f32[384,384]{1,0:T(8,128)}, f32[384,1536]{1,0:T(8,128)}, f32[1536,384]{1,0:T(8,128)}) async-done(((f32[384,1152]{1,0:T(8,128)}, f32[384,384]{1,0:T(8,128)}, f32[384,1536]{1,0:T(8,128)}, f32[1536,384]{1,0:T(8,128)}), (f32[384,1152]{1,0:T(8,128)}, f32[384,384]{1,0:T(8,128)}, f32[384,1536]{1,0:T(8,128)}, ...) | async-done | bytes 7077904 | tf_op jit(solution)/shard_map/psum | solution.py:263
  (386 shorter events, 267.8 us)
Async XLA Ops:
  7.2 389.3 %copy-start = (bf16[384,1536]{1,0:T(8,128)(2,1)S(1)}, bf16[384,1536]{1,0:T(8,128)(2,1)}, u32[]{:S(2)}) copy-start(bf16[384,1536]{1,0:T(8,128)(2,1)} %param.32) | copy-start | bytes 3538948
  7.2 7.2 copy-start.53
  7.2 7.2 copy-start.54
  7.2 7.2 copy-start.55
  7.2 7.2 copy-start.56
  7.2 1143.8 %all-reduce.4.cloned.1.call-start = ((), (), s32[]{:S(2)}) async-start(), calls=%async_computation | async-start | bytes 14155776 | tf_op jit(solution)/shard_map/psum | solution.py:263
  9.7 12.4 %copy-start.19 = (f32[3136]{0:T(1024)}, f32[3136]{0:T(1024)S(1)}, u32[]{:S(2)}) copy-start(f32[3136]{0:T(1024)S(1)} %div.55) | copy-start | bytes 37636
  14.4 7.8 copy-start.35
  14.4 7.7 copy-start.37
  16.9 5.3 copy-start.21
  16.9 5.3 copy-start.13
  47.0 109.7 %collective-permute-start.1 = (bf16[1,16,196,768]{3,1,2,0:T(8,128)(2,1)}, bf16[1,16,196,768]{3,1,2,0:T(8,128)(2,1)}, u32[]{:S(2)}, u32[]{:S(2)}) collective-permute-start(bf16[1,16,196,768]{3,1,2,0:T(8,128)(2,1)} %copy.119), channel_id=1, source_target_pairs={{8,0},{16,8},{24,16},{0,24},{9,1},{17,9},{25,17},{1,25},{10,2},{18... | collective-permute-start | bytes 14450696 | tf_op jit(solution)/shard_map/ppermute | solution.py:23
  52.1 207.6 %collective-permute-start = (bf16[1,16,196,768]{3,1,2,0:T(8,128)(2,1)}, bf16[1,16,196,768]{3,1,2,0:T(8,128)(2,1)}, u32[]{:S(2)}, u32[]{:S(2)}) collective-permute-start(bf16[1,16,196,768]{3,1,2,0:T(8,128)(2,1)} %copy.119), channel_id=1, source_target_pairs={{0,8},{8,16},{16,24},{24,0},{1,9},{9,17},{17,25},{25,1},{2,10},{10... | collective-permute-start | bytes 14450696 | tf_op jit(solution)/shard_map/ppermute | solution.py:22
  52.3 7.3 copy-start.52
  52.4 7.7 copy-start.57
  52.4 8.3 copy-start.58
  52.4 8.8 copy-start.59
  52.4 9.4 copy-start.60
  52.4 10.8 copy-start.46
  386.0 9.3 copy-start.29
  386.0 9.3 copy-start.31
  395.2 83.8 %copy-start.3 = (f32[3136,384]{1,0:T(8,128)}, f32[3136,384]{1,0:T(8,128)S(1)}, u32[]{:S(2)}) copy-start(f32[3136,384]{1,0:T(8,128)S(1)} %get-tuple-element.397) | copy-start | bytes 14450692
  395.3 83.7 %copy-start.25 = (f32[3136]{0:T(1024)}, f32[3136]{0:T(1024)S(1)}, u32[]{:S(2)}) copy-start(f32[3136]{0:T(1024)S(1)} %broadcast_multiply_fusion) | copy-start | bytes 37636
  396.4 48.5 %copy-start.15 = (f32[3136]{0:T(1024)}, f32[3136]{0:T(1024)S(1)}, u32[]{:S(2)}) copy-start(f32[3136]{0:T(1024)S(1)} %multiply_reduce_fusion.5) | copy-start | bytes 37636
  396.5 82.6 %copy-start.27 = (f32[3136]{0:T(1024)}, f32[3136]{0:T(1024)S(1)}, u32[]{:S(2)}) copy-start(f32[3136]{0:T(1024)S(1)} %fusion.35) | copy-start | bytes 37636
  396.5 48.4 %copy-start.33 = (pred[3136]{0:T(1024)(128)(4,1)S(1)}, pred[3136]{0:T(1024)(128)(4,1)}, u32[]{:S(2)}) copy-start(pred[3136]{0:T(1024)(128)(4,1)} %broadcast_in_dim.121) | copy-start | bytes 9412
  396.5 48.4 %copy-start.61 = (bf16[1536,384]{1,0:T(8,128)(2,1)S(1)}, bf16[1536,384]{1,0:T(8,128)(2,1)}, u32[]{:S(2)}) copy-start(bf16[1536,384]{1,0:T(8,128)(2,1)} %param.34) | copy-start | bytes 3538948
  467.8 11.2 copy-start.16
  486.0 7.1 copy-start.30
  486.0 7.1 copy-start.32
  719.3 19.8 %slice-start.10 = ((s8[4816896]{0:T(1024)(128)(4,1)}), s8[622592]{0:T(1024)(128)(4,1)S(1)}, s32[]{:S(2)}) async-start(s8[4816896]{0:T(1024)(128)(4,1)} %bitcast.189), calls=%async_computation.11 | async-start | bytes 1245184
  728.2 10.9 slice-start.11
  728.2 20.3 %slice-start = ((s8[4816896]{0:T(1024)(128)(4,1)}), s8[622592]{0:T(1024)(128)(4,1)S(1)}, s32[]{:S(2)}) async-start(s8[4816896]{0:T(1024)(128)(4,1)} %bitcast.167), calls=%async_computation.1 | async-start | bytes 1245184
  728.2 20.3 %slice-start.4 = ((s8[4816896]{0:T(1024)(128)(4,1)}), s8[4194304]{0:T(1024)(128)(4,1)S(1)}, s32[]{:S(2)}) async-start(s8[4816896]{0:T(1024)(128)(4,1)} %bitcast.173), calls=%async_computation.5 | async-start | bytes 8388608
  737.4 11.0 slice-start.1
  737.4 11.0 slice-start.5
  737.4 11.1 copy-start.34
  737.4 11.1 copy-start.51
  737.4 109.1 %collective-permute-start.3 = (bf16[16,196,768]{2,0,1:T(8,128)(2,1)}, bf16[16,196,768]{2,0,1:T(8,128)(2,1)}, u32[]{:S(2)}, u32[]{:S(2)}) collective-permute-start(bf16[16,196,768]{2,0,1:T(8,128)(2,1)} %fusion.27), channel_id=1, source_target_pairs={{0,8},{8,16},{16,24},{24,0},{1,9},{9,17},{17,25},{25,1},{2,10},{10... | collective-permute-start | bytes 14450696 | tf_op jit(solution)/shard_map/ppermute | solution.py:31
  743.9 203.7 %collective-permute-start.2 = (bf16[16,196,768]{2,0,1:T(8,128)(2,1)}, bf16[16,196,768]{2,0,1:T(8,128)(2,1)}, u32[]{:S(2)}, u32[]{:S(2)}) collective-permute-start(bf16[16,196,768]{2,0,1:T(8,128)(2,1)} %fusion.26), channel_id=1, source_target_pairs={{0,24},{8,0},{16,8},{24,16},{1,25},{9,1},{17,9},{25,17},{2,26},{10... | collective-permute-start | bytes 14450696 | tf_op jit(solution)/shard_map/ppermute | solution.py:31
  801.6 7.7 copy-start.8
  801.6 9.3 slice-start.6
  804.2 6.7 slice-start.7
  804.2 6.7 copy-start.26
  804.3 6.7 copy-start.28
  804.3 6.7 copy-start.45
  804.3 6.7 copy-start.50
  809.2 12.1 %slice-start.8 = ((s8[4816896]{0:T(1024)(128)(4,1)}), s8[4194304]{0:T(1024)(128)(4,1)S(1)}, s32[]{:S(2)}) async-start(s8[4816896]{0:T(1024)(128)(4,1)} %bitcast.182), calls=%async_computation.9 | async-start | bytes 8388608
  809.2 12.1 %slice-start.12 = ((s8[9633792]{0:T(1024)(128)(4,1)}), s8[4194304]{0:T(1024)(128)(4,1)S(1)}, s32[]{:S(2)}) async-start(s8[9633792]{0:T(1024)(128)(4,1)} %bitcast.193), calls=%async_computation.13 | async-start | bytes 8388608
  811.0 10.4 slice-start.9
  811.0 10.4 slice-start.13
  811.0 10.4 slice-start.14
  971.9 4.9 copy-start.36
  971.9 4.9 copy-start.38
  986.3 12.2 %slice-start.2 = ((s8[4816896]{0:T(1024)(128)(4,1)}), s8[622592]{0:T(1024)(128)(4,1)S(1)}, s32[]{:S(2)}) async-start(s8[4816896]{0:T(1024)(128)(4,1)} %bitcast.169), calls=%async_computation.3 | async-start | bytes 1245184
  987.5 11.0 copy-start.18
  987.5 11.1 slice-start.3
  1012.7 5.7 copy-start.40
  1012.7 5.7 copy-start.41
  1012.8 5.7 copy-start.42
  1012.8 5.7 copy-start.47
  1012.8 5.7 copy-start.48
  1151.0 5.0 copy-start.10
  1151.0 6.4 copy-start.9
  (21 other events, 58.0 us)
Sparse Core Ops, SparseCore 0:
  986.5 164.4 all-reduce.3
where the time goes:
time: 1180 us; the launch traced here: 1170 us
  waiting for transfers between devices  358 us (30%)
  local copies, waits for them, and re-layouts  333 us (28%)
  matrix products  249 us (21%)
  other arithmetic  159 us (13%)
  blocking collectives  40.1 us (3%)
  between operations  15.5 us (1%)
    ppermute x2, waiting for transfers between devices, from_behind(): return lax.ppermute(value, axis, pairs)  119 us
    psum x1, waiting for transfers between devices, body(): lax.psum((grad_pre_gain, grad_pre_bias, grad_w_project, grad_query_bias,...  92.5 us
    ppermute x1, waiting for transfers between devices, extended(): before = lax.ppermute(last, axis, up)  82.4 us
    unnamed x168, local copies, waits for them, and re-layouts  69.2 us
    ppermute x1, waiting for transfers between devices, extended(): after = lax.ppermute(initial, axis, down)  63.8 us
    dot_general x1, matrix products, body(): jnp.dot(normed_two, w_up, preferred_element_type=jnp.float32)  48.4 us
    psum x1, blocking collectives, body(): lax.psum((grad_pre_gain, grad_pre_bias, grad_w_project, grad_query_bias,...  40.1 us
    dot_general x4, matrix products, attend_back(): jnp.einsum('bqhe,bkhe->bhqk', grad_heads, value_heads, preferred_element_...  33.6 us
  transfers between devices with their start and end apart: 5, of which 5 were waited for; matrix products, arithmetic and copies ran while one was open for 15% of the time, Pallas kernels for 0%

commit v1 on v0

v1 whole, which is shorter than its diff:
```python
import functools

import jax
import jax.numpy as jnp
from jax import lax
from jax.experimental import pallas as pl
from jax.experimental.pallas import tpu as pltpu
from jax.sharding import PartitionSpec as P

HEAD_DIM = 64
GROUP = 4
EPSILON = 1e-06
FAR = 1e30
F32 = jnp.float32
BF16 = jnp.bfloat16
NN = (((1,), (0,)), ((), ()))
NT = (((1,), (1,)), ((), ()))
TN = (((0,), (0,)), ((), ()))


def dot(a, b, dims=NN):
    return lax.dot_general(a, b, dims, preferred_element_type=F32)


def row_mean(value):
    return jnp.sum(value, -1, keepdims=True) * (1.0 / value.shape[-1])


def normalise(x):
    center = x - row_mean(x)
    rate = lax.rsqrt(row_mean(center * center) + EPSILON)
    return center * rate, rate


def norm_back(grad, xhat, rate, gain):
    e = grad * gain
    return rate * (e - row_mean(e) - xhat * row_mean(e * xhat))


def gelu_parts(h):
    bell = jnp.exp(-0.5 * (h * h))
    t = 1.0 / (1.0 + 0.23164190 * jnp.abs(h))
    poly = t * (0.127414796 + t * (-0.142248368 + t * (0.7107068705 + t * (-0.7265760135 + t * 0.5307027145))))
    tail = poly * bell
    phi = jnp.where(h >= 0.0, 1.0 - tail, tail)
    return h * phi, phi + h * (bell * 0.3989422804014327)


def column_sum(value):
    return jnp.sum(value, 0, keepdims=True)


def block_kernel(
    first, spatial, features, hidden, tm_count,
    tm_ref, low_ok_ref, up_ok_ref, full_ref,
    tok_ref, low_ref, low_wrap_ref, up_ref, up_wrap_ref, cot_ref,
    pre_gain_ref, pre_bias_ref, wq_t_ref, w_project_ref, query_bias_ref, value_bias_ref,
    w_out_ref, out_bias_ref, mid_gain_ref, mid_bias_ref, w_up_ref, up_bias_ref, w_down_ref, down_bias_ref,
    *rest,
):
    count = 6
    if first:
        olds = (None,) * count
        rest = rest[0:]
    else:
        olds = rest[:count]
        rest = rest[count + 2 :]
    (out_ref, own_ref, gl_ref, gu_ref, a_project, a_out, a_up, a_down, a_small, a_upb) = rest[:10]
    (n1_s, k_s, v_s, kt_s, vt_s, qt_s, p_s, inv_s, att_s, attt_s, res_s, n2_s, act_s, gh_s, dao_s, dres_s, dq_s, dkv_s, dt_s) = rest[10:]
    f = features
    pad = n1_s.shape[1] // GROUP
    heads = f // HEAD_DIM
    tm = tm_ref[0]
    at_low, at_high = tm == 0, tm == tm_count - 1
    pre_gain, pre_bias = pre_gain_ref[...], pre_bias_ref[...]
    mid_gain, mid_bias = mid_gain_ref[...], mid_bias_ref[...]

    for old, new in zip(olds, (a_project, a_out, a_up, a_down, a_small, a_upb)):
        if old is None:
            new[...] = jnp.zeros_like(new)
        else:
            new[...] = old[...]

    def neighbour_rows(j):
        below = jnp.where(at_low, low_wrap_ref[0, jnp.maximum(j - 1, 0)].astype(F32), low_ref[0, j].astype(F32))
        above = jnp.where(at_high, up_wrap_ref[0, jnp.minimum(j, GROUP - 2)].astype(F32), up_ref[0, j].astype(F32))
        return below, above

    def rows_of(j):
        return pl.ds(pl.multiple_of(j * pad, pad), spatial)

    for ref in (n1_s, att_s, dao_s, dq_s, dkv_s, res_s, dres_s):
        for j in range(GROUP):
            if len(ref.shape) == 3:
                ref[:, pl.ds(j * pad + pad - 16, 16), :] = jnp.zeros((ref.shape[0], 16, ref.shape[2]), ref.dtype)
            else:
                ref[pl.ds(j * pad + pad - 16, 16), :] = jnp.zeros((16, ref.shape[1]), ref.dtype)

    def forward(j, carry):
        below, above = neighbour_rows(j)
        for s, x in enumerate((below, tok_ref[0, j].astype(F32), above)):
            xhat, _ = normalise(x)
            n1 = (xhat * pre_gain + pre_bias).astype(BF16)
            n1_s[s, rows_of(j), :] = n1
            kv = dot(n1, w_project_ref[:, f:])
            k = kv[:, :f].astype(BF16)
            v = (kv[:, f:] + value_bias_ref[...]).astype(BF16)
            k_s[s, j] = k
            v_s[s, j] = v
            kt_s[s, j] = k.T
            vt_s[s, j] = v.T
            if s == 1:
                qt = (dot(wq_t_ref[...], n1, NT) + query_bias_ref[...]).astype(BF16)
                qt_s[j] = qt * jnp.asarray(HEAD_DIM ** (-0.5), BF16)
        low_ok, up_ok = low_ok_ref[j] > 0, up_ok_ref[j] > 0
        low_far, up_far = jnp.where(low_ok, 0.0, FAR), jnp.where(up_ok, 0.0, FAR)
        zero_half = jnp.zeros((HEAD_DIM, spatial), BF16)
        for h in range(heads):
            pair = slice(h // 2 * 2 * HEAD_DIM, (h // 2 + 1) * 2 * HEAD_DIM)
            mine = slice(h * HEAD_DIM, (h + 1) * HEAD_DIM)
            qh = qt_s[j, mine, :]
            qz = jnp.concatenate([qh, zero_half] if h % 2 == 0 else [zero_half, qh], 0)
            scores = [dot(k_s[s, j, :, pair], qz) for s in range(3)]
            tops = [jnp.max(x, 0, keepdims=True) for x in scores]
            top = jnp.maximum(jnp.maximum(tops[0] - low_far, tops[2] - up_far), tops[1])
            total, attended = None, None
            for s, shift in enumerate((top + low_far, top, top + up_far)):
                prob = jnp.exp(scores[s] - shift)
                part = column_sum(prob)
                total = part if total is None else total + part
                low_prob = prob.astype(BF16)
                p_s[j, h, s] = low_prob
                got = dot(vt_s[s, j, mine, :], low_prob)
                attended = got if attended is None else attended + got
            inverse = 1.0 / total
            inv_s[j, h : h + 1, :] = inverse
            attt_s[j, mine, :] = (attended * inverse).astype(BF16)
        att_s[rows_of(j), :] = attt_s[j].T
        res_s[rows_of(j), :] = tok_ref[0, j].astype(F32)
        return carry

    lax.fori_loop(0, GROUP, forward, 0)

    residual = res_s[...] + dot(att_s[...], w_out_ref[...]) + out_bias_ref[...]
    res_s[...] = residual
    xhat2, rate2 = normalise(residual)
    n2_s[...] = (xhat2 * mid_gain + mid_bias).astype(BF16)
    for j in range(GROUP):
        full = full_ref[j] > 0
        g = cot_ref[0, j]
        dao_s[pl.ds(j * pad, spatial), :] = jnp.where(full, g.astype(F32), 0.0).astype(BF16)

    wide = 256

    def mlp(c, carry):
        cols = pl.ds(pl.multiple_of(c * wide, wide), wide)
        h = dot(n2_s[...], w_up_ref[:, cols]) + up_bias_ref[:, cols]
        act, slope = gelu_parts(h)
        act_s[:, cols] = act.astype(BF16)
        gh = (dot(dao_s[...], w_down_ref[cols, :], NT) * slope).astype(BF16)
        gh_s[:, cols] = gh
        a_upb[:, cols] += column_sum(gh.astype(F32))
        return carry

    lax.fori_loop(0, hidden // wide, mlp, 0)
    a_up[...] += dot(n2_s[...], gh_s[...], TN)
    a_down[...] += dot(dao_s[...], act_s[...], TN)
    total_out = dot(act_s[...], w_down_ref[...]) + down_bias_ref[...] + res_s[...]
    grad_n2 = dot(gh_s[...], w_up_ref[...], NT)
    for j in range(GROUP):
        full = full_ref[j] > 0
        mine = total_out[j * pad : j * pad + spatial]
        out_ref[0, j] = jnp.where(full, mine, tok_ref[0, j].astype(F32)).astype(BF16)
    g = dao_s[...].astype(F32)
    xhat2, rate2 = normalise(res_s[...])
    dres = g + norm_back(grad_n2, xhat2, rate2, mid_gain)
    dres_s[...] = dres
    dao = dres.astype(BF16)
    dao_s[...] = dao
    a_small[3:4, :] += column_sum(dao.astype(F32))
    a_small[4:5, :] += column_sum(grad_n2 * xhat2)
    a_small[5:6, :] += column_sum(grad_n2)
    a_small[6:7, :] += column_sum(g)
    a_out[...] += dot(att_s[...], dao, TN)

    def backward(j, carry):
        dot_rows = dao_s[rows_of(j), :]
        dt = dot(w_out_ref[...], dot_rows, NT).astype(BF16)
        zero_half = jnp.zeros((HEAD_DIM, spatial), BF16)
        for h in range(heads):
            pair = slice(h // 2 * 2 * HEAD_DIM, (h // 2 + 1) * 2 * HEAD_DIM)
            mine = slice(h * HEAD_DIM, (h + 1) * HEAD_DIM)
            dh = dt[mine, :].astype(F32) * inv_s[j, h : h + 1, :]
            delta = column_sum(dh * attt_s[j, mine, :].astype(F32))
            dh = dh.astype(BF16)
            dz = jnp.concatenate([dh, zero_half] if h % 2 == 0 else [zero_half, dh], 0)
            qh = qt_s[j, mine, :]
            grad_q = None
            for s in range(3):
                prob = p_s[j, h, s]
                grad_prob = dot(v_s[s, j, :, pair], dz)
                grad_score = (prob.astype(F32) * (grad_prob - delta)).astype(BF16)
                dt_s[1 + s, mine, :] = dot(qh, grad_score, NT).astype(BF16)
                dt_s[4 + s, mine, :] = dot(dh, prob, NT).astype(BF16)
                got = dot(kt_s[s, j, mine, :], grad_score)
                grad_q = got if grad_q is None else grad_q + got
            dt_s[0, mine, :] = (grad_q * HEAD_DIM ** (-0.5)).astype(BF16)
        dq_s[rows_of(j), :] = dt_s[0].T
        for s in range(3):
            dkv_s[s, rows_of(j), :f] = dt_s[1 + s].T
            dkv_s[s, rows_of(j), f:] = dt_s[4 + s].T
        return carry

    lax.fori_loop(0, GROUP, backward, 0)

    dq = dq_s[...]
    a_project[:, :f] += dot(n1_s[1], dq, TN)
    a_small[2:3, :] += column_sum(dq.astype(F32))
    for s in range(3):
        dkv = dkv_s[s]
        a_project[:, f:] += dot(n1_s[s], dkv, TN)
        a_small[7:8, :] += column_sum(dkv[:, f:].astype(F32))

    def finish(j, carry):
        below, above = neighbour_rows(j)
        for s, x in enumerate((below, tok_ref[0, j].astype(F32), above)):
            grad = dot(dkv_s[s, rows_of(j), :], w_project_ref[:, f:], NT)
            if s == 1:
                grad += dot(dq_s[rows_of(j), :], w_project_ref[:, :f], NT)
            xhat, rate = normalise(x)
            a_small[0:1, :] += column_sum(grad * xhat)
            a_small[1:2, :] += column_sum(grad)
            back = norm_back(grad, xhat, rate, pre_gain)
            if s == 1:
                straight = jnp.where(full_ref[j] > 0, 0.0, cot_ref[0, j].astype(F32))
                own_ref[0, j] = (back + dres_s[rows_of(j), :] + straight).astype(BF16)
            else:
                (gl_ref if s == 0 else gu_ref)[0, j] = back.astype(BF16)
        return carry

    lax.fori_loop(0, GROUP, finish, 0)


def block_call(c, lanes, spatial, features, hidden, tm_count, scalars, streams, weights, previous):
    first = previous is None
    f = features
    pad = -(-spatial // 16) * 16
    rows = GROUP * pad
    smem = pl.BlockSpec(memory_space=pltpu.SMEM)
    vmem = pl.BlockSpec(memory_space=pltpu.VMEM)
    block = pl.BlockSpec((1, GROUP, spatial, f), lambda i: (0, c, 0, 0))
    whole = pl.BlockSpec((1, GROUP, spatial, f), lambda i: (0, 0, 0, 0))
    wrap = pl.BlockSpec((1, GROUP - 1, spatial, f), lambda i: (0, 0, 0, 0))
    in_specs = [smem] * 4 + [block, whole, wrap, whole, wrap, block] + [vmem] * len(weights)
    accumulators = [(f, 3 * f), (f, f), (f, hidden), (f, hidden), (8, f), (1, hidden)]
    out_shape = (
        [jax.ShapeDtypeStruct((1, lanes, spatial, f), BF16)] * 2
        + [jax.ShapeDtypeStruct((1, GROUP, spatial, f), BF16)] * 2
        + [jax.ShapeDtypeStruct(s, F32) for s in accumulators]
    )
    out_specs = [block, block, whole, whole] + [vmem] * len(accumulators)
    operands = list(scalars) + list(streams) + list(weights)
    aliases = {}
    if not first:
        base = len(operands)
        operands += list(previous)
        in_specs += [vmem] * len(accumulators) + [pl.BlockSpec(memory_space=pl.ANY)] * 2
        aliases = {base + i: 4 + i for i in range(len(accumulators))}
        aliases[base + len(accumulators)] = 0
        aliases[base + len(accumulators) + 1] = 1
    lane = lambda *s: pltpu.VMEM(s, BF16)
    scratch = [
        lane(3, rows, f), lane(3, GROUP, spatial, f), lane(3, GROUP, spatial, f),
        lane(3, GROUP, f, spatial), lane(3, GROUP, f, spatial), lane(GROUP, f, spatial),
        lane(GROUP, f // HEAD_DIM, 3, spatial, spatial), pltpu.VMEM((GROUP, 8, spatial), F32),
        lane(rows, f), lane(GROUP, f, spatial), pltpu.VMEM((rows, f), F32), lane(rows, f),
        lane(rows, hidden), lane(rows, hidden), lane(rows, f), pltpu.VMEM((rows, f), F32),
        lane(rows, f), lane(3, rows, 2 * f), lane(7, f, spatial),
    ]
    return pl.pallas_call(
        functools.partial(block_kernel, first, spatial, f, hidden, tm_count),
        grid=(1,),
        in_specs=in_specs,
        out_specs=out_specs,
        out_shape=out_shape,
        scratch_shapes=scratch,
        input_output_aliases=aliases,
        name="layer_block",
        compiler_params=pltpu.CompilerParams(vmem_limit_bytes=63 * 1024 * 1024),
        cost_estimate=pl.CostEstimate(flops=25 * 10**9, bytes_accessed=20 * 10**6, transcendentals=0),
    )(*operands)


def body(
    tokens, cotangent, lane_frames, pre_gain, pre_bias, w_project, query_bias, value_bias,
    w_out, out_bias, mid_gain, mid_bias, w_up, up_bias, w_down, down_bias,
):
    lanes, spatial, f = tokens.shape[1:]
    hidden = w_up.shape[1]
    tm_count = lax.axis_size("tm")
    tm_index = lax.axis_index("tm")
    lane_span = jnp.maximum(lane_frames // (2 * tm_count), 1)
    lane_offset = jnp.arange(lanes, dtype=jnp.int32) % lane_span
    occupied = lane_frames > 0
    low_ok = (occupied & ((tm_index > 0) | (lane_offset > 0))).astype(jnp.int32)
    up_ok = (occupied & ((tm_index < tm_count - 1) | (lane_offset < lane_span - 1))).astype(jnp.int32)
    full = occupied.astype(jnp.int32)
    tm_arr = tm_index.astype(jnp.int32).reshape(1)
    row = lambda v: v.astype(F32).reshape(1, -1)
    weights = (
        row(pre_gain), row(pre_bias), w_project[:, :f].T, w_project,
        query_bias.astype(F32).reshape(-1, 1), row(value_bias), w_out, row(out_bias),
        row(mid_gain), row(mid_bias), w_up, row(up_bias), w_down, row(down_bias),
    )
    last = tm_count - 1
    rising = [(i, i + 1) for i in range(last)]
    falling = [(i + 1, i) for i in range(last)]
    round_up, round_down = [(last, 0)], [(0, last)]
    send = lambda v, pairs: lax.ppermute(v, "tm", pairs)

    blocks = lanes // GROUP
    streams = []
    token = None
    for c in range(blocks):
        mine = tokens[:, c * GROUP : (c + 1) * GROUP]
        if token is not None:
            mine, _ = lax.optimization_barrier((mine, token))
        low = send(mine, rising)
        up = send(mine, falling)
        low_wrap = send(mine[:, : GROUP - 1], round_up)
        up_wrap = send(mine[:, 1:], round_down)
        streams.append((low, low_wrap, up, up_wrap))
        token = (low, low_wrap, up, up_wrap)

    previous, returned = None, []
    for c in range(blocks):
        lane = slice(c * GROUP, (c + 1) * GROUP)
        low, low_wrap, up, up_wrap = streams[c]
        got = block_call(
            c, lanes, spatial, f, hidden, tm_count, (tm_arr, low_ok[lane], up_ok[lane], full[lane]),
            (tokens, low, low_wrap, up, up_wrap, cotangent), weights, previous,
        )
        out, own, gl, gu = got[:4]
        previous = tuple(got[4:]) + (out, own)
        from_above = send(gl, falling)
        from_above_wrap = send(gl[:, 1:], round_down)
        from_below = send(gu, rising)
        from_below_wrap = send(gu[:, : GROUP - 1], round_up)
        returned.append((from_above, from_above_wrap, from_below, from_below_wrap))

    g_project, g_out, g_up, g_down, g_small, g_upb = previous[:6]
    pieces = [g_project.reshape(-1, f), g_out, g_up.reshape(-1, f), g_down.reshape(-1, f), g_small, g_upb.reshape(-1, f)]
    sizes = [p.shape[0] for p in pieces]
    packed = jnp.concatenate(pieces, 0).astype(BF16)
    packed = lax.psum(packed, ("tm", "clip")).astype(F32)
    parts, at = [], 0
    for n in sizes:
        parts.append(packed[at : at + n])
        at += n
    g_project, g_out, g_up, g_down, g_small, g_upb = parts
    g_project = g_project.reshape(f, 3 * f)
    g_up = g_up.reshape(f, hidden)
    g_down = g_down.reshape(f, hidden).T
    g_upb = g_upb.reshape(hidden)

    received = []
    for above, above_wrap, below, below_wrap in returned:
        one = jnp.zeros_like(above_wrap[:, :1])
        received.append(
            above.astype(F32) + below.astype(F32)
            + jnp.concatenate([above_wrap, one], 1).astype(F32)
            + jnp.concatenate([one, below_wrap], 1).astype(F32)
        )
    input_grad = (own.astype(F32) + jnp.concatenate(received, 1)).astype(BF16)
    return (
        out, input_grad, g_small[0], g_small[1], g_project, g_small[2], g_small[7], g_out, g_small[3],
        g_small[4], g_small[5], g_up, g_upb, g_down, g_small[6],
    )


def solution(mesh):
    spread = P("tm", "clip", None, None)
    return jax.shard_map(
        body,
        mesh=mesh,
        in_specs=(spread, spread, P("clip")) + (P(),) * 13,
        out_specs=(spread, spread) + (P(),) * 13,
        check_vma=False,
    )
```

time: 1180 us -> 594 us (0.50)
  matrix products: 249 us -> 0 us
  local copies, waits for them, and re-layouts: 333 us -> 95.1 us
  Pallas kernels: 0 us -> 231 us
  waiting for transfers between devices: 358 us -> 142 us
  other arithmetic: 159 us -> 13.5 us
  starting transfers between devices: 11.5 us -> 91.8 us
  blocking collectives: 40.1 us -> 0 us
    dot_general x40 -> x0, matrix products: 249 us -> none  [the longest x1 48.4 us: body(): jnp.dot(normed_two, w_up, preferred_element_type=jnp.float32)]
    pallas_call x0 -> x4, Pallas kernels: none -> 231 us  [block_call(): pl.pallas_call(functools.partial(block_kernel, first, spatial, f, hidden,...]
    ppermute x4 -> x32, waiting for transfers between devices: 266 us -> 51.3 us  [body(): send = lambda v, pairs: lax.ppermute(v, 'tm', pairs)]
    ppermute x4 -> x32, starting transfers between devices: 11.5 us -> 91.7 us  [body(): send = lambda v, pairs: lax.ppermute(v, 'tm', pairs)]
    convert_element_type x18 -> x4, other arithmetic: 64.3 us -> 1.76 us  [the longest x1 1.04 us: body(): input_grad = (own.astype(F32) + jnp.concatenate(received, 1)).astype(BF16)]
    unnamed x168 -> x61, local copies, waits for them, and re-layouts: 69.2 us -> 18.7 us
    squeeze x18 -> x0, local copies, waits for them, and re-layouts: 47.1 us -> none  [the longest x16 28.9 us: body(): attended, log_total = lax.map(attend, forward_in)]
    convert_element_type x8 -> x0, local copies, waits for them, and re-layouts: 41.3 us -> none  [the longest x2 13.4 us: body(): kv_grads.astype(jnp.bfloat16)]
  transfers between devices with their start and end apart: 5 -> 33, of which waited for: 5 -> 6; matrix products, arithmetic and copies ran while one was open for 15% -> 14% of each run, Pallas kernels for 0% -> 39%
where the time goes in v1:
time: 594 us; the launch traced here: 588 us
  Pallas kernels  231 us (39%)
  waiting for transfers between devices  142 us (24%)
  local copies, waits for them, and re-layouts  95.1 us (16%)
  starting transfers between devices  91.8 us (15%)
  between operations  14.9 us (3%)
  other arithmetic  13.5 us (2%)
    pallas_call x4, Pallas kernels, block_call(): pl.pallas_call(functools.partial(block_kernel, first, spatial, f, hidden,...  231 us
    ppermute x32, starting transfers between devices, body(): send = lambda v, pairs: lax.ppermute(v, 'tm', pairs)  91.7 us
    psum x1, waiting for transfers between devices, body(): packed = lax.psum(packed, ('tm', 'clip')).astype(F32)  90.9 us
    ppermute x32, waiting for transfers between devices, body(): send = lambda v, pairs: lax.ppermute(v, 'tm', pairs)  51.3 us
    unnamed x61, local copies, waits for them, and re-layouts  18.7 us
    ppermute x8, local copies, waits for them, and re-layouts, body(): send = lambda v, pairs: lax.ppermute(v, 'tm', pairs)  15.7 us
  transfers between devices with their start and end apart: 33, of which 6 were waited for; matrix products, arithmetic and copies ran while one was open for 14% of the time, Pallas kernels for 39%

profile of v1, /device:TPU:0, one launch (start us, length us, event | category | flops | bytes accessed | tf_op | source)
XLA Modules:
  0.0 588.4 jit_solution(15019729076469404633)
XLA Ops:
  7.2 2.3 slice.155
  9.5 5.9 %collective-permute-start = (bf16[1,4,196,384]{3,1,2,0:T(4,128)(2,1)}, bf16[1,4,196,384]{3,1,2,0:T(4,128)(2,1)}, u32[]{:S(2)}, u32[]{:S(2)}) collective-permute-start(bf16[1,4,196,384]{3,1,2,0:T(4,128)(2,1)} %slice.155), channel_id=1, source_target_pairs={{0,8},{8,16},{16,24},{1,9},{9,17},{17,25},{2,10},{10,18},{18,26},{... | collective-permute-start | bytes 1806344 | tf_op jit(solution)/shard_map/ppermute | solution.py:319
  16.7 2.2 copy.121.tok_ref
  21.3 8.1 %collective-permute-start.3 = (bf16[1,3,196,384]{3,2,1,0:T(8,128)(2,1)}, bf16[1,3,196,384]{3,2,1,0:T(8,128)(2,1)}, u32[]{:S(2)}, u32[]{:S(2)}) collective-permute-start(bf16[1,3,196,384]{3,2,1,0:T(8,128)(2,1)} %get-tuple-element.158), channel_id=1, source_target_pairs={{0,24},{1,25},{2,26},{3,27},{4,28},{5,29},{6,30},{7,31}} | collective-permute-start | bytes 1354760 | tf_op jit(solution)/shard_map/ppermute | solution.py:319
  30.5 3.8 copy.124.cot_ref
  42.2 1.5 collective-permute-done.1.low_wrap_ref
  44.8 2.1 collective-permute-start.4
  50.5 8.1 %collective-permute-start.7 = (bf16[1,3,196,384]{3,2,1,0:T(8,128)(2,1)}, bf16[1,3,196,384]{3,2,1,0:T(8,128)(2,1)}, u32[]{:S(2)}, u32[]{:S(2)}) collective-permute-start(bf16[1,3,196,384]{3,2,1,0:T(8,128)(2,1)} %get-tuple-element.167), channel_id=1, source_target_pairs={{0,24},{1,25},{2,26},{3,27},{4,28},{5,29},{6,30},{7,31}} | collective-permute-start | bytes 1354760 | tf_op jit(solution)/shard_map/ppermute | solution.py:319
  58.6 2.0 copy.107.low_ref
  60.6 2.0 copy.108.up_ref
  62.5 55.7 %layer_block.4 = (bf16[1,16,196,384]{3,2,1,0:T(8,128)(2,1)}, bf16[1,16,196,384]{3,2,1,0:T(8,128)(2,1)}, bf16[1,4,196,384]{3,2,1,0:T(8,128)(2,1)}, bf16[1,4,196,3...) custom-call(s32[1]{0:T(128)} %bitcast.tm_ref, ...), custom_call_target="tpu_custom_call" | custom-call | flops 24999999488 | bytes 20000000 | tf_op jit(solution)/shard_map/layer_block/pallas_call | solution.py:280
  118.2 2.2 copy.126
  120.5 1.9 slice.174
  126.6 5.4 collective-permute-start.8
  134.2 2.1 collective-permute-start.11
  137.6 2.0 copy.112.low_ref
  139.6 2.0 copy.113.up_ref
  141.6 58.4 %layer_block.5 = (bf16[1,16,196,384]{3,2,1,0:T(8,128)(2,1)}, bf16[1,16,196,384]{3,2,1,0:T(8,128)(2,1)}, bf16[1,4,196,384]{3,2,1,0:T(8,128)(2,1)}, bf16[1,4,196,3...) custom-call(s32[1]{0:T(128)} %bitcast.tm_ref, ...), custom_call_target="tpu_custom_call", output_to_operand_aliasing={{4}: (24, {}), {5}: (25, {}), {6}: (26, {}), {7}: (27, {}),... | custom-call | flops 24999999488 | bytes 20000000 | tf_op jit(solution)/shard_map/layer_block/pallas_call | solution.py:280
  200.0 2.2 copy.130
  202.2 1.8 slice.176
  207.0 4.8 collective-permute-start.12
  215.5 7.7 %collective-permute-start.15 = (bf16[1,3,196,384]{3,2,1,0:T(8,128)(2,1)}, bf16[1,3,196,384]{3,2,1,0:T(8,128)(2,1)S(1)}, u32[]{:S(2)}, u32[]{:S(2)}) collective-permute-start(bf16[1,3,196,384]{3,2,1,0:T(8,128)(2,1)} %get-tuple-element.163), channel_id=1, source_target_pairs={{0,24},{1,25},{2,26},{3,27},{4,28},{5,29},{6,30},{7,31}} | collective-permute-start | bytes 1354760 | tf_op jit(solution)/shard_map/ppermute | solution.py:319
  223.2 2.0 copy.117.low_ref
  225.2 2.0 copy.118.up_ref
  227.2 58.3 %layer_block.6 = (bf16[1,16,196,384]{3,2,1,0:T(8,128)(2,1)}, bf16[1,16,196,384]{3,2,1,0:T(8,128)(2,1)}, bf16[1,4,196,384]{3,2,1,0:T(8,128)(2,1)}, bf16[1,4,196,3...) custom-call(s32[1]{0:T(128)} %bitcast.tm_ref, ...), custom_call_target="tpu_custom_call", output_to_operand_aliasing={{4}: (24, {}), {5}: (25, {}), {6}: (26, {}), {7}: (27, {}),... | custom-call | flops 24999999488 | bytes 20000000 | tf_op jit(solution)/shard_map/layer_block/pallas_call | solution.py:280
  285.4 2.1 copy.134
  287.6 1.8 slice.178
  289.4 2.1 collective-permute-start.17
  291.6 2.0 copy.122.low_ref
  293.5 2.0 collective-permute-start.18
  295.6 2.0 copy.123.up_ref
  300.2 58.5 %layer_block.7 = (bf16[1,16,196,384]{3,2,1,0:T(8,128)(2,1)}, bf16[1,16,196,384]{3,2,1,0:T(8,128)(2,1)}, bf16[1,4,196,384]{3,2,1,0:T(8,128)(2,1)}, bf16[1,4,196,3...) custom-call(s32[1]{0:T(128)} %bitcast.tm_ref, ...), custom_call_target="tpu_custom_call", output_to_operand_aliasing={{4}: (24, {}), {5}: (25, {}), {6}: (26, {}), {7}: (27, {}),... | custom-call | flops 24999999488 | bytes 20000000 | tf_op jit(solution)/shard_map/layer_block/pallas_call | solution.py:280
  358.7 1.6 convert.31
  360.3 1.3 reshape.125
  361.6 1.4 constant_dynamic-update-slice_fusion.4
  365.3 3.1 reshape.126
  368.4 2.8 convert.34
  371.2 3.1 reshape.127
  374.3 1.6 constant_dynamic-update-slice_fusion.3
  375.9 8.6 %collective-permute-start.22 = (bf16[1,3,196,384]{3,2,1,0:T(8,128)(2,1)}, bf16[1,3,196,384]{3,2,1,0:T(8,128)(2,1)}, u32[]{:S(2)}, u32[]{:S(2)}) collective-permute-start(bf16[1,3,196,384]{3,2,1,0:T(8,128)(2,1)} %slice.176), channel_id=1, source_target_pairs={{0,24},{1,25},{2,26},{3,27},{4,28},{5,29},{6,30},{7,31}} | collective-permute-start | bytes 1354760 | tf_op jit(solution)/shard_map/ppermute | solution.py:319
  384.8 2.1 collective-permute-start.21
  388.3 7.9 %collective-permute-start.26 = (bf16[1,3,196,384]{3,2,1,0:T(8,128)(2,1)}, bf16[1,3,196,384]{3,2,1,0:T(8,128)(2,1)}, u32[]{:S(2)}, u32[]{:S(2)}) collective-permute-start(bf16[1,3,196,384]{3,2,1,0:T(8,128)(2,1)} %slice.178), channel_id=1, source_target_pairs={{0,24},{1,25},{2,26},{3,27},{4,28},{5,29},{6,30},{7,31}} | collective-permute-start | bytes 1354760 | tf_op jit(solution)/shard_map/ppermute | solution.py:319
  398.8 1.8 copy-done.3
  401.8 2.7 collective-permute-done.23
  405.8 1.3 copy.136
  407.1 1.3 collective-permute-start.25
  410.2 13.9 %collective-permute-done.26 = bf16[1,3,196,384]{3,2,1,0:T(8,128)(2,1)} collective-permute-done((bf16[1,3,196,384]{3,2,1,0:T(8,128)(2,1)}, bf16[1,3,196,384]{3,2,1,0:T(8,128)(2,1)}, u32[]{:S(2)}, u32[]{:S(2)}) %collective-permute-start.26) | collective-permute-done | bytes 451616 | tf_op jit(solution)/shard_map/ppermute | solution.py:319
  424.2 1.3 collective-permute-start.29
  425.5 1.7 convert_add_fusion.3
  427.3 12.4 %collective-permute-done.27 = bf16[1,3,196,384]{3,2,1,0:T(8,128)(2,1)S(1)} collective-permute-done((bf16[1,3,196,384]{3,2,1,0:T(8,128)(2,1)S(1)}, bf16[1,3,196,384]{3,2,1,0:T(8,128)(2,1)S(1)}, u32[]{:S(2)}, u32[]{:S(2)}) %collective-permute-start.27) | collective-permute-done | bytes 451616 | tf_op jit(solution)/shard_map/ppermute | solution.py:319
  439.8 1.5 collective-permute-start.30
  442.6 1.7 convert_add_fusion.2
  444.3 1.7 copy.142
  446.1 1.4 convert_add_fusion.1
  447.5 20.6 %collective-permute-done.30 = bf16[1,3,196,384]{3,2,1,0:T(8,128)(2,1)S(1)} collective-permute-done((bf16[1,3,196,384]{3,2,1,0:T(8,128)(2,1)S(1)}, bf16[1,3,196,384]{3,2,1,0:T(8,128)(2,1)S(1)}, u32[]{:S(2)}, u32[]{:S(2)}) %collective-permute-start.30) | collective-permute-done | bytes 451616 | tf_op jit(solution)/shard_map/ppermute | solution.py:319
  469.4 1.7 copy.143
  471.1 90.9 %all-reduce.10.cloned.1.call-done = bf16[4620,384]{1,0:T(8,128)(2,1)} async-done(((bf16[4620,384]{1,0:T(8,128)(2,1)}), bf16[4620,384]{1,0:T(8,128)(2,1)}) %all-reduce.10.cloned.1.call-update) | async-done | bytes 3548176 | tf_op jit(solution)/shard_map/psum | solution.py:355
  562.0 3.4 fusion.4
  565.4 1.6 reshape.132
  567.0 3.2 copy.144
  571.3 3.3 reshape.130
  574.5 1.4 slice.202
  575.9 2.7 reshape.129
  579.2 1.3 reshape.131
  (142 shorter events, 50.1 us)
Async XLA Ops:
  7.2 554.8 %all-reduce.10.cloned.1.call-start = ((), (), s32[]{:S(2)}) async-start(), calls=%async_computation | async-start | bytes 7102464 | tf_op jit(solution)/shard_map/psum | solution.py:355
  9.5 19.9 %copy-start.15 = (s32[16]{0:T(128)S(1)}, s32[16]{0:T(128)}, u32[]{:S(2)}) copy-start(s32[16]{0:T(128)} %param.18) | copy-start | bytes 196
  9.5 34.2 %collective-permute-start = (bf16[1,4,196,384]{3,1,2,0:T(4,128)(2,1)}, bf16[1,4,196,384]{3,1,2,0:T(4,128)(2,1)}, u32[]{:S(2)}, u32[]{:S(2)}) collective-permute-start(bf16[1,4,196,384]{3,1,2,0:T(4,128)(2,1)} %slice.155), channel_id=1, source_target_pairs={{0,8},{8,16},{16,24},{1,9},{9,17},{17,25},{2,10},{10,18},{18,26},{... | collective-permute-start | bytes 1806344 | tf_op jit(solution)/shard_map/ppermute | solution.py:319
  15.4 28.3 %collective-permute-start.2 = (bf16[1,4,196,384]{3,1,2,0:T(4,128)(2,1)}, bf16[1,4,196,384]{3,1,2,0:T(4,128)(2,1)}, u32[]{:S(2)}, u32[]{:S(2)}) collective-permute-start(bf16[1,4,196,384]{3,1,2,0:T(4,128)(2,1)} %slice.155), channel_id=1, source_target_pairs={{8,0},{16,8},{24,16},{9,1},{17,9},{25,17},{10,2},{18,10},{26,18},{... | collective-permute-start | bytes 1806344 | tf_op jit(solution)/shard_map/ppermute | solution.py:319
  18.9 22.3 %copy-start.1 = (bf16[1,16,196,384]{3,2,1,0:T(8,128)(2,1)}, bf16[1,16,196,384]{3,2,1,0:T(8,128)(2,1)S(1)}, u32[]{:S(2)}) copy-start(bf16[1,16,196,384]{3,2,1,0:T(8,128)(2,1)S(1)} %copy.121.tok_ref) | copy-start | bytes 7225348
  20.0 23.7 %collective-permute-start.1 = (bf16[1,3,196,384]{3,2,1,0:T(8,128)(2,1)}, bf16[1,3,196,384]{3,2,1,0:T(8,128)(2,1)}, u32[]{:S(2)}, u32[]{:S(2)}) collective-permute-start(bf16[1,3,196,384]{3,2,1,0:T(8,128)(2,1)} %get-tuple-element.159), channel_id=1, source_target_pairs={{24,0},{25,1},{26,2},{27,3},{28,4},{29,5},{30,6},{31,7}} | collective-permute-start | bytes 1354760 | tf_op jit(solution)/shard_map/ppermute | solution.py:319
  21.3 22.4 %collective-permute-start.3 = (bf16[1,3,196,384]{3,2,1,0:T(8,128)(2,1)}, bf16[1,3,196,384]{3,2,1,0:T(8,128)(2,1)}, u32[]{:S(2)}, u32[]{:S(2)}) collective-permute-start(bf16[1,3,196,384]{3,2,1,0:T(8,128)(2,1)} %get-tuple-element.158), channel_id=1, source_target_pairs={{0,24},{1,25},{2,26},{3,27},{4,28},{5,29},{6,30},{7,31}} | collective-permute-start | bytes 1354760 | tf_op jit(solution)/shard_map/ppermute | solution.py:319
  30.4 3.9 slice-start
  30.4 4.8 copy-start.16
  30.4 5.6 copy-start.14
  30.4 6.2 %copy-start.17 = (bf16[384]{0:T(512)(128)(2,1)S(1)}, bf16[384]{0:T(512)(128)(2,1)}, u32[]{:S(2)}) copy-start(bf16[384]{0:T(512)(128)(2,1)} %param.19) | copy-start | bytes 2308
  30.4 6.8 %copy-start.18 = (bf16[384]{0:T(512)(128)(2,1)S(1)}, bf16[384]{0:T(512)(128)(2,1)}, u32[]{:S(2)}) copy-start(bf16[384]{0:T(512)(128)(2,1)} %param.20) | copy-start | bytes 2308
  30.4 7.3 %copy-start.19 = (bf16[384]{0:T(512)(128)(2,1)S(1)}, bf16[384]{0:T(512)(128)(2,1)}, u32[]{:S(2)}) copy-start(bf16[384]{0:T(512)(128)(2,1)} %param.23) | copy-start | bytes 2308
  30.4 7.9 %copy-start.20 = (bf16[384]{0:T(512)(128)(2,1)S(1)}, bf16[384]{0:T(512)(128)(2,1)}, u32[]{:S(2)}) copy-start(bf16[384]{0:T(512)(128)(2,1)} %param.25) | copy-start | bytes 2308
  30.4 8.4 %copy-start.21 = (bf16[384]{0:T(512)(128)(2,1)S(1)}, bf16[384]{0:T(512)(128)(2,1)}, u32[]{:S(2)}) copy-start(bf16[384]{0:T(512)(128)(2,1)} %param.26) | copy-start | bytes 2308
  30.4 9.0 %copy-start.22 = (bf16[384]{0:T(512)(128)(2,1)S(1)}, bf16[384]{0:T(512)(128)(2,1)}, u32[]{:S(2)}) copy-start(bf16[384]{0:T(512)(128)(2,1)} %param.27) | copy-start | bytes 2308
  30.4 9.5 %copy-start.23 = (bf16[384]{0:T(512)(128)(2,1)S(1)}, bf16[384]{0:T(512)(128)(2,1)}, u32[]{:S(2)}) copy-start(bf16[384]{0:T(512)(128)(2,1)} %param.31) | copy-start | bytes 2308
  44.8 80.7 %collective-permute-start.4 = (bf16[1,4,196,384]{3,1,2,0:T(4,128)(2,1)}, bf16[1,4,196,384]{3,1,2,0:T(4,128)(2,1)}, u32[]{:S(2)}, u32[]{:S(2)}) collective-permute-start(bf16[1,4,196,384]{3,1,2,0:T(4,128)(2,1)} %copy.99), channel_id=1, source_target_pairs={{0,8},{8,16},{16,24},{1,9},{9,17},{17,25},{2,10},{10,18},{18,26},{... | collective-permute-start | bytes 1806344 | tf_op jit(solution)/shard_map/ppermute | solution.py:319
  46.9 78.6 %collective-permute-start.6 = (bf16[1,4,196,384]{3,1,2,0:T(4,128)(2,1)}, bf16[1,4,196,384]{3,1,2,0:T(4,128)(2,1)}, u32[]{:S(2)}, u32[]{:S(2)}) collective-permute-start(bf16[1,4,196,384]{3,1,2,0:T(4,128)(2,1)} %copy.99), channel_id=1, source_target_pairs={{8,0},{16,8},{24,16},{9,1},{17,9},{25,17},{10,2},{18,10},{26,18},{... | collective-permute-start | bytes 1806344 | tf_op jit(solution)/shard_map/ppermute | solution.py:319
  49.2 76.2 %collective-permute-start.5 = (bf16[1,3,196,384]{3,2,1,0:T(8,128)(2,1)}, bf16[1,3,196,384]{3,2,1,0:T(8,128)(2,1)}, u32[]{:S(2)}, u32[]{:S(2)}) collective-permute-start(bf16[1,3,196,384]{3,2,1,0:T(8,128)(2,1)} %get-tuple-element.168), channel_id=1, source_target_pairs={{24,0},{25,1},{26,2},{27,3},{28,4},{29,5},{30,6},{31,7}} | collective-permute-start | bytes 1354760 | tf_op jit(solution)/shard_map/ppermute | solution.py:319
  50.5 74.9 %collective-permute-start.7 = (bf16[1,3,196,384]{3,2,1,0:T(8,128)(2,1)}, bf16[1,3,196,384]{3,2,1,0:T(8,128)(2,1)}, u32[]{:S(2)}, u32[]{:S(2)}) collective-permute-start(bf16[1,3,196,384]{3,2,1,0:T(8,128)(2,1)} %get-tuple-element.167), channel_id=1, source_target_pairs={{0,24},{1,25},{2,26},{3,27},{4,28},{5,29},{6,30},{7,31}} | collective-permute-start | bytes 1354760 | tf_op jit(solution)/shard_map/ppermute | solution.py:319
  118.2 4.1 copy-start.11
  118.2 7.3 %copy-start.2 = (bf16[1,4,196,384]{3,2,1,0:T(8,128)(2,1)S(1)}, bf16[1,4,196,384]{3,2,1,0:T(8,128)(2,1)}, u32[]{:S(2)}) copy-start(bf16[1,4,196,384]{3,2,1,0:T(8,128)(2,1)} %get-tuple-element.59) | copy-start | bytes 1806340
  124.2 262.8 %collective-permute-start.16 = (bf16[1,4,196,384]{3,1,2,0:T(4,128)(2,1)}, bf16[1,4,196,384]{3,1,2,0:T(4,128)(2,1)}, u32[]{:S(2)}, u32[]{:S(2)}) collective-permute-start(bf16[1,4,196,384]{3,1,2,0:T(4,128)(2,1)} %copy.126), channel_id=1, source_target_pairs={{8,0},{16,8},{24,16},{9,1},{17,9},{25,17},{10,2},{18,10},{26,18},{... | collective-permute-start | bytes 1806344 | tf_op jit(solution)/shard_map/ppermute | solution.py:319
  126.6 79.4 %collective-permute-start.8 = (bf16[1,4,196,384]{3,1,2,0:T(4,128)(2,1)}, bf16[1,4,196,384]{3,1,2,0:T(4,128)(2,1)}, u32[]{:S(2)}, u32[]{:S(2)}) collective-permute-start(bf16[1,4,196,384]{3,1,2,0:T(4,128)(2,1)} %copy.101), channel_id=1, source_target_pairs={{0,8},{8,16},{16,24},{1,9},{9,17},{17,25},{2,10},{10,18},{18,26},{... | collective-permute-start | bytes 1806344 | tf_op jit(solution)/shard_map/ppermute | solution.py:319
  131.9 74.0 %collective-permute-start.10 = (bf16[1,4,196,384]{3,1,2,0:T(4,128)(2,1)}, bf16[1,4,196,384]{3,1,2,0:T(4,128)(2,1)}, u32[]{:S(2)}, u32[]{:S(2)}) collective-permute-start(bf16[1,4,196,384]{3,1,2,0:T(4,128)(2,1)} %copy.101), channel_id=1, source_target_pairs={{8,0},{16,8},{24,16},{9,1},{17,9},{25,17},{10,2},{18,10},{26,18},{... | collective-permute-start | bytes 1806344 | tf_op jit(solution)/shard_map/ppermute | solution.py:319
  134.2 71.7 %collective-permute-start.11 = (bf16[1,3,196,384]{3,2,1,0:T(8,128)(2,1)}, bf16[1,3,196,384]{3,2,1,0:T(8,128)(2,1)}, u32[]{:S(2)}, u32[]{:S(2)}) collective-permute-start(bf16[1,3,196,384]{3,2,1,0:T(8,128)(2,1)} %get-tuple-element.165), channel_id=1, source_target_pairs={{0,24},{1,25},{2,26},{3,27},{4,28},{5,29},{6,30},{7,31}} | collective-permute-start | bytes 1354760 | tf_op jit(solution)/shard_map/ppermute | solution.py:319
  136.3 69.6 %collective-permute-start.9 = (bf16[1,3,196,384]{3,2,1,0:T(8,128)(2,1)}, bf16[1,3,196,384]{3,2,1,0:T(8,128)(2,1)}, u32[]{:S(2)}, u32[]{:S(2)}) collective-permute-start(bf16[1,3,196,384]{3,2,1,0:T(8,128)(2,1)} %get-tuple-element.166), channel_id=1, source_target_pairs={{24,0},{25,1},{26,2},{27,3},{28,4},{29,5},{30,6},{31,7}} | collective-permute-start | bytes 1354760 | tf_op jit(solution)/shard_map/ppermute | solution.py:319
  200.0 4.1 copy-start.10
  207.0 82.4 %collective-permute-start.12 = (bf16[1,4,196,384]{3,1,2,0:T(4,128)(2,1)}, bf16[1,4,196,384]{3,1,2,0:T(4,128)(2,1)}, u32[]{:S(2)}, u32[]{:S(2)}) collective-permute-start(bf16[1,4,196,384]{3,1,2,0:T(4,128)(2,1)} %copy.103), channel_id=1, source_target_pairs={{0,8},{8,16},{16,24},{1,9},{9,17},{17,25},{2,10},{10,18},{18,26},{... | collective-permute-start | bytes 1806344 | tf_op jit(solution)/shard_map/ppermute | solution.py:319
  211.9 81.7 %collective-permute-start.14 = (bf16[1,4,196,384]{3,1,2,0:T(4,128)(2,1)}, bf16[1,4,196,384]{3,1,2,0:T(4,128)(2,1)}, u32[]{:S(2)}, u32[]{:S(2)}) collective-permute-start(bf16[1,4,196,384]{3,1,2,0:T(4,128)(2,1)} %copy.103), channel_id=1, source_target_pairs={{8,0},{16,8},{24,16},{9,1},{17,9},{25,17},{10,2},{18,10},{26,18},{... | collective-permute-start | bytes 1806344 | tf_op jit(solution)/shard_map/ppermute | solution.py:319
  214.2 83.3 %collective-permute-start.13 = (bf16[1,3,196,384]{3,2,1,0:T(8,128)(2,1)}, bf16[1,3,196,384]{3,2,1,0:T(8,128)(2,1)S(1)}, u32[]{:S(2)}, u32[]{:S(2)}) collective-permute-start(bf16[1,3,196,384]{3,2,1,0:T(8,128)(2,1)} %get-tuple-element.164), channel_id=1, source_target_pairs={{24,0},{25,1},{26,2},{27,3},{28,4},{29,5},{30,6},{31,7}} | collective-permute-start | bytes 1354760 | tf_op jit(solution)/shard_map/ppermute | solution.py:319
  215.5 83.3 %collective-permute-start.15 = (bf16[1,3,196,384]{3,2,1,0:T(8,128)(2,1)}, bf16[1,3,196,384]{3,2,1,0:T(8,128)(2,1)S(1)}, u32[]{:S(2)}, u32[]{:S(2)}) collective-permute-start(bf16[1,3,196,384]{3,2,1,0:T(8,128)(2,1)} %get-tuple-element.163), channel_id=1, source_target_pairs={{0,24},{1,25},{2,26},{3,27},{4,28},{5,29},{6,30},{7,31}} | collective-permute-start | bytes 1354760 | tf_op jit(solution)/shard_map/ppermute | solution.py:319
  289.4 98.8 %collective-permute-start.17 = (bf16[1,4,196,384]{3,1,2,0:T(4,128)(2,1)}, bf16[1,4,196,384]{3,1,2,0:T(4,128)(2,1)}, u32[]{:S(2)}, u32[]{:S(2)}) collective-permute-start(bf16[1,4,196,384]{3,1,2,0:T(4,128)(2,1)} %copy.128), channel_id=1, source_target_pairs={{0,8},{8,16},{16,24},{1,9},{9,17},{17,25},{2,10},{10,18},{18,26},{... | collective-permute-start | bytes 1806344 | tf_op jit(solution)/shard_map/ppermute | solution.py:319
  293.5 82.4 %collective-permute-start.18 = (bf16[1,3,196,384]{3,2,1,0:T(8,128)(2,1)}, bf16[1,3,196,384]{3,2,1,0:T(8,128)(2,1)}, u32[]{:S(2)}, u32[]{:S(2)}) collective-permute-start(bf16[1,3,196,384]{3,2,1,0:T(8,128)(2,1)} %slice.174), channel_id=1, source_target_pairs={{0,24},{1,25},{2,26},{3,27},{4,28},{5,29},{6,30},{7,31}} | collective-permute-start | bytes 1354760 | tf_op jit(solution)/shard_map/ppermute | solution.py:319
  297.5 2.6 copy-start.24
  297.6 87.3 %collective-permute-start.19 = (bf16[1,3,196,384]{3,2,1,0:T(8,128)(2,1)}, bf16[1,3,196,384]{3,2,1,0:T(8,128)(2,1)}, u32[]{:S(2)}, u32[]{:S(2)}) collective-permute-start(bf16[1,3,196,384]{3,2,1,0:T(8,128)(2,1)} %slice.175), channel_id=1, source_target_pairs={{24,0},{25,1},{26,2},{27,3},{28,4},{29,5},{30,6},{31,7}} | collective-permute-start | bytes 1354760 | tf_op jit(solution)/shard_map/ppermute | solution.py:319
  298.8 1.3 copy-start.25
  298.9 108.2 %collective-permute-start.20 = (bf16[1,4,196,384]{3,1,2,0:T(4,128)(2,1)}, bf16[1,4,196,384]{3,1,2,0:T(4,128)(2,1)}, u32[]{:S(2)}, u32[]{:S(2)}) collective-permute-start(bf16[1,4,196,384]{3,1,2,0:T(4,128)(2,1)} %copy.130), channel_id=1, source_target_pairs={{8,0},{16,8},{24,16},{9,1},{17,9},{25,17},{10,2},{18,10},{26,18},{... | collective-permute-start | bytes 1806344 | tf_op jit(solution)/shard_map/ppermute | solution.py:319
  361.6 2.5 copy-start.7
  374.3 10.3 %copy-start.4 = (bf16[1536,384]{1,0:T(8,128)(2,1)S(1)}, bf16[1536,384]{1,0:T(8,128)(2,1)}, u32[]{:S(2)}) copy-start(bf16[1536,384]{1,0:T(8,128)(2,1)} %reshape.127) | copy-start | bytes 3538948
  374.3 21.8 %copy-start.12 = (f32[8,384]{1,0:T(8,128)S(1)}, f32[8,384]{1,0:T(8,128)}, u32[]{:S(2)}) copy-start(f32[8,384]{1,0:T(8,128)} %get-tuple-element.99) | copy-start | bytes 36868
  374.3 23.1 %copy-start.13 = (f32[1,1536]{1,0:T(1,128)S(1)}, f32[1,1536]{1,0:T(1,128)}, u32[]{:S(2)}) copy-start(f32[1,1536]{1,0:T(1,128)} %get-tuple-element.100) | copy-start | bytes 18436
  375.9 20.2 %collective-permute-start.22 = (bf16[1,3,196,384]{3,2,1,0:T(8,128)(2,1)}, bf16[1,3,196,384]{3,2,1,0:T(8,128)(2,1)}, u32[]{:S(2)}, u32[]{:S(2)}) collective-permute-start(bf16[1,3,196,384]{3,2,1,0:T(8,128)(2,1)} %slice.176), channel_id=1, source_target_pairs={{0,24},{1,25},{2,26},{3,27},{4,28},{5,29},{6,30},{7,31}} | collective-permute-start | bytes 1354760 | tf_op jit(solution)/shard_map/ppermute | solution.py:319
  384.8 24.1 %collective-permute-start.21 = (bf16[1,4,196,384]{3,1,2,0:T(4,128)(2,1)}, bf16[1,4,196,384]{3,1,2,0:T(4,128)(2,1)}, u32[]{:S(2)}, u32[]{:S(2)}) collective-permute-start(bf16[1,4,196,384]{3,1,2,0:T(4,128)(2,1)} %copy.132), channel_id=1, source_target_pairs={{0,8},{8,16},{16,24},{1,9},{9,17},{17,25},{2,10},{10,18},{18,26},{... | collective-permute-start | bytes 1806344 | tf_op jit(solution)/shard_map/ppermute | solution.py:319
  387.0 17.5 %collective-permute-start.23 = (bf16[1,3,196,384]{3,2,1,0:T(8,128)(2,1)}, bf16[1,3,196,384]{3,2,1,0:T(8,128)(2,1)}, u32[]{:S(2)}, u32[]{:S(2)}) collective-permute-start(bf16[1,3,196,384]{3,2,1,0:T(8,128)(2,1)} %slice.177), channel_id=1, source_target_pairs={{24,0},{25,1},{26,2},{27,3},{28,4},{29,5},{30,6},{31,7}} | collective-permute-start | bytes 1354760 | tf_op jit(solution)/shard_map/ppermute | solution.py:319
  388.3 35.9 %collective-permute-start.26 = (bf16[1,3,196,384]{3,2,1,0:T(8,128)(2,1)}, bf16[1,3,196,384]{3,2,1,0:T(8,128)(2,1)}, u32[]{:S(2)}, u32[]{:S(2)}) collective-permute-start(bf16[1,3,196,384]{3,2,1,0:T(8,128)(2,1)} %slice.178), channel_id=1, source_target_pairs={{0,24},{1,25},{2,26},{3,27},{4,28},{5,29},{6,30},{7,31}} | collective-permute-start | bytes 1354760 | tf_op jit(solution)/shard_map/ppermute | solution.py:319
  396.2 45.1 %collective-permute-start.24 = (bf16[1,4,196,384]{3,1,2,0:T(4,128)(2,1)}, bf16[1,4,196,384]{3,1,2,0:T(4,128)(2,1)}, u32[]{:S(2)}, u32[]{:S(2)}) collective-permute-start(bf16[1,4,196,384]{3,1,2,0:T(4,128)(2,1)} %copy.134), channel_id=1, source_target_pairs={{8,0},{16,8},{24,16},{9,1},{17,9},{25,17},{10,2},{18,10},{26,18},{... | collective-permute-start | bytes 1806344 | tf_op jit(solution)/shard_map/ppermute | solution.py:319
  398.8 1.8 copy-start.3
  400.6 7.8 %copy-start.9 = (bf16[1,4,196,384]{3,2,1,0:T(8,128)(2,1)S(1)}, bf16[1,4,196,384]{3,2,1,0:T(8,128)(2,1)}, u32[]{:S(2)}) copy-start(bf16[1,4,196,384]{3,2,1,0:T(8,128)(2,1)} %get-tuple-element.93) | copy-start | bytes 1806340
  400.6 8.1 %copy-start.8 = (bf16[1,4,196,384]{3,2,1,0:T(8,128)(2,1)S(1)}, bf16[1,4,196,384]{3,2,1,0:T(8,128)(2,1)}, u32[]{:S(2)}) copy-start(bf16[1,4,196,384]{3,2,1,0:T(8,128)(2,1)} %get-tuple-element.94) | copy-start | bytes 1806340
  404.5 35.3 %collective-permute-start.27 = (bf16[1,3,196,384]{3,2,1,0:T(8,128)(2,1)S(1)}, bf16[1,3,196,384]{3,2,1,0:T(8,128)(2,1)S(1)}, u32[]{:S(2)}, u32[]{:S(2)}) collective-permute-start(bf16[1,3,196,384]{3,2,1,0:T(8,128)(2,1)S(1)} %slice.179), channel_id=1, source_target_pairs={{24,0},{25,1},{26,2},{27,3},{28,4},{29,5},{30,6},{31,7}} | collective-permute-start | bytes 1354760 | tf_op jit(solution)/shard_map/ppermute | solution.py:319
  407.1 39.0 %collective-permute-start.25 = (bf16[1,4,196,384]{3,1,2,0:T(4,128)(2,1)S(1)}, bf16[1,4,196,384]{3,1,2,0:T(4,128)(2,1)S(1)}, u32[]{:S(2)}, u32[]{:S(2)}) collective-permute-start(bf16[1,4,196,384]{3,1,2,0:T(4,128)(2,1)S(1)} %copy.136), channel_id=1, source_target_pairs={{0,8},{8,16},{16,24},{1,9},{9,17},{17,25},{2,10},{10,18},{18,26},{... | collective-permute-start | bytes 1806344 | tf_op jit(solution)/shard_map/ppermute | solution.py:319
  408.9 59.2 %collective-permute-start.28 = (bf16[1,4,196,384]{3,1,2,0:T(4,128)(2,1)S(1)}, bf16[1,4,196,384]{3,1,2,0:T(4,128)(2,1)S(1)}, u32[]{:S(2)}, u32[]{:S(2)}) collective-permute-start(bf16[1,4,196,384]{3,1,2,0:T(4,128)(2,1)S(1)} %copy.138), channel_id=1, source_target_pairs={{8,0},{16,8},{24,16},{9,1},{17,9},{25,17},{10,2},{18,10},{26,18},{... | collective-permute-start | bytes 1806344 | tf_op jit(solution)/shard_map/ppermute | solution.py:319
  424.2 44.0 %collective-permute-start.29 = (bf16[1,4,196,384]{3,1,2,0:T(4,128)(2,1)S(1)}, bf16[1,4,196,384]{3,1,2,0:T(4,128)(2,1)S(1)}, u32[]{:S(2)}, u32[]{:S(2)}) collective-permute-start(bf16[1,4,196,384]{3,1,2,0:T(4,128)(2,1)S(1)} %copy.140), channel_id=1, source_target_pairs={{0,8},{8,16},{16,24},{1,9},{9,17},{17,25},{2,10},{10,18},{18,26},{... | collective-permute-start | bytes 1806344 | tf_op jit(solution)/shard_map/ppermute | solution.py:319
  427.3 17.0 %copy-start.5 = (bf16[1,16,196,384]{3,2,1,0:T(8,128)(2,1)S(1)}, bf16[1,16,196,384]{3,2,1,0:T(8,128)(2,1)}, u32[]{:S(2)}) copy-start(bf16[1,16,196,384]{3,2,1,0:T(8,128)(2,1)} %get-tuple-element.131) | copy-start | bytes 7225348
  439.8 28.3 %collective-permute-start.30 = (bf16[1,3,196,384]{3,2,1,0:T(8,128)(2,1)S(1)}, bf16[1,3,196,384]{3,2,1,0:T(8,128)(2,1)S(1)}, u32[]{:S(2)}, u32[]{:S(2)}) collective-permute-start(bf16[1,3,196,384]{3,2,1,0:T(8,128)(2,1)S(1)} %slice.180), channel_id=1, source_target_pairs={{0,24},{1,25},{2,26},{3,27},{4,28},{5,29},{6,30},{7,31}} | collective-permute-start | bytes 1354760 | tf_op jit(solution)/shard_map/ppermute | solution.py:319
  441.3 26.8 %collective-permute-start.31 = (bf16[1,3,196,384]{3,2,1,0:T(8,128)(2,1)S(1)}, bf16[1,3,196,384]{3,2,1,0:T(8,128)(2,1)S(1)}, u32[]{:S(2)}, u32[]{:S(2)}) collective-permute-start(bf16[1,3,196,384]{3,2,1,0:T(8,128)(2,1)S(1)} %slice.181), channel_id=1, source_target_pairs={{24,0},{25,1},{26,2},{27,3},{28,4},{29,5},{30,6},{31,7}} | collective-permute-start | bytes 1354760 | tf_op jit(solution)/shard_map/ppermute | solution.py:319
  447.5 20.9 %copy-start.6 = (bf16[1,16,196,384]{3,2,1,0:T(8,128)(2,1)S(1)}, bf16[1,16,196,384]{3,2,1,0:T(8,128)(2,1)}, u32[]{:S(2)}) copy-start(bf16[1,16,196,384]{3,2,1,0:T(8,128)(2,1)} %get-tuple-element.86) | copy-start | bytes 7225348
  567.0 3.2 copy-start
Sparse Core Ops, SparseCore 0:
  400.7 161.2 all-reduce.9

commit v2 on v1

v2 whole, which is shorter than its diff:
```python
import functools

import jax
import jax.numpy as jnp
from jax import lax
from jax.experimental import pallas as pl
from jax.experimental.pallas import tpu as pltpu
from jax.sharding import PartitionSpec as P

HEAD_DIM = 64
GROUP = 2
WRAP = 4
MESH = pl.DeviceIdType.MESH
EPSILON = 1e-06
FAR = 1e30
F32 = jnp.float32
BF16 = jnp.bfloat16
NN = (((1,), (0,)), ((), ()))
NT = (((1,), (1,)), ((), ()))
TN = (((0,), (0,)), ((), ()))


def dot(a, b, dims=NN):
    return lax.dot_general(a, b, dims, preferred_element_type=F32)


def row_mean(value):
    return jnp.sum(value, -1, keepdims=True) * (1.0 / value.shape[-1])


def normalise(x):
    center = x - row_mean(x)
    rate = lax.rsqrt(row_mean(center * center) + EPSILON)
    return center * rate, rate


def norm_back(grad, xhat, rate, gain):
    e = grad * gain
    return rate * (e - row_mean(e) - xhat * row_mean(e * xhat))


def gelu_parts(h):
    bell = jnp.exp(-0.5 * (h * h))
    t = 1.0 / (1.0 + 0.23164190 * jnp.abs(h))
    poly = t * (0.127414796 + t * (-0.142248368 + t * (0.7107068705 + t * (-0.7265760135 + t * 0.5307027145))))
    tail = poly * bell
    phi = jnp.where(h >= 0.0, 1.0 - tail, tail)
    return h * phi, phi + h * (bell * 0.3989422804014327)


def column_sum(value):
    return jnp.sum(value, 0, keepdims=True)


def layer_kernel(
    lanes, spatial, features, hidden, tm_count,
    low_ok_ref, up_ok_ref, full_ref, tok_hbm, tok_ref, cot_ref,
    pre_gain_ref, pre_bias_ref, wq_t_ref, w_project_ref, query_bias_ref, value_bias_ref,
    w_out_ref, out_bias_ref, mid_gain_ref, mid_bias_ref, w_up_ref, up_bias_ref, w_down_ref, down_bias_ref,
    out_ref, own_ref, above_ref, below_ref, a_project, a_out, a_up, a_down, a_small, a_upb,
    low_s, up_s, gl_s, gu_s, n1_s, k_s, v_s, kt_s, vt_s, qt_s, p_s, inv_s, att_s, attt_s, res_s, n2_s, act_s, gh_s,
    dao_s, dres_s, dq_s, dkv_s, dt_s,
    send_up, send_down, recv_low, recv_up, send_gl, send_gu, recv_above, recv_below,
):
    f = features
    pad = n1_s.shape[1] // GROUP
    heads = f // HEAD_DIM
    tm = lax.axis_index("tm")
    last = tm_count - 1
    at_low, at_high = tm == 0, tm == last
    higher, lower = lax.rem(tm + 1, tm_count), lax.rem(tm + last, tm_count)
    step_up, step_down = (tm + 1) // tm_count, (tm_count - tm) // tm_count
    pre_gain, pre_bias = pre_gain_ref[...], pre_bias_ref[...]
    mid_gain, mid_bias = mid_gain_ref[...], mid_bias_ref[...]

    def has_low(l):
        return jnp.logical_or(tm > 0, lax.rem(l, WRAP) != 0)

    def has_up(l):
        return jnp.logical_or(tm < last, lax.rem(l, WRAP) != WRAP - 1)

    def copy(src, dst, send, recv, device):
        return pltpu.make_async_remote_copy(
            src_ref=src, dst_ref=dst, send_sem=send, recv_sem=recv, device_id={"tm": device}, device_id_type=MESH
        )

    def rising(l):
        return copy(tok_hbm.at[0, l], low_s.at[l + step_up], send_up.at[l], recv_low.at[l + step_up], higher)

    def falling(l):
        return copy(tok_hbm.at[0, l], up_s.at[l - step_down], send_down.at[l], recv_up.at[l - step_down], lower)

    def returning_low(l):
        return copy(gl_s.at[l], above_ref.at[0, l - step_down], send_gl.at[l], recv_above.at[l - step_down], lower)

    def returning_up(l):
        return copy(gu_s.at[l], below_ref.at[0, l + step_up], send_gu.at[l], recv_below.at[l + step_up], higher)

    barrier = pltpu.get_barrier_semaphore()
    for device in (lower, higher):
        pl.semaphore_signal(barrier, inc=1, device_id={"tm": device}, device_id_type=MESH)
    pl.semaphore_wait(barrier, 2)

    def start_tokens(l, carry):
        pl.when(has_up(l))(lambda: rising(l).start())
        pl.when(has_low(l))(lambda: falling(l).start())
        return carry

    lax.fori_loop(0, lanes, start_tokens, 0)

    def fill(l, carry):
        @pl.when(jnp.logical_not(has_low(l)))
        def _():
            low_s[l] = jnp.zeros(low_s.shape[1:], BF16)

        @pl.when(jnp.logical_not(has_up(l)))
        def _():
            up_s[l] = jnp.zeros(up_s.shape[1:], BF16)

        return carry

    lax.fori_loop(0, lanes, fill, 0)

    for new in (a_project, a_out, a_up, a_down, a_small, a_upb):
        new[...] = jnp.zeros_like(new)

    def rows_of(j):
        return pl.ds(pl.multiple_of(j * pad, pad), spatial)

    for ref in (n1_s, att_s, dao_s, dq_s, dkv_s, res_s, dres_s):
        for j in range(GROUP):
            if len(ref.shape) == 3:
                ref[:, pl.ds(j * pad + pad - 16, 16), :] = jnp.zeros((ref.shape[0], 16, ref.shape[2]), ref.dtype)
            else:
                ref[pl.ds(j * pad + pad - 16, 16), :] = jnp.zeros((16, ref.shape[1]), ref.dtype)

    def group(g, carry):
        base = g * GROUP

        def arrive(j, carry):
            l = base + j
            pl.when(has_low(l))(lambda: copy(tok_hbm.at[0, l], low_s.at[l], send_up.at[l], recv_low.at[l], lower).wait_recv())
            pl.when(has_up(l))(lambda: copy(tok_hbm.at[0, l], up_s.at[l], send_down.at[l], recv_up.at[l], higher).wait_recv())
            return carry

        lax.fori_loop(0, GROUP, arrive, 0)

        def forward(j, carry):
            below, above = low_s[base + j].astype(F32), up_s[base + j].astype(F32)
            for s, x in enumerate((below, tok_ref[0, base + j].astype(F32), above)):
                xhat, _ = normalise(x)
                n1 = (xhat * pre_gain + pre_bias).astype(BF16)
                n1_s[s, rows_of(j), :] = n1
                kv = dot(n1, w_project_ref[:, f:])
                k = kv[:, :f].astype(BF16)
                v = (kv[:, f:] + value_bias_ref[...]).astype(BF16)
                k_s[s, j] = k
                v_s[s, j] = v
                kt_s[s, j] = k.T
                vt_s[s, j] = v.T
                if s == 1:
                    qt = (dot(wq_t_ref[...], n1, NT) + query_bias_ref[...]).astype(BF16)
                    qt_s[j] = qt * jnp.asarray(HEAD_DIM ** (-0.5), BF16)
            low_ok, up_ok = low_ok_ref[base + j] > 0, up_ok_ref[base + j] > 0
            low_far, up_far = jnp.where(low_ok, 0.0, FAR), jnp.where(up_ok, 0.0, FAR)
            zero_half = jnp.zeros((HEAD_DIM, spatial), BF16)
            for h in range(heads):
                pair = slice(h // 2 * 2 * HEAD_DIM, (h // 2 + 1) * 2 * HEAD_DIM)
                mine = slice(h * HEAD_DIM, (h + 1) * HEAD_DIM)
                qh = qt_s[j, mine, :]
                qz = jnp.concatenate([qh, zero_half] if h % 2 == 0 else [zero_half, qh], 0)
                scores = [dot(k_s[s, j, :, pair], qz) for s in range(3)]
                tops = [jnp.max(x, 0, keepdims=True) for x in scores]
                top = jnp.maximum(jnp.maximum(tops[0] - low_far, tops[2] - up_far), tops[1])
                total, attended = None, None
                for s, shift in enumerate((top + low_far, top, top + up_far)):
                    prob = jnp.exp(scores[s] - shift)
                    part = column_sum(prob)
                    total = part if total is None else total + part
                    low_prob = prob.astype(BF16)
                    p_s[j, h, s] = low_prob
                    got = dot(vt_s[s, j, mine, :], low_prob)
                    attended = got if attended is None else attended + got
                inverse = 1.0 / total
                inv_s[j, h : h + 1, :] = inverse
                attt_s[j, mine, :] = (attended * inverse).astype(BF16)
            att_s[rows_of(j), :] = attt_s[j].T
            res_s[rows_of(j), :] = tok_ref[0, base + j].astype(F32)
            return carry

        lax.fori_loop(0, GROUP, forward, 0)

        residual = res_s[...] + dot(att_s[...], w_out_ref[...]) + out_bias_ref[...]
        res_s[...] = residual
        xhat2, rate2 = normalise(residual)
        n2_s[...] = (xhat2 * mid_gain + mid_bias).astype(BF16)
        for j in range(GROUP):
            full = full_ref[base + j] > 0
            g = cot_ref[0, base + j]
            dao_s[pl.ds(j * pad, spatial), :] = jnp.where(full, g.astype(F32), 0.0).astype(BF16)

        wide = 256

        def mlp(c, carry):
            cols = pl.ds(pl.multiple_of(c * wide, wide), wide)
            h = dot(n2_s[...], w_up_ref[:, cols]) + up_bias_ref[:, cols]
            act, slope = gelu_parts(h)
            act_s[:, cols] = act.astype(BF16)
            gh = (dot(dao_s[...], w_down_ref[cols, :], NT) * slope).astype(BF16)
            gh_s[:, cols] = gh
            a_upb[:, cols] += column_sum(gh.astype(F32))
            return carry

        lax.fori_loop(0, hidden // wide, mlp, 0)
        a_up[...] += dot(n2_s[...], gh_s[...], TN)
        a_down[...] += dot(dao_s[...], act_s[...], TN)
        total_out = dot(act_s[...], w_down_ref[...]) + down_bias_ref[...] + res_s[...]
        grad_n2 = dot(gh_s[...], w_up_ref[...], NT)
        for j in range(GROUP):
            full = full_ref[base + j] > 0
            mine = total_out[j * pad : j * pad + spatial]
            out_ref[0, base + j] = jnp.where(full, mine, tok_ref[0, base + j].astype(F32)).astype(BF16)
        g = dao_s[...].astype(F32)
        xhat2, rate2 = normalise(res_s[...])
        dres = g + norm_back(grad_n2, xhat2, rate2, mid_gain)
        dres_s[...] = dres
        dao = dres.astype(BF16)
        dao_s[...] = dao
        a_small[3:4, :] += column_sum(dao.astype(F32))
        a_small[4:5, :] += column_sum(grad_n2 * xhat2)
        a_small[5:6, :] += column_sum(grad_n2)
        a_small[6:7, :] += column_sum(g)
        a_out[...] += dot(att_s[...], dao, TN)

        def backward(j, carry):
            dot_rows = dao_s[rows_of(j), :]
            dt = dot(w_out_ref[...], dot_rows, NT).astype(BF16)
            zero_half = jnp.zeros((HEAD_DIM, spatial), BF16)
            for h in range(heads):
                pair = slice(h // 2 * 2 * HEAD_DIM, (h // 2 + 1) * 2 * HEAD_DIM)
                mine = slice(h * HEAD_DIM, (h + 1) * HEAD_DIM)
                dh = dt[mine, :].astype(F32) * inv_s[j, h : h + 1, :]
                delta = column_sum(dh * attt_s[j, mine, :].astype(F32))
                dh = dh.astype(BF16)
                dz = jnp.concatenate([dh, zero_half] if h % 2 == 0 else [zero_half, dh], 0)
                qh = qt_s[j, mine, :]
                grad_q = None
                for s in range(3):
                    prob = p_s[j, h, s]
                    grad_prob = dot(v_s[s, j, :, pair], dz)
                    grad_score = (prob.astype(F32) * (grad_prob - delta)).astype(BF16)
                    dt_s[1 + s, mine, :] = dot(qh, grad_score, NT).astype(BF16)
                    dt_s[4 + s, mine, :] = dot(dh, prob, NT).astype(BF16)
                    got = dot(kt_s[s, j, mine, :], grad_score)
                    grad_q = got if grad_q is None else grad_q + got
                dt_s[0, mine, :] = (grad_q * HEAD_DIM ** (-0.5)).astype(BF16)
            dq_s[rows_of(j), :] = dt_s[0].T
            for s in range(3):
                dkv_s[s, rows_of(j), :f] = dt_s[1 + s].T
                dkv_s[s, rows_of(j), f:] = dt_s[4 + s].T
            return carry

        lax.fori_loop(0, GROUP, backward, 0)

        dq = dq_s[...]
        a_project[:, :f] += dot(n1_s[1], dq, TN)
        a_small[2:3, :] += column_sum(dq.astype(F32))
        for s in range(3):
            dkv = dkv_s[s]
            a_project[:, f:] += dot(n1_s[s], dkv, TN)
            a_small[7:8, :] += column_sum(dkv[:, f:].astype(F32))

        def finish(j, carry):
            below, above = low_s[base + j].astype(F32), up_s[base + j].astype(F32)
            for s, x in enumerate((below, tok_ref[0, base + j].astype(F32), above)):
                grad = dot(dkv_s[s, rows_of(j), :], w_project_ref[:, f:], NT)
                if s == 1:
                    grad += dot(dq_s[rows_of(j), :], w_project_ref[:, :f], NT)
                xhat, rate = normalise(x)
                a_small[0:1, :] += column_sum(grad * xhat)
                a_small[1:2, :] += column_sum(grad)
                back = norm_back(grad, xhat, rate, pre_gain)
                if s == 1:
                    straight = jnp.where(full_ref[base + j] > 0, 0.0, cot_ref[0, base + j].astype(F32))
                    own_ref[0, base + j] = (back + dres_s[rows_of(j), :] + straight).astype(BF16)
                else:
                    (gl_s if s == 0 else gu_s)[base + j] = back.astype(BF16)
            return carry

        lax.fori_loop(0, GROUP, finish, 0)

        def give_back(j, carry):
            l = base + j
            pl.when(has_low(l))(lambda: returning_low(l).start())
            pl.when(has_up(l))(lambda: returning_up(l).start())
            return carry

        lax.fori_loop(0, GROUP, give_back, 0)
        return carry

    lax.fori_loop(0, lanes // GROUP, group, 0)

    def settle(l, carry):
        @pl.when(has_up(l))
        def _():
            rising(l).wait_send()
            returning_up(l).wait_send()
            copy(gl_s.at[l], above_ref.at[0, l], send_gl.at[l], recv_above.at[l], higher).wait_recv()

        @pl.when(has_low(l))
        def _():
            falling(l).wait_send()
            returning_low(l).wait_send()
            copy(gu_s.at[l], below_ref.at[0, l], send_gu.at[l], recv_below.at[l], lower).wait_recv()

        return carry

    lax.fori_loop(0, lanes, settle, 0)


def finish_kernel(tm_ref, own_ref, above_ref, below_ref, out_ref):
    i = pl.program_id(0)
    tm, last = tm_ref[0], tm_ref[1]
    lane = lax.rem(i, WRAP)
    has_above = jnp.logical_or(tm < last, lane != WRAP - 1)
    has_below = jnp.logical_or(tm > 0, lane != 0)
    total = own_ref[...].astype(F32)
    total += jnp.where(has_above, above_ref[...].astype(F32), 0.0)
    total += jnp.where(has_below, below_ref[...].astype(F32), 0.0)
    out_ref[...] = total.astype(BF16)


def layer_call(lanes, spatial, f, hidden, tm_count, scalars, tokens, cotangent, weights):
    pad = -(-spatial // 16) * 16
    rows = GROUP * pad
    smem = pl.BlockSpec(memory_space=pltpu.SMEM)
    vmem = pl.BlockSpec(memory_space=pltpu.VMEM)
    hbm = pl.BlockSpec(memory_space=pl.ANY)
    accumulators = [(f, 3 * f), (f, f), (f, hidden), (f, hidden), (8, f), (1, hidden)]
    whole = jax.ShapeDtypeStruct((1, lanes, spatial, f), BF16)
    lane = lambda *s: pltpu.VMEM(s, BF16)
    dma = pltpu.SemaphoreType.DMA((lanes,))
    scratch = [
        lane(lanes, spatial, f), lane(lanes, spatial, f), lane(lanes, spatial, f), lane(lanes, spatial, f),
        lane(3, rows, f), lane(3, GROUP, spatial, f), lane(3, GROUP, spatial, f),
        lane(3, GROUP, f, spatial), lane(3, GROUP, f, spatial), lane(GROUP, f, spatial),
        lane(GROUP, f // HEAD_DIM, 3, spatial, spatial), pltpu.VMEM((GROUP, 8, spatial), F32),
        lane(rows, f), lane(GROUP, f, spatial), pltpu.VMEM((rows, f), F32), lane(rows, f),
        lane(rows, hidden), lane(rows, hidden), lane(rows, f), pltpu.VMEM((rows, f), F32),
        lane(rows, f), lane(3, rows, 2 * f), lane(7, f, spatial),
    ] + [dma] * 8
    return pl.pallas_call(
        functools.partial(layer_kernel, lanes, spatial, f, hidden, tm_count),
        in_specs=[smem] * 3 + [hbm] + [vmem] * (2 + len(weights)),
        out_specs=[vmem, vmem, hbm, hbm] + [vmem] * len(accumulators),
        out_shape=[whole] * 4 + [jax.ShapeDtypeStruct(s, F32) for s in accumulators],
        scratch_shapes=scratch,
        name="layer",
        compiler_params=pltpu.CompilerParams(
            vmem_limit_bytes=63 * 1024 * 1024, collective_id=0, has_side_effects=True
        ),
        cost_estimate=pl.CostEstimate(flops=100 * 10**9, bytes_accessed=40 * 10**6, transcendentals=0),
    )(*scalars, tokens, tokens, cotangent, *weights)


def body(
    tokens, cotangent, lane_frames, pre_gain, pre_bias, w_project, query_bias, value_bias,
    w_out, out_bias, mid_gain, mid_bias, w_up, up_bias, w_down, down_bias,
):
    lanes, spatial, f = tokens.shape[1:]
    hidden = w_up.shape[1]
    tm_count = lax.axis_size("tm")
    tm_index = lax.axis_index("tm")
    lane_span = jnp.maximum(lane_frames // (2 * tm_count), 1)
    lane_offset = jnp.arange(lanes, dtype=jnp.int32) % lane_span
    occupied = lane_frames > 0
    low_ok = (occupied & ((tm_index > 0) | (lane_offset > 0))).astype(jnp.int32)
    up_ok = (occupied & ((tm_index < tm_count - 1) | (lane_offset < lane_span - 1))).astype(jnp.int32)
    full = occupied.astype(jnp.int32)
    row = lambda v: v.astype(F32).reshape(1, -1)
    weights = (
        row(pre_gain), row(pre_bias), w_project[:, :f].T, w_project,
        query_bias.astype(F32).reshape(-1, 1), row(value_bias), w_out, row(out_bias),
        row(mid_gain), row(mid_bias), w_up, row(up_bias), w_down, row(down_bias),
    )
    got = layer_call(lanes, spatial, f, hidden, tm_count, (low_ok, up_ok, full), tokens, cotangent, weights)
    out, own, above, below = got[:4]
    block = pl.BlockSpec((1, 1, spatial, f), lambda i: (0, i, 0, 0))
    tm_arr = jnp.stack([tm_index, jnp.asarray(tm_count - 1, tm_index.dtype)]).astype(jnp.int32)
    input_grad = pl.pallas_call(
        finish_kernel,
        grid=(lanes,),
        in_specs=[pl.BlockSpec(memory_space=pltpu.SMEM), block, block, block],
        out_specs=block,
        out_shape=jax.ShapeDtypeStruct(tokens.shape, BF16),
        name="finish",
    )(tm_arr, own, above, below)

    g_project, g_out, g_up, g_down, g_small, g_upb = got[4:]
    pieces = [g_project.reshape(-1, f), g_out, g_up.reshape(-1, f), g_down.reshape(-1, f), g_small, g_upb.reshape(-1, f)]
    sizes = [p.shape[0] for p in pieces]
    packed = jnp.concatenate(pieces, 0).astype(BF16)
    packed = lax.psum(packed, ("tm", "clip")).astype(F32)
    parts, at = [], 0
    for n in sizes:
        parts.append(packed[at : at + n])
        at += n
    g_project, g_out, g_up, g_down, g_small, g_upb = parts
    g_project = g_project.reshape(f, 3 * f)
    g_up = g_up.reshape(f, hidden)
    g_down = g_down.reshape(f, hidden).T
    g_upb = g_upb.reshape(hidden)
    return (
        out, input_grad, g_small[0], g_small[1], g_project, g_small[2], g_small[7], g_out, g_small[3],
        g_small[4], g_small[5], g_up, g_upb, g_down, g_small[6],
    )


def solution(mesh):
    spread = P("tm", "clip", None, None)
    return jax.shard_map(
        body,
        mesh=mesh,
        in_specs=(spread, spread, P("clip")) + (P(),) * 13,
        out_specs=(spread, spread) + (P(),) * 13,
        check_vma=False,
    )
```

time: 594 us -> 459 us (0.77)
  starting transfers between devices: 91.8 us -> 0.04 us
  local copies, waits for them, and re-layouts: 95.1 us -> 51.3 us
  Pallas kernels: 231 us -> 258 us
  waiting for transfers between devices: 142 us -> 120 us
    ppermute x32 -> x0, starting transfers between devices: 91.7 us -> none  [body(): send = lambda v, pairs: lax.ppermute(v, 'tm', pairs)]
    ppermute x32 -> x0, waiting for transfers between devices: 51.3 us -> none  [body(): send = lambda v, pairs: lax.ppermute(v, 'tm', pairs)]
    psum x1, waiting for transfers between devices: 90.9 us -> 120 us  [body(): packed = lax.psum(packed, ('tm', 'clip')).astype(F32)]
    pallas_call x4 -> x2, Pallas kernels: 231 us -> 258 us  [the longest x1 247 us: layer_call(): pl.pallas_call(functools.partial(layer_kernel, lanes, spatial, f, hidden,...]
    slice x16 -> x0, local copies, waits for them, and re-layouts: 17.2 us -> none  [the longest x4 5.58 us: body(): from_above_wrap = send(gl[:, 1:], round_down)]
    ppermute x8 -> x0, local copies, waits for them, and re-layouts: 15.7 us -> none  [body(): send = lambda v, pairs: lax.ppermute(v, 'tm', pairs)]
    pallas_call x8 -> x0, local copies, waits for them, and re-layouts: 10.5 us -> none  [block_call(): pl.pallas_call(functools.partial(block_kernel, first, spatial, f, hidden,...]
    unnamed x61 -> x41, local copies, waits for them, and re-layouts: 18.7 us -> 21.4 us
  transfers between devices with their start and end apart: 33 -> 1, of which waited for: 6 -> 1; matrix products, arithmetic and copies ran while one was open for 14% -> 2% of each run, Pallas kernels for 39% -> 2%
where the time goes in v2:
time: 459 us; the launch traced here: 458 us
  Pallas kernels  258 us (56%)
  waiting for transfers between devices  120 us (26%)
  local copies, waits for them, and re-layouts  51.3 us (11%)
  between operations  14.2 us (3%)
  other arithmetic  13.6 us (3%)
    pallas_call x1, Pallas kernels, layer_call(): pl.pallas_call(functools.partial(layer_kernel, lanes, spatial, f, hidden,...  247 us
    psum x1, waiting for transfers between devices, body(): packed = lax.psum(packed, ('tm', 'clip')).astype(F32)  120 us
    unnamed x41, local copies, waits for them, and re-layouts  21.4 us
    pallas_call x1, Pallas kernels, body(): pl.pallas_call(finish_kernel, grid=(lanes,), in_specs=[pl.BlockSpec(memor...  11.2 us
  transfers between devices with their start and end apart: 1, of which 1 were waited for; matrix products, arithmetic and copies ran while one was open for 2% of the time, Pallas kernels for 2%

profile of v2, /device:TPU:0, one launch (start us, length us, event | category | flops | bytes accessed | tf_op | source)
XLA Modules:
  0.0 458.0 jit_solution(3099065574105430995)
XLA Ops:
  7.2 0.0 copy-start.3
  7.2 0.0 all-reduce.2.cloned.1.call-start
  7.2 3.8 copy.38.tok_hbm.tok_ref
  11.0 0.0 copy-done.3
  11.0 0.0 copy-start.8
  11.0 0.0 copy-start.11
  11.1 0.0 copy-start.12
  11.1 0.0 copy-start.13
  11.1 0.0 copy-start.14
  11.1 0.0 copy-start.6
  11.1 0.0 copy-start.15
  11.1 0.0 copy-start.7
  11.1 2.0 copy.40.cot_ref
  13.1 0.0 copy-done.9
  13.1 0.6 reshape.130.pre_gain_ref
  13.7 0.0 copy-done.10
  13.7 0.6 reshape.132.pre_bias_ref
  14.3 0.0 slice-done
  14.3 0.9 copy.45
  15.2 0.8 reshape.147.query_bias_ref
  16.0 0.6 reshape.136.value_bias_ref
  16.5 0.6 reshape.138.out_bias_ref
  17.1 0.6 reshape.140.mid_gain_ref
  17.7 0.0 copy-done.14
  17.7 0.6 reshape.142.mid_bias_ref
  18.2 0.6 reshape.144.up_bias_ref
  18.8 0.6 reshape.146.down_bias_ref
  19.4 0.0 copy-done.7
  19.4 0.6 and_convert_fusion
  20.0 0.6 fusion.1
  20.7 247.2 %layer.1 = (bf16[1,16,196,384]{3,2,1,0:T(8,128)(2,1)}, bf16[1,16,196,384]{3,2,1,0:T(8,128)(2,1)}, bf16[1,16,196,384]{3,2,1,0:T(8,128)(2,1)}, bf16[1,16,196,384]{...) custom-call(s32[16]{0:T(128)} %get-tuple-element.78.low_ok_ref, ...), custom_call_target="tpu_custom_call" | custom-call | flops 99999997952 | bytes 40000000 | tf_op jit(solution)/shard_map/layer/pallas_call | solution.py:352
  267.9 1.6 convert.31
  269.4 1.3 reshape.121
  270.7 1.3 constant_dynamic-update-slice_fusion.4
  272.0 2.8 convert.33
  274.8 3.1 reshape.122
  277.9 2.8 convert.34
  280.7 3.1 reshape.123
  283.8 0.7 convert_reduce_fusion
  284.6 0.6 reshape.124
  285.2 1.2 convert_dynamic-update-slice_fusion
  286.4 0.0 copy-start.4
  286.4 1.5 constant_dynamic-update-slice_fusion.3
  287.9 0.0 copy-done.2
  287.9 0.2 constant_dynamic-update-slice_fusion.2
  288.2 0.0 copy-done.4
  288.2 1.7 copy-done.1
  290.0 0.0 all-reduce.2.cloned.1.call-update
  290.0 3.4 copy.42
  293.4 0.6 pad_add_fusion.tm_ref
  294.0 11.2 %finish.1 = bf16[1,16,196,384]{3,2,1,0:T(8,128)(2,1)} custom-call(s32[2]{0:T(128)} %pad_add_fusion.tm_ref, bf16[1,16,196,384]{3,2,1,0:T(8,128)(2,1)} %get-tuple-element.26.own_ref, bf16[1,16,196,384]{3,2,1,0:T(8,128)(2,1)} %get-tuple-element.27.above_ref, bf16[1,16,196,384]{3,2,1,0:T(8,128)(2,1)} %get-tuple-element.28.below_ref), custom_call_target="tpu_custom_call" | custom-call | tf_op jit(solution)/shard_map/finish/pallas_call | solution.py:390
  305.2 3.5 copy.43
  308.7 120.4 %all-reduce.2.cloned.1.call-done = bf16[4620,384]{1,0:T(8,128)(2,1)} async-done(((bf16[4620,384]{1,0:T(8,128)(2,1)}), bf16[4620,384]{1,0:T(8,128)(2,1)}) %all-reduce.2.cloned.1.call-update) | async-done | bytes 3548176 | tf_op jit(solution)/shard_map/psum | solution.py:403
  429.1 2.6 convert_element_type.11
  431.7 0.6 slice_reduce_fusion
  432.3 1.3 slice.67
  433.7 2.7 reshape.125
  436.4 2.5 fusion.3
  438.8 3.3 reshape.126
  442.1 0.6 slice.75
  442.7 1.3 reshape.127
  444.0 3.3 reshape.128
  447.3 3.0 copy.44
  450.3 0.9 slice.70
  (17 shorter events, 0.1 us)
Async XLA Ops:
  7.2 3.8 copy-start.3
  7.2 421.9 %all-reduce.2.cloned.1.call-start = ((), (), s32[]{:S(2)}) async-start(), calls=%async_computation | async-start | bytes 7102464 | tf_op jit(solution)/shard_map/psum | solution.py:403
  11.0 2.1 copy-start.9
  11.0 2.7 copy-start.10
  11.0 3.2 slice-start
  11.0 4.1 copy-start.8
  11.0 4.9 %copy-start.11 = (bf16[384]{0:T(512)(128)(2,1)S(1)}, bf16[384]{0:T(512)(128)(2,1)}, u32[]{:S(2)}) copy-start(bf16[384]{0:T(512)(128)(2,1)} %param.23) | copy-start | bytes 2308
  11.1 5.5 %copy-start.12 = (bf16[384]{0:T(512)(128)(2,1)S(1)}, bf16[384]{0:T(512)(128)(2,1)}, u32[]{:S(2)}) copy-start(bf16[384]{0:T(512)(128)(2,1)} %param.25) | copy-start | bytes 2308
  11.1 6.0 %copy-start.13 = (bf16[384]{0:T(512)(128)(2,1)S(1)}, bf16[384]{0:T(512)(128)(2,1)}, u32[]{:S(2)}) copy-start(bf16[384]{0:T(512)(128)(2,1)} %param.26) | copy-start | bytes 2308
  11.1 6.6 %copy-start.14 = (bf16[384]{0:T(512)(128)(2,1)S(1)}, bf16[384]{0:T(512)(128)(2,1)}, u32[]{:S(2)}) copy-start(bf16[384]{0:T(512)(128)(2,1)} %param.27) | copy-start | bytes 2308
  11.1 7.1 %copy-start.6 = (bf16[1536]{0:T(1024)(128)(2,1)S(1)}, bf16[1536]{0:T(1024)(128)(2,1)}, u32[]{:S(2)}) copy-start(bf16[1536]{0:T(1024)(128)(2,1)} %param.29) | copy-start | bytes 9220
  11.1 7.7 %copy-start.15 = (bf16[384]{0:T(512)(128)(2,1)S(1)}, bf16[384]{0:T(512)(128)(2,1)}, u32[]{:S(2)}) copy-start(bf16[384]{0:T(512)(128)(2,1)} %param.31) | copy-start | bytes 2308
  11.1 8.3 %copy-start.7 = (s32[16]{0:T(128)S(1)}, s32[16]{0:T(128)}, u32[]{:S(2)}) copy-start(s32[16]{0:T(128)} %param.18) | copy-start | bytes 196
  285.2 2.8 copy-start.2
  286.4 1.8 copy-start.5
  286.4 1.8 copy-start.4
  288.2 1.7 copy-start.1
  429.1 3.3 copy-start
Sparse Core Ops, SparseCore 0:
  290.1 138.9 all-reduce.1

commit v3 on v2

--- a/solution.py
+++ b/solution.py
@@ -52,15 +52,242 @@
     return jnp.sum(value, 0, keepdims=True)
 
 
+class Reduction:
+    def __init__(
+        self, f, hidden, tm, tm_count, masks, bit, across, others, sums, sends,
+        r_core, r_one, r_two, r_tm, own_chunk, gathered, small, r_small, send_sems, recv_sems, local_sems,
+    ):
+        self.f, self.hidden, self.tm, self.tm_count = f, hidden, tm, tm_count
+        self.masks, self.bit, self.across, self.others = masks, bit, across, others
+        self.sums, self.sends = sums, sends
+        self.r_core, self.r_one, self.r_two, self.r_tm = r_core, r_one, r_two, r_tm
+        self.own_chunk, self.gathered, self.small, self.r_small = own_chunk, gathered, small, r_small
+        self.send_sems, self.recv_sems, self.local_sems = send_sems, recv_sems, local_sems
+        self.used, self.trades = 0, 0
+        half = (len(masks) - 1) // 2
+        self.extra = masks[2 : 1 + half] + masks[2 + half :]
+        one, two = masks[1], masks[1 + half]
+        wide = hidden // 2
+        self.pieces = [
+            (1, 0, hidden, one, two), (2, 0, hidden, two, one), (0, 0, wide, one, two), (0, wide, wide, two, one),
+        ]
+        self.core = {a: None for a in range(3)}
+
+    def sem(self, n=1):
+        at = self.used
+        self.used += n
+        return at
+
+    def copy(self, src, dst, at, device):
+        return pltpu.make_async_remote_copy(
+            src_ref=src, dst_ref=dst, send_sem=self.send_sems.at[at], recv_sem=self.recv_sems.at[at],
+            device_id=device, device_id_type=MESH,
+        )
+
+    def rows(self, at, count):
+        return pl.ds(pl.multiple_of(at, 16), count)
+
+    def start_core(self, arrays):
+        count = self.f // 2
+        away = self.rows((1 - self.bit[1]) * count, count)
+        for a in arrays:
+            self.sends[a][away, :] = self.sums[a][away, :].astype(BF16)
+            copy = self.copy(self.sends[a].at[away, :], self.r_core.at[a], a, {"clip": self.across[1]})
+            copy.start()
+
+    def run(self):
+        f = self.f
+        self.used = 3
+        halves = [f // 2, f // 4, f // 8]
+        flying = []
+
+        def exchange_small(device):
+            at = self.sem()
+            slot = self.trades
+            self.trades += 1
+            copy = self.copy(self.small, self.r_small.at[slot], at, device)
+            copy.start()
+            return copy, slot
+
+        def join_small(pair):
+            copy, at = pair
+            copy.wait()
+            self.small[...] += self.r_small[at]
+
+        trading = exchange_small({"clip": self.across[1]})
+        base = self.bit[1] * halves[0]
+        away = self.rows((1 - self.bit[1]) * halves[0], halves[0])
+        for a in (1, 2, 0):
+            self.copy(self.sends[a].at[away, :], self.r_core.at[a], a, {"clip": self.across[1]}).wait()
+        join_small(trading)
+
+        def add(a, cols, at, count, got):
+            where = self.rows(at, count)
+            self.sums[a][where, cols] += got.astype(F32)
+
+        def half_step(level, bases, boxes, which):
+            count = halves[level]
+            sent, new = [], []
+            for i, (a, c, n, *ms) in enumerate(self.pieces):
+                m = ms[which]
+                cols = slice(c, c + n)
+                away = self.rows(bases[i] + (1 - self.bit[m]) * count, count)
+                if level == 1:
+                    got = self.r_core[a, pl.ds(pl.multiple_of((1 - self.bit[m]) * count, 16), count), cols]
+                    add(a, cols, bases[i] + (1 - self.bit[m]) * count, count, got)
+                self.sends[a][away, cols] = self.sums[a][away, cols].astype(BF16)
+                copy = self.copy(
+                    self.sends[a].at[away, cols], boxes.at[a, :, cols], self.sem(), {"clip": self.across[m]}
+                )
+                copy.start()
+                sent.append(copy)
+                new.append(bases[i] + self.bit[m] * count)
+            for i, (a, c, n, *ms) in enumerate(self.pieces):
+                cols = slice(c, c + n)
+                if level == 1:
+                    m = ms[which]
+                    got = self.r_core[a, pl.ds(pl.multiple_of(self.bit[m] * count, 16), count), cols]
+                    add(a, cols, new[i], count, got)
+            for i, (a, c, n, *ms) in enumerate(self.pieces):
+                sent[i].wait()
+                cols = slice(c, c + n)
+                add(a, cols, new[i], count, boxes[a, :, cols])
+            return new
+
+        trading = exchange_small({"clip": self.across[self.masks[1]]})
+        bases = half_step(1, [base] * 4, self.r_one, 0)
+        join_small(trading)
+        trading = exchange_small({"clip": self.across[self.pieces[0][4]]})
+        bases = half_step(2, bases, self.r_two, 1)
+        join_small(trading)
+        count = halves[2]
+        for n_extra, m in enumerate(self.extra):
+            trading = exchange_small({"clip": self.across[m]})
+            sent = []
+            for i, (a, c, n, *ms) in enumerate(self.pieces):
+                cols = slice(c, c + n)
+                here = self.rows(bases[i], count)
+                box = self.own_chunk.at[1 + n_extra, a, :, cols]
+                self.sends[a][here, cols] = self.sums[a][here, cols].astype(BF16)
+                copy = self.copy(self.sends[a].at[here, cols], box, self.sem(), {"clip": self.across[m]})
+                copy.start()
+                sent.append((copy, box))
+            for i, (a, c, n, *ms) in enumerate(self.pieces):
+                copy, box = sent[i]
+                copy.wait()
+                cols = slice(c, c + n)
+                here = self.rows(bases[i], count)
+                self.sums[a][here, cols] = self.sends[a][here, cols].astype(F32) + box[...].astype(F32)
+            join_small(trading)
+
+        chunks = []
+        for first in (0, 2):
+            for q in range(4):
+                a, c, n = self.pieces[first + q // 2][:3]
+                cols = slice(c + (q % 2) * (n // 2), c + (q % 2) * (n // 2) + n // 2)
+                chunks.append((first // 2, q, a, cols, bases[first + q // 2], n // 2))
+        parts = self.tm_count
+        arrival = {0: self.sem(parts), 1: self.sem(parts)}
+        departure = {}
+        for which, q, a, cols, at, n in chunks:
+            departure[which, q] = self.sem()
+            here = self.rows(at, count)
+
+            def send(which=which, q=q, a=a, cols=cols, here=here, n=n):
+                self.sends[a][here, cols] = self.sums[a][here, cols].astype(BF16)
+                self.chunk_copy(which, q, a, cols, here, n, departure, arrival).start()
+
+            pl.when(self.tm != q)(send)
+        trading = exchange_small({"tm": self.tm + 1 - 2 * (self.tm % 2)})
+        join_small(trading)
+        trading = exchange_small({"tm": self.tm + 2 - 4 * (self.tm // 2)})
+        join_small(trading)
+        back = {0: self.sem(parts), 1: self.sem(parts)}
+        outgoing = self.sem(2 * parts)
+        for which, q, a, cols, at, n in chunks:
+            here = self.rows(at, count)
+
+            def settle(which=which, q=q, a=a, cols=cols, here=here, n=n):
+                total = self.sums[a][here, cols]
+                for other in range(parts):
+                    if other != q:
+                        pltpu.make_async_copy(
+                            self.r_tm.at[which, other, :, pl.ds(0, n)], self.r_tm.at[which, other, :, pl.ds(0, n)],
+                            self.recv_sems.at[arrival[which] + other],
+                        ).wait()
+                        total += self.r_tm[which, other, :, :n].astype(F32)
+                self.own_chunk[0, which, :, :n] = total.astype(BF16)
+                self.publish(which, q, a, cols, here, n, back, outgoing, "start")
+
+            pl.when(self.tm == q)(settle)
+        for which, q, a, cols, at, n in chunks:
+            here = self.rows(at, count)
+
+            def arrive(which=which, q=q, a=a, cols=cols, here=here, n=n):
+                self.chunk_copy(which, q, a, cols, here, n, departure, arrival).wait_send()
+                place = self.gathered.at[a, here, cols]
+                pltpu.make_async_copy(place, place, self.recv_sems.at[back[which] + q]).wait()
+
+            def left(which=which, q=q, a=a, cols=cols, here=here, n=n):
+                self.publish(which, q, a, cols, here, n, back, outgoing, "wait")
+
+            pl.when(self.tm != q)(arrive)
+            pl.when(self.tm == q)(left)
+
+        for level, which in ((2, 1), (1, 0)):
+            count = halves[level]
+            sent = []
+            for i, (a, c, n, *ms) in enumerate(self.pieces):
+                m = ms[which]
+                cols = slice(c, c + n)
+                place = self.gathered.at[a, self.rows(bases[i], count), cols]
+                copy = self.copy(place, place, self.sem(), {"clip": self.across[m]})
+                copy.start()
+                sent.append((copy, self.gathered.at[a, self.rows(bases[i] + (1 - 2 * self.bit[m]) * count, count), cols]))
+                bases[i] = bases[i] - self.bit[m] * count
+            for copy, theirs in sent:
+                copy.wait_send()
+                copy.wait_recv()
+        sent = []
+        for a in range(3):
+            place = self.gathered.at[a, self.rows(base, halves[0]), :]
+            copy = self.copy(place, place, self.sem(), {"clip": self.across[1]})
+            copy.start()
+            sent.append(copy)
+        for copy in sent:
+            copy.wait()
+
+    def chunk_copy(self, which, q, a, cols, here, n, departure, arrival):
+        return pltpu.make_async_remote_copy(
+            src_ref=self.sends[a].at[here, cols], dst_ref=self.r_tm.at[which, self.tm, :, pl.ds(0, n)],
+            send_sem=self.send_sems.at[departure[which, q]], recv_sem=self.recv_sems.at[arrival[which] + self.tm],
+            device_id={"tm": q}, device_id_type=MESH,
+        )
+
+    def publish(self, which, q, a, cols, here, n, back, outgoing, do):
+        place = self.gathered.at[a, here, cols]
+        chunk = self.own_chunk.at[0, which, :, pl.ds(0, n)]
+        local = pltpu.make_async_copy(chunk, place, self.local_sems.at[which])
+        local.start() if do == "start" else local.wait()
+        for other in range(self.tm_count):
+            if other != q:
+                copy = pltpu.make_async_remote_copy(
+                    src_ref=chunk, dst_ref=place, send_sem=self.send_sems.at[outgoing + which * self.tm_count + other],
+                    recv_sem=self.recv_sems.at[back[which] + q], device_id={"tm": other}, device_id_type=MESH,
+                )
+                copy.start() if do == "start" else copy.wait_send()
+
+
 def layer_kernel(
-    lanes, spatial, features, hidden, tm_count,
+    lanes, spatial, features, hidden, tm_count, clip_count,
     low_ok_ref, up_ok_ref, full_ref, tok_hbm, tok_ref, cot_ref,
     pre_gain_ref, pre_bias_ref, wq_t_ref, w_project_ref, query_bias_ref, value_bias_ref,
     w_out_ref, out_bias_ref, mid_gain_ref, mid_bias_ref, w_up_ref, up_bias_ref, w_down_ref, down_bias_ref,
-    out_ref, own_ref, above_ref, below_ref, a_project, a_out, a_up, a_down, a_small, a_upb,
-    low_s, up_s, gl_s, gu_s, n1_s, k_s, v_s, kt_s, vt_s, qt_s, p_s, inv_s, att_s, attt_s, res_s, n2_s, act_s, gh_s,
+    out_ref, own_ref, above_ref, below_ref, gathered_ref, total_small_ref,
+    a_w, a_up, a_down, a_small, a_upb, low_s, up_s, gl_s, gu_s, n1_s, k_s, v_s, kt_s, vt_s, qt_s, p_s, inv_s, att_s, attt_s, res_s, n2_s, act_s, gh_s,
     dao_s, dres_s, dq_s, dkv_s, dt_s,
     send_up, send_down, recv_low, recv_up, send_gl, send_gu, recv_above, recv_below,
+    s_w, s_up, s_down, r_core, r_one, r_two, r_tm, own_chunk, r_small, ar_send, ar_recv, ar_local,
 ):
     f = features
     pad = n1_s.shape[1] // GROUP
@@ -96,10 +323,18 @@
     def returning_up(l):
         return copy(gu_s.at[l], below_ref.at[0, l + step_up], send_gu.at[l], recv_below.at[l + step_up], higher)
 
+    clip = lax.axis_index("clip")
+    masks = [1 << i for i in range((clip_count - 1).bit_length())]
+    bit = {m: (clip // m) % 2 for m in masks}
+    across = {m: clip + m * (1 - 2 * bit[m]) for m in masks}
+    others = [lax.rem(tm + i, tm_count) for i in range(1, tm_count)]
+
     barrier = pltpu.get_barrier_semaphore()
-    for device in (lower, higher):
+    for device in others:
         pl.semaphore_signal(barrier, inc=1, device_id={"tm": device}, device_id_type=MESH)
-    pl.semaphore_wait(barrier, 2)
+    for m in masks:
+        pl.semaphore_signal(barrier, inc=1, device_id={"clip": across[m]}, device_id_type=MESH)
+    pl.semaphore_wait(barrier, len(others) + len(masks))
 
     def start_tokens(l, carry):
         pl.when(has_up(l))(lambda: rising(l).start())
@@ -121,7 +356,7 @@
 
     lax.fori_loop(0, lanes, fill, 0)
 
-    for new in (a_project, a_out, a_up, a_down, a_small, a_upb):
+    for new in (a_w, a_up, a_down, a_small, a_upb):
         new[...] = jnp.zeros_like(new)
 
     def rows_of(j):
@@ -134,8 +369,13 @@
             else:
                 ref[pl.ds(j * pad + pad - 16, 16), :] = jnp.zeros((16, ref.shape[1]), ref.dtype)
 
-    def group(g, carry):
-        base = g * GROUP
+    sums = Reduction(
+        f, hidden, tm, tm_count, masks, bit, across, others, (a_w, a_up, a_down), (s_w, s_up, s_down),
+        r_core, r_one, r_two, r_tm, own_chunk, gathered_ref, a_small, r_small, ar_send, ar_recv, ar_local,
+    )
+
+    def group(index, carry):
+        base = index * GROUP
 
         def arrive(j, carry):
             l = base + j
@@ -214,6 +454,7 @@
         lax.fori_loop(0, hidden // wide, mlp, 0)
         a_up[...] += dot(n2_s[...], gh_s[...], TN)
         a_down[...] += dot(dao_s[...], act_s[...], TN)
+        pl.when(index == lanes // GROUP - 1)(lambda: sums.start_core((1, 2)))
         total_out = dot(act_s[...], w_down_ref[...]) + down_bias_ref[...] + res_s[...]
         grad_n2 = dot(gh_s[...], w_up_ref[...], NT)
         for j in range(GROUP):
@@ -230,7 +471,7 @@
         a_small[4:5, :] += column_sum(grad_n2 * xhat2)
         a_small[5:6, :] += column_sum(grad_n2)
         a_small[6:7, :] += column_sum(g)
-        a_out[...] += dot(att_s[...], dao, TN)
+        a_w[:, 3 * f :] += dot(att_s[...], dao, TN)
 
         def backward(j, carry):
             dot_rows = dao_s[rows_of(j), :]
@@ -263,11 +504,11 @@
         lax.fori_loop(0, GROUP, backward, 0)
 
         dq = dq_s[...]
-        a_project[:, :f] += dot(n1_s[1], dq, TN)
+        a_w[:, :f] += dot(n1_s[1], dq, TN)
         a_small[2:3, :] += column_sum(dq.astype(F32))
         for s in range(3):
             dkv = dkv_s[s]
-            a_project[:, f:] += dot(n1_s[s], dkv, TN)
+            a_w[:, f : 3 * f] += dot(n1_s[s], dkv, TN)
             a_small[7:8, :] += column_sum(dkv[:, f:].astype(F32))
 
         def finish(j, carry):
@@ -299,6 +540,11 @@
         return carry
 
     lax.fori_loop(0, lanes // GROUP, group, 0)
+    for i in range(hidden // f):
+        a_small[8 + i : 9 + i, :] = a_upb[:, i * f : (i + 1) * f]
+    sums.start_core((0,))
+    sums.run()
+    total_small_ref[...] = a_small[...]
 
     def settle(l, carry):
         @pl.when(has_up(l))
@@ -319,28 +565,36 @@
 
 
 def finish_kernel(tm_ref, own_ref, above_ref, below_ref, out_ref):
-    i = pl.program_id(0)
     tm, last = tm_ref[0], tm_ref[1]
-    lane = lax.rem(i, WRAP)
-    has_above = jnp.logical_or(tm < last, lane != WRAP - 1)
-    has_below = jnp.logical_or(tm > 0, lane != 0)
-    total = own_ref[...].astype(F32)
-    total += jnp.where(has_above, above_ref[...].astype(F32), 0.0)
-    total += jnp.where(has_below, below_ref[...].astype(F32), 0.0)
-    out_ref[...] = total.astype(BF16)
-
-
-def layer_call(lanes, spatial, f, hidden, tm_count, scalars, tokens, cotangent, weights):
+    for lane in range(WRAP):
+        total = own_ref[0, lane].astype(F32)
+        above, below = above_ref[0, lane].astype(F32), below_ref[0, lane].astype(F32)
+        total += above if lane < WRAP - 1 else jnp.where(tm < last, above, 0.0)
+        total += below if lane > 0 else jnp.where(tm > 0, below, 0.0)
+        out_ref[0, lane] = total.astype(BF16)
+
+
+def unpack_kernel(in_ref, project_ref, out_ref, up_ref, down_ref):
+    f = out_ref.shape[1]
+    project_ref[...] = in_ref[0, :, : 3 * f].astype(F32)
+    out_ref[...] = in_ref[0, :, 3 * f :].astype(F32)
+    up_ref[...] = in_ref[1].astype(F32)
+    down_ref[...] = in_ref[2].astype(F32).T
+
+
+def layer_call(lanes, spatial, f, hidden, tm_count, clip_count, scalars, tokens, cotangent, weights):
     pad = -(-spatial // 16) * 16
     rows = GROUP * pad
     smem = pl.BlockSpec(memory_space=pltpu.SMEM)
     vmem = pl.BlockSpec(memory_space=pltpu.VMEM)
     hbm = pl.BlockSpec(memory_space=pl.ANY)
-    accumulators = [(f, 3 * f), (f, f), (f, hidden), (f, hidden), (8, f), (1, hidden)]
+    masks = (clip_count - 1).bit_length()
+    extra = masks - 3
+    sums = [pltpu.VMEM(s, F32) for s in [(f, hidden)] * 3 + [(16, f), (1, hidden)]]
     whole = jax.ShapeDtypeStruct((1, lanes, spatial, f), BF16)
     lane = lambda *s: pltpu.VMEM(s, BF16)
     dma = pltpu.SemaphoreType.DMA((lanes,))
-    scratch = [
+    scratch = sums + [
         lane(lanes, spatial, f), lane(lanes, spatial, f), lane(lanes, spatial, f), lane(lanes, spatial, f),
         lane(3, rows, f), lane(3, GROUP, spatial, f), lane(3, GROUP, spatial, f),
         lane(3, GROUP, f, spatial), lane(3, GROUP, f, spatial), lane(GROUP, f, spatial),
@@ -349,11 +603,17 @@
         lane(rows, hidden), lane(rows, hidden), lane(rows, f), pltpu.VMEM((rows, f), F32),
         lane(rows, f), lane(3, rows, 2 * f), lane(7, f, spatial),
     ] + [dma] * 8
+    sems = pltpu.SemaphoreType.DMA((96,))
+    scratch += [
+        lane(f, hidden), lane(f, hidden), lane(f, hidden), lane(3, f // 2, hidden), lane(3, f // 4, hidden),
+        lane(3, f // 8, hidden), lane(2, tm_count, f // 8, hidden // 2), lane(1 + extra, 3, f // 8, hidden),
+        pltpu.VMEM((masks + 2, 16, f), F32), sems, sems, pltpu.SemaphoreType.DMA((2,)),
+    ]
     return pl.pallas_call(
-        functools.partial(layer_kernel, lanes, spatial, f, hidden, tm_count),
+        functools.partial(layer_kernel, lanes, spatial, f, hidden, tm_count, clip_count),
         in_specs=[smem] * 3 + [hbm] + [vmem] * (2 + len(weights)),
-        out_specs=[vmem, vmem, hbm, hbm] + [vmem] * len(accumulators),
-        out_shape=[whole] * 4 + [jax.ShapeDtypeStruct(s, F32) for s in accumulators],
+        out_specs=[vmem, vmem, hbm, hbm, hbm, vmem],
+        out_shape=[whole] * 4 + [jax.ShapeDtypeStruct((3, f, hidden), BF16), jax.ShapeDtypeStruct((16, f), F32)],
         scratch_shapes=scratch,
         name="layer",
         compiler_params=pltpu.CompilerParams(
@@ -383,33 +643,31 @@
         query_bias.astype(F32).reshape(-1, 1), row(value_bias), w_out, row(out_bias),
         row(mid_gain), row(mid_bias), w_up, row(up_bias), w_down, row(down_bias),
     )
-    got = layer_call(lanes, spatial, f, hidden, tm_count, (low_ok, up_ok, full), tokens, cotangent, weights)
-    out, own, above, below = got[:4]
-    block = pl.BlockSpec((1, 1, spatial, f), lambda i: (0, i, 0, 0))
+    out, own, above, below, gathered, small = layer_call(
+        lanes, spatial, f, hidden, tm_count, lax.axis_size("clip"), (low_ok, up_ok, full), tokens, cotangent, weights
+    )
+    block = pl.BlockSpec((1, WRAP, spatial, f), lambda i: (0, i, 0, 0))
     tm_arr = jnp.stack([tm_index, jnp.asarray(tm_count - 1, tm_index.dtype)]).astype(jnp.int32)
     input_grad = pl.pallas_call(
         finish_kernel,
-        grid=(lanes,),
+        grid=(lanes // WRAP,),
         in_specs=[pl.BlockSpec(memory_space=pltpu.SMEM), block, block, block],
         out_specs=block,
         out_shape=jax.ShapeDtypeStruct(tokens.shape, BF16),
         name="finish",
     )(tm_arr, own, above, below)
 
-    g_project, g_out, g_up, g_down, g_small, g_upb = got[4:]
-    pieces = [g_project.reshape(-1, f), g_out, g_up.reshape(-1, f), g_down.reshape(-1, f), g_small, g_upb.reshape(-1, f)]
-    sizes = [p.shape[0] for p in pieces]
-    packed = jnp.concatenate(pieces, 0).astype(BF16)
-    packed = lax.psum(packed, ("tm", "clip")).astype(F32)
-    parts, at = [], 0
-    for n in sizes:
-        parts.append(packed[at : at + n])
-        at += n
-    g_project, g_out, g_up, g_down, g_small, g_upb = parts
-    g_project = g_project.reshape(f, 3 * f)
-    g_up = g_up.reshape(f, hidden)
-    g_down = g_down.reshape(f, hidden).T
-    g_upb = g_upb.reshape(hidden)
+    tall = 128
+    wide_block = lambda n: pl.BlockSpec((tall, n), lambda i: (i, 0))
+    g_project, g_out, g_up, g_down = pl.pallas_call(
+        unpack_kernel,
+        grid=(f // tall,),
+        in_specs=[pl.BlockSpec((3, tall, hidden), lambda i: (0, i, 0))],
+        out_specs=[wide_block(3 * f), wide_block(f), wide_block(hidden), pl.BlockSpec((hidden, tall), lambda i: (0, i))],
+        out_shape=[jax.ShapeDtypeStruct(n, F32) for n in ((f, 3 * f), (f, f), (f, hidden), (hidden, f))],
+        name="unpack",
+    )(gathered)
+    g_small, g_upb = small[:8], small[8 : 8 + hidden // f].reshape(hidden)
     return (
         out, input_grad, g_small[0], g_small[1], g_project, g_small[2], g_small[7], g_out, g_small[3],
         g_small[4], g_small[5], g_up, g_upb, g_down, g_small[6],

time: 459 us -> 343 us (0.75)
  waiting for transfers between devices: 120 us -> 0 us
  Pallas kernels: 258 us -> 311 us
  local copies, waits for them, and re-layouts: 51.3 us -> 27.2 us
  between operations: 14.2 us -> 0.68 us
  other arithmetic: 13.6 us -> 3.18 us
    psum x1 -> x0, waiting for transfers between devices: 120 us -> none  [body(): packed = lax.psum(packed, ('tm', 'clip')).astype(F32)]
    pallas_call x1, Pallas kernels: 247 us -> 301 us  [layer_call(): pl.pallas_call(functools.partial(layer_kernel, lanes, spatial, f, hidden,...]
    reshape x8 -> x1, local copies, waits for them, and re-layouts: 18.6 us -> 0.61 us  [body(): g_small, g_upb = (small[:8], small[8:8 + hidden // f].reshape(hidden))]
    another operation x4 -> x0, other arithmetic: 7.9 us -> none
    unnamed x41 -> x9, local copies, waits for them, and re-layouts: 21.4 us -> 13.6 us
    reshape x8, local copies, waits for them, and re-layouts: 4.55 us -> 9.98 us  [body(): row = lambda v: v.astype(F32).reshape(1, -1)]
    slice x4 -> x1, local copies, waits for them, and re-layouts: 5.27 us -> 0.01 us  [body(): g_small, g_upb = (small[:8], small[8:8 + hidden // f].reshape(hidden))]
    pallas_call x1 -> x2, Pallas kernels: 11.2 us -> 10.6 us  [the longest x1 5.36 us: body(): pl.pallas_call(finish_kernel, grid=(lanes // WRAP,), in_specs=[pl.BlockSp...]
  transfers between devices with their start and end apart: 1 -> 0, of which waited for: 1 -> 0; matrix products, arithmetic and copies ran while one was open for 2% -> 0% of each run, Pallas kernels for 2% -> 0%
where the time goes in v3:
time: 343 us; the launch traced here: 342 us
  Pallas kernels  311 us (91%)
  local copies, waits for them, and re-layouts  27.2 us (8%)
    pallas_call x1, Pallas kernels, layer_call(): pl.pallas_call(functools.partial(layer_kernel, lanes, spatial, f, hidden,...  301 us
    unnamed x9, local copies, waits for them, and re-layouts  13.6 us
    reshape x8, local copies, waits for them, and re-layouts, body(): row = lambda v: v.astype(F32).reshape(1, -1)  9.98 us

profile of v3, /device:TPU:0, one launch (start us, length us, event | category | flops | bytes accessed | tf_op | source)
XLA Modules:
  0.0 342.2 jit_solution(18405757529021537217)
XLA Ops:
  0.7 0.6 pad_add_fusion.tm_ref
  1.2 1.3 and_convert_fusion
  2.5 1.3 fusion.1
  3.8 1.2 reshape.98.pre_gain_ref
  5.1 1.2 reshape.100.pre_bias_ref
  6.3 1.2 reshape.104.value_bias_ref
  7.6 1.2 reshape.106.out_bias_ref
  8.8 1.2 reshape.108.mid_gain_ref
  10.0 1.2 reshape.110.mid_bias_ref
  11.3 1.2 reshape.114.down_bias_ref
  12.5 1.3 reshape.112.up_bias_ref
  13.8 1.5 reshape.115.query_bias_ref
  15.3 1.0 slice.39
  16.3 0.9 copy.44
  17.2 0.0 copy-start
  17.2 3.9 %copy.38.tok_hbm.tok_ref = bf16[1,16,196,384]{3,2,1,0:T(8,128)(2,1)} copy(bf16[1,16,196,384]{3,1,2,0:T(8,128)(2,1)} %param.16) | data formatting | bytes 4816896 | tf_op args[0]
  21.0 0.0 copy-done
  21.0 2.0 copy.40.cot_ref
  23.0 300.6 %layer.1 = (bf16[1,16,196,384]{3,2,1,0:T(8,128)(2,1)}, bf16[1,16,196,384]{3,2,1,0:T(8,128)(2,1)}, bf16[1,16,196,384]{3,2,1,0:T(8,128)(2,1)}, bf16[1,16,196,384]{...) custom-call(s32[16]{0:T(128)} %get-tuple-element.76.low_ok_ref, s32[16]{0:T(128)} %get-tuple-element.73.up_ok_ref, ...), custom_call_target="tpu_custom_call" | custom-call | flops 99999997952 | bytes 40000000 | tf_op jit(solution)/shard_map/layer/pallas_call | solution.py:612
  323.6 0.0 copy-start.1
  323.6 3.4 %copy.42 = bf16[1,16,196,384]{3,1,2,0:T(8,128)(2,1)} copy(bf16[1,16,196,384]{3,2,1,0:T(8,128)(2,1)} %get-tuple-element.50) | data formatting | bytes 4816896
  327.0 0.0 copy-done.1
  327.0 0.6 slice_reduce_fusion
  327.6 0.6 reshape.96
  328.2 5.4 %finish.1 = bf16[1,16,196,384]{3,2,1,0:T(8,128)(2,1)} custom-call(s32[2]{0:T(128)} %pad_add_fusion.tm_ref, bf16[1,16,196,384]{3,2,1,0:T(8,128)(2,1)} %get-tuple-element.26.own_ref, bf16[1,16,196,384]{3,2,1,0:T(8,128)(2,1)} %get-tuple-element.27.above_ref, bf16[1,16,196,384]{3,2,1,0:T(8,128)(2,1)} %get-tuple-element.28.below_ref), custom_call_target="tpu_custom_call" | custom-call | tf_op jit(solution)/shard_map/finish/pallas_call | solution.py:651
  333.6 3.4 copy.43
  337.0 5.2 %unpack.1 = (f32[384,1152]{1,0:T(8,128)}, f32[384,384]{1,0:T(8,128)}, f32[384,1536]{1,0:T(8,128)}, f32[1536,384]{1,0:T(8,128)}) custom-call(bf16[3,384,1536]{2,1,0:T(8,128)(2,1)} %get-tuple-element.30.in_ref), custom_call_target="tpu_custom_call" | custom-call | tf_op jit(solution)/shard_map/unpack/pallas_call | solution.py:662
  (1 shorter events, 0.0 us)
Async XLA Ops:
  17.2 3.9 %copy-start = (bf16[1,16,196,384]{3,1,2,0:T(8,128)(2,1)S(1)}, bf16[1,16,196,384]{3,1,2,0:T(8,128)(2,1)}, u32[]{:S(2)}) copy-start(bf16[1,16,196,384]{3,1,2,0:T(8,128)(2,1)} %param.17) | copy-start | bytes 7225348
  323.6 3.4 %copy-start.1 = (f32[16,384]{1,0:T(8,128)S(1)}, f32[16,384]{1,0:T(8,128)}, u32[]{:S(2)}) copy-start(f32[16,384]{1,0:T(8,128)} %get-tuple-element.29) | copy-start | bytes 73732

commit v4 on v3

--- a/solution.py
+++ b/solution.py
@@ -280,8 +280,8 @@
 
 def layer_kernel(
     lanes, spatial, features, hidden, tm_count, clip_count,
-    low_ok_ref, up_ok_ref, full_ref, tok_hbm, tok_ref, cot_ref,
-    pre_gain_ref, pre_bias_ref, wq_t_ref, w_project_ref, query_bias_ref, value_bias_ref,
+    frames_ref, tok_hbm, tok_ref, cot_ref,
+    pre_gain_ref, pre_bias_ref, w_project_ref, query_bias_ref, value_bias_ref,
     w_out_ref, out_bias_ref, mid_gain_ref, mid_bias_ref, w_up_ref, up_bias_ref, w_down_ref, down_bias_ref,
     out_ref, own_ref, above_ref, below_ref, gathered_ref, total_small_ref,
     a_w, a_up, a_down, a_small, a_upb, low_s, up_s, gl_s, gu_s, n1_s, k_s, v_s, kt_s, vt_s, qt_s, p_s, inv_s, att_s, attt_s, res_s, n2_s, act_s, gh_s,
@@ -297,8 +297,22 @@
     at_low, at_high = tm == 0, tm == last
     higher, lower = lax.rem(tm + 1, tm_count), lax.rem(tm + last, tm_count)
     step_up, step_down = (tm + 1) // tm_count, (tm_count - tm) // tm_count
-    pre_gain, pre_bias = pre_gain_ref[...], pre_bias_ref[...]
-    mid_gain, mid_bias = mid_gain_ref[...], mid_bias_ref[...]
+
+    def row(ref):
+        return ref[...].astype(F32).reshape(1, -1)
+
+    pre_gain, pre_bias, mid_gain, mid_bias = row(pre_gain_ref), row(pre_bias_ref), row(mid_gain_ref), row(mid_bias_ref)
+    out_bias, down_bias, up_bias = row(out_bias_ref), row(down_bias_ref), row(up_bias_ref)
+    query_bias, value_bias = row(query_bias_ref), row(value_bias_ref)
+
+    def full_lane(l):
+        return frames_ref[l] > 0
+
+    def joined(l):
+        frames = frames_ref[l]
+        inner_low = ((frames == 4 * tm_count) & (l % 2 > 0)) | ((frames == 8 * tm_count) & (l % 4 > 0))
+        inner_up = ((frames == 4 * tm_count) & (l % 2 < 1)) | ((frames == 8 * tm_count) & (l % 4 < 3))
+        return (frames > 0) & (inner_low | (tm > 0)), (frames > 0) & (inner_up | (tm < last))
 
     def has_low(l):
         return jnp.logical_or(tm > 0, lax.rem(l, WRAP) != 0)
@@ -393,23 +407,29 @@
                 n1_s[s, rows_of(j), :] = n1
                 kv = dot(n1, w_project_ref[:, f:])
                 k = kv[:, :f].astype(BF16)
-                v = (kv[:, f:] + value_bias_ref[...]).astype(BF16)
+                v = (kv[:, f:] + value_bias).astype(BF16)
                 k_s[s, j] = k
                 v_s[s, j] = v
                 kt_s[s, j] = k.T
                 vt_s[s, j] = v.T
                 if s == 1:
-                    qt = (dot(wq_t_ref[...], n1, NT) + query_bias_ref[...]).astype(BF16)
-                    qt_s[j] = qt * jnp.asarray(HEAD_DIM ** (-0.5), BF16)
-            low_ok, up_ok = low_ok_ref[base + j] > 0, up_ok_ref[base + j] > 0
+                    q = (dot(n1, w_project_ref[:, :f]) + query_bias).astype(BF16)
+                    qt_s[j] = (q * jnp.asarray(HEAD_DIM ** (-0.5), BF16)).T
+            low_ok, up_ok = joined(base + j)
             low_far, up_far = jnp.where(low_ok, 0.0, FAR), jnp.where(up_ok, 0.0, FAR)
             zero_half = jnp.zeros((HEAD_DIM, spatial), BF16)
+            def get_scores(h):
+                pair = slice(h // 2 * 2 * HEAD_DIM, (h // 2 + 1) * 2 * HEAD_DIM)
+                qh = qt_s[j, h * HEAD_DIM : (h + 1) * HEAD_DIM, :]
+                qz = jnp.concatenate([qh, zero_half] if h % 2 == 0 else [zero_half, qh], 0)
+                return [dot(k_s[s, j, :, pair], qz) for s in range(3)]
+
+            later = get_scores(0)
             for h in range(heads):
-                pair = slice(h // 2 * 2 * HEAD_DIM, (h // 2 + 1) * 2 * HEAD_DIM)
                 mine = slice(h * HEAD_DIM, (h + 1) * HEAD_DIM)
-                qh = qt_s[j, mine, :]
-                qz = jnp.concatenate([qh, zero_half] if h % 2 == 0 else [zero_half, qh], 0)
-                scores = [dot(k_s[s, j, :, pair], qz) for s in range(3)]
+                scores = later
+                if h + 1 < heads:
+                    later = get_scores(h + 1)
                 tops = [jnp.max(x, 0, keepdims=True) for x in scores]
                 top = jnp.maximum(jnp.maximum(tops[0] - low_far, tops[2] - up_far), tops[1])
                 total, attended = None, None
@@ -428,14 +448,15 @@
             res_s[rows_of(j), :] = tok_ref[0, base + j].astype(F32)
             return carry
 
-        lax.fori_loop(0, GROUP, forward, 0)
-
-        residual = res_s[...] + dot(att_s[...], w_out_ref[...]) + out_bias_ref[...]
+        for j in range(GROUP):
+            forward(j, 0)
+
+        residual = res_s[...] + dot(att_s[...], w_out_ref[...]) + out_bias
         res_s[...] = residual
         xhat2, rate2 = normalise(residual)
         n2_s[...] = (xhat2 * mid_gain + mid_bias).astype(BF16)
         for j in range(GROUP):
-            full = full_ref[base + j] > 0
+            full = full_lane(base + j)
             g = cot_ref[0, base + j]
             dao_s[pl.ds(j * pad, spatial), :] = jnp.where(full, g.astype(F32), 0.0).astype(BF16)
 
@@ -443,7 +464,7 @@
 
         def mlp(c, carry):
             cols = pl.ds(pl.multiple_of(c * wide, wide), wide)
-            h = dot(n2_s[...], w_up_ref[:, cols]) + up_bias_ref[:, cols]
+            h = dot(n2_s[...], w_up_ref[:, cols]) + up_bias[:, c * wide : (c + 1) * wide]
             act, slope = gelu_parts(h)
             act_s[:, cols] = act.astype(BF16)
             gh = (dot(dao_s[...], w_down_ref[cols, :], NT) * slope).astype(BF16)
@@ -451,14 +472,15 @@
             a_upb[:, cols] += column_sum(gh.astype(F32))
             return carry
 
-        lax.fori_loop(0, hidden // wide, mlp, 0)
+        for c in range(hidden // wide):
+            mlp(c, 0)
         a_up[...] += dot(n2_s[...], gh_s[...], TN)
         a_down[...] += dot(dao_s[...], act_s[...], TN)
         pl.when(index == lanes // GROUP - 1)(lambda: sums.start_core((1, 2)))
-        total_out = dot(act_s[...], w_down_ref[...]) + down_bias_ref[...] + res_s[...]
+        total_out = dot(act_s[...], w_down_ref[...]) + down_bias + res_s[...]
         grad_n2 = dot(gh_s[...], w_up_ref[...], NT)
         for j in range(GROUP):
-            full = full_ref[base + j] > 0
+            full = full_lane(base + j)
             mine = total_out[j * pad : j * pad + spatial]
             out_ref[0, base + j] = jnp.where(full, mine, tok_ref[0, base + j].astype(F32)).astype(BF16)
         g = dao_s[...].astype(F32)
@@ -477,22 +499,31 @@
             dot_rows = dao_s[rows_of(j), :]
             dt = dot(w_out_ref[...], dot_rows, NT).astype(BF16)
             zero_half = jnp.zeros((HEAD_DIM, spatial), BF16)
-            for h in range(heads):
+            def prepare(h):
                 pair = slice(h // 2 * 2 * HEAD_DIM, (h // 2 + 1) * 2 * HEAD_DIM)
                 mine = slice(h * HEAD_DIM, (h + 1) * HEAD_DIM)
                 dh = dt[mine, :].astype(F32) * inv_s[j, h : h + 1, :]
                 delta = column_sum(dh * attt_s[j, mine, :].astype(F32))
                 dh = dh.astype(BF16)
                 dz = jnp.concatenate([dh, zero_half] if h % 2 == 0 else [zero_half, dh], 0)
+                return dh, delta, [dot(v_s[s, j, :, pair], dz) for s in range(3)]
+
+            later = prepare(0)
+            for h in range(heads):
+                mine = slice(h * HEAD_DIM, (h + 1) * HEAD_DIM)
+                dh, delta, grad_probs = later
+                if h + 1 < heads:
+                    later = prepare(h + 1)
                 qh = qt_s[j, mine, :]
+                probs = [p_s[j, h, s] for s in range(3)]
+                for s in range(3):
+                    dt_s[4 + s, mine, :] = dot(dh, probs[s], NT).astype(BF16)
+                ds = [(probs[s].astype(F32) * (grad_probs[s] - delta)).astype(BF16) for s in range(3)]
+                for s in range(3):
+                    dt_s[1 + s, mine, :] = dot(qh, ds[s], NT).astype(BF16)
                 grad_q = None
                 for s in range(3):
-                    prob = p_s[j, h, s]
-                    grad_prob = dot(v_s[s, j, :, pair], dz)
-                    grad_score = (prob.astype(F32) * (grad_prob - delta)).astype(BF16)
-                    dt_s[1 + s, mine, :] = dot(qh, grad_score, NT).astype(BF16)
-                    dt_s[4 + s, mine, :] = dot(dh, prob, NT).astype(BF16)
-                    got = dot(kt_s[s, j, mine, :], grad_score)
+                    got = dot(kt_s[s, j, mine, :], ds[s])
                     grad_q = got if grad_q is None else grad_q + got
                 dt_s[0, mine, :] = (grad_q * HEAD_DIM ** (-0.5)).astype(BF16)
             dq_s[rows_of(j), :] = dt_s[0].T
@@ -501,7 +532,8 @@
                 dkv_s[s, rows_of(j), f:] = dt_s[4 + s].T
             return carry
 
-        lax.fori_loop(0, GROUP, backward, 0)
+        for j in range(GROUP):
+            backward(j, 0)
 
         dq = dq_s[...]
         a_w[:, :f] += dot(n1_s[1], dq, TN)
@@ -522,13 +554,14 @@
                 a_small[1:2, :] += column_sum(grad)
                 back = norm_back(grad, xhat, rate, pre_gain)
                 if s == 1:
-                    straight = jnp.where(full_ref[base + j] > 0, 0.0, cot_ref[0, base + j].astype(F32))
+                    straight = jnp.where(full_lane(base + j), 0.0, cot_ref[0, base + j].astype(F32))
                     own_ref[0, base + j] = (back + dres_s[rows_of(j), :] + straight).astype(BF16)
                 else:
                     (gl_s if s == 0 else gu_s)[base + j] = back.astype(BF16)
             return carry
 
-        lax.fori_loop(0, GROUP, finish, 0)
+        for j in range(GROUP):
+            finish(j, 0)
 
         def give_back(j, carry):
             l = base + j
@@ -582,7 +615,7 @@
     down_ref[...] = in_ref[2].astype(F32).T
 
 
-def layer_call(lanes, spatial, f, hidden, tm_count, clip_count, scalars, tokens, cotangent, weights):
+def layer_call(lanes, spatial, f, hidden, tm_count, clip_count, frames, tokens, cotangent, weights):
     pad = -(-spatial // 16) * 16
     rows = GROUP * pad
     smem = pl.BlockSpec(memory_space=pltpu.SMEM)
@@ -611,7 +644,7 @@
     ]
     return pl.pallas_call(
         functools.partial(layer_kernel, lanes, spatial, f, hidden, tm_count, clip_count),
-        in_specs=[smem] * 3 + [hbm] + [vmem] * (2 + len(weights)),
+        in_specs=[smem, hbm] + [vmem] * (2 + len(weights)),
         out_specs=[vmem, vmem, hbm, hbm, hbm, vmem],
         out_shape=[whole] * 4 + [jax.ShapeDtypeStruct((3, f, hidden), BF16), jax.ShapeDtypeStruct((16, f), F32)],
         scratch_shapes=scratch,
@@ -620,7 +653,7 @@
             vmem_limit_bytes=63 * 1024 * 1024, collective_id=0, has_side_effects=True
         ),
         cost_estimate=pl.CostEstimate(flops=100 * 10**9, bytes_accessed=40 * 10**6, transcendentals=0),
-    )(*scalars, tokens, tokens, cotangent, *weights)
+    )(frames, tokens, tokens, cotangent, *weights)
 
 
 def body(
@@ -631,20 +664,12 @@
     hidden = w_up.shape[1]
     tm_count = lax.axis_size("tm")
     tm_index = lax.axis_index("tm")
-    lane_span = jnp.maximum(lane_frames // (2 * tm_count), 1)
-    lane_offset = jnp.arange(lanes, dtype=jnp.int32) % lane_span
-    occupied = lane_frames > 0
-    low_ok = (occupied & ((tm_index > 0) | (lane_offset > 0))).astype(jnp.int32)
-    up_ok = (occupied & ((tm_index < tm_count - 1) | (lane_offset < lane_span - 1))).astype(jnp.int32)
-    full = occupied.astype(jnp.int32)
-    row = lambda v: v.astype(F32).reshape(1, -1)
     weights = (
-        row(pre_gain), row(pre_bias), w_project[:, :f].T, w_project,
-        query_bias.astype(F32).reshape(-1, 1), row(value_bias), w_out, row(out_bias),
-        row(mid_gain), row(mid_bias), w_up, row(up_bias), w_down, row(down_bias),
+        pre_gain, pre_bias, w_project, query_bias, value_bias, w_out, out_bias,
+        mid_gain, mid_bias, w_up, up_bias, w_down, down_bias,
     )
     out, own, above, below, gathered, small = layer_call(
-        lanes, spatial, f, hidden, tm_count, lax.axis_size("clip"), (low_ok, up_ok, full), tokens, cotangent, weights
+        lanes, spatial, f, hidden, tm_count, lax.axis_size("clip"), lane_frames, tokens, cotangent, weights
     )
     block = pl.BlockSpec((1, WRAP, spatial, f), lambda i: (0, i, 0, 0))
     tm_arr = jnp.stack([tm_index, jnp.asarray(tm_count - 1, tm_index.dtype)]).astype(jnp.int32)

time: 343 us -> 265 us (0.77)
  Pallas kernels: 311 us -> 251 us
  local copies, waits for them, and re-layouts: 27.2 us -> 12.2 us
    pallas_call x1, Pallas kernels: 301 us -> 241 us  [layer_call(): pl.pallas_call(functools.partial(layer_kernel, lanes, spatial, f, hidden,...]
    reshape x9 -> x0, local copies, waits for them, and re-layouts: 11.4 us -> none  [the longest x8 9.98 us: body(): row = lambda v: v.astype(F32).reshape(1, -1)]
    unnamed x9 -> x10, local copies, waits for them, and re-layouts: 13.6 us -> 10.9 us
where the time goes in v4:
time: 265 us
  Pallas kernels  251 us (95%)
  local copies, waits for them, and re-layouts  12.2 us (5%)
    pallas_call x1, Pallas kernels, layer_call(): pl.pallas_call(functools.partial(layer_kernel, lanes, spatial, f, hidden,...  241 us
    unnamed x10, local copies, waits for them, and re-layouts  10.9 us
    pallas_call x1, Pallas kernels, body(): pl.pallas_call(finish_kernel, grid=(lanes // WRAP,), in_specs=[pl.BlockSp...  5.37 us
    pallas_call x1, Pallas kernels, body(): pl.pallas_call(unpack_kernel, grid=(f // tall,), in_specs=[pl.BlockSpec((...  5.34 us

profile of v4, /device:TPU:0, one launch (start us, length us, event | category | flops | bytes accessed | tf_op | source)
XLA Modules:
  0.0 264.7 jit_solution(11705743510227755936)
XLA Ops:
  0.6 0.0 copy-start.1
  0.7 3.8 %copy.31.tok_hbm.tok_ref = bf16[1,16,196,384]{3,2,1,0:T(8,128)(2,1)} copy(bf16[1,16,196,384]{3,1,2,0:T(8,128)(2,1)} %param.16) | data formatting | bytes 4816896 | tf_op args[0]
  4.4 0.0 copy-done.1
  4.4 2.0 copy.33.cot_ref
  6.4 240.5 %layer.1 = (bf16[1,16,196,384]{3,2,1,0:T(8,128)(2,1)}, bf16[1,16,196,384]{3,2,1,0:T(8,128)(2,1)}, bf16[1,16,196,384]{3,2,1,0:T(8,128)(2,1)}, bf16[1,16,196,384]{...) custom-call(s32[16]{0:T(128)} %frames_ref.1, bf16[1,16,196,384]{3,2,1,0:T(8,128)(2,1)} %copy.31.tok_hbm.tok_ref, ...), custom_call_target="tpu_custom_call" | custom-call | flops 99999997952 | bytes 40000000 | tf_op jit(solution)/shard_map/layer/pallas_call | solution.py:645
  246.9 0.6 pad_add_fusion.tm_ref
  247.5 5.4 %finish.1 = bf16[1,16,196,384]{3,2,1,0:T(8,128)(2,1)} custom-call(s32[2]{0:T(128)} %pad_add_fusion.tm_ref, bf16[1,16,196,384]{3,2,1,0:T(8,128)(2,1)} %get-tuple-element.26.own_ref, bf16[1,16,196,384]{3,2,1,0:T(8,128)(2,1)} %get-tuple-element.27.above_ref, bf16[1,16,196,384]{3,2,1,0:T(8,128)(2,1)} %get-tuple-element.28.below_ref), custom_call_target="tpu_custom_call" | custom-call | tf_op jit(solution)/shard_map/finish/pallas_call | solution.py:676
  252.9 0.0 copy-start.2
  252.9 3.4 %copy.35 = bf16[1,16,196,384]{3,1,2,0:T(8,128)(2,1)} copy(bf16[1,16,196,384]{3,2,1,0:T(8,128)(2,1)} %finish.1) | data formatting | bytes 4816896
  256.3 0.0 copy-start
  256.3 0.0 copy-done.2
  256.3 0.6 slice_reduce_fusion
  257.0 5.3 %unpack.1 = (f32[384,1152]{1,0:T(8,128)}, f32[384,384]{1,0:T(8,128)}, f32[384,1536]{1,0:T(8,128)}, f32[1536,384]{1,0:T(8,128)}) custom-call(bf16[3,384,1536]{2,1,0:T(8,128)(2,1)} %get-tuple-element.30.in_ref), custom_call_target="tpu_custom_call" | custom-call | tf_op jit(solution)/shard_map/unpack/pallas_call | solution.py:687
  262.3 0.6 reshape.33
  262.9 0.0 copy-done
  262.9 1.7 copy.34
  (1 shorter events, 0.0 us)
Async XLA Ops:
  0.6 3.8 %copy-start.1 = (bf16[1,16,196,384]{3,1,2,0:T(8,128)(2,1)S(1)}, bf16[1,16,196,384]{3,1,2,0:T(8,128)(2,1)}, u32[]{:S(2)}) copy-start(bf16[1,16,196,384]{3,1,2,0:T(8,128)(2,1)} %param.17) | copy-start | bytes 7225348
  252.9 3.4 %copy-start.2 = (f32[16,384]{1,0:T(8,128)S(1)}, f32[16,384]{1,0:T(8,128)}, u32[]{:S(2)}) copy-start(f32[16,384]{1,0:T(8,128)} %get-tuple-element.29) | copy-start | bytes 73732
  256.3 6.6 %copy-start = (bf16[1,16,196,384]{3,2,1,0:T(8,128)(2,1)S(1)}, bf16[1,16,196,384]{3,2,1,0:T(8,128)(2,1)}, u32[]{:S(2)}) copy-start(bf16[1,16,196,384]{3,2,1,0:T(8,128)(2,1)} %get-tuple-element.35) | copy-start | bytes 7225348

commit v5 on v4

--- a/solution.py
+++ b/solution.py
@@ -95,11 +95,12 @@
             copy = self.copy(self.sends[a].at[away, :], self.r_core.at[a], a, {"clip": self.across[1]})
             copy.start()
 
-    def run(self):
+    def run(self, between):
         f = self.f
         self.used = 3
         halves = [f // 2, f // 4, f // 8]
-        flying = []
+        parts = self.tm_count
+        groups = ((0, 1), (2, 3))
 
         def exchange_small(device):
             at = self.sem()
@@ -110,55 +111,76 @@
             return copy, slot
 
         def join_small(pair):
-            copy, at = pair
+            copy, slot = pair
             copy.wait()
-            self.small[...] += self.r_small[at]
-
-        trading = exchange_small({"clip": self.across[1]})
-        base = self.bit[1] * halves[0]
-        away = self.rows((1 - self.bit[1]) * halves[0], halves[0])
-        for a in (1, 2, 0):
-            self.copy(self.sends[a].at[away, :], self.r_core.at[a], a, {"clip": self.across[1]}).wait()
-        join_small(trading)
+            self.small[...] += self.r_small[slot]
 
         def add(a, cols, at, count, got):
             where = self.rows(at, count)
             self.sums[a][where, cols] += got.astype(F32)
 
-        def half_step(level, bases, boxes, which):
+        base = self.bit[1] * halves[0]
+        away = self.rows((1 - self.bit[1]) * halves[0], halves[0])
+        bases = [base] * 4
+        flying = {}
+
+        def wait_core(arrays):
+            for a in arrays:
+                self.copy(self.sends[a].at[away, :], self.r_core.at[a], a, {"clip": self.across[1]}).wait()
+
+        def start_half(level, members, boxes, which):
             count = halves[level]
-            sent, new = [], []
-            for i, (a, c, n, *ms) in enumerate(self.pieces):
+            for i in members:
+                a, c, n, *ms = self.pieces[i]
                 m = ms[which]
                 cols = slice(c, c + n)
-                away = self.rows(bases[i] + (1 - self.bit[m]) * count, count)
+                off = (1 - self.bit[m]) * count
+                away = self.rows(bases[i] + off, count)
                 if level == 1:
-                    got = self.r_core[a, pl.ds(pl.multiple_of((1 - self.bit[m]) * count, 16), count), cols]
-                    add(a, cols, bases[i] + (1 - self.bit[m]) * count, count, got)
+                    add(a, cols, bases[i] + off, count, self.r_core[a, self.rows(off, count), cols])
                 self.sends[a][away, cols] = self.sums[a][away, cols].astype(BF16)
                 copy = self.copy(
                     self.sends[a].at[away, cols], boxes.at[a, :, cols], self.sem(), {"clip": self.across[m]}
                 )
                 copy.start()
-                sent.append(copy)
-                new.append(bases[i] + self.bit[m] * count)
-            for i, (a, c, n, *ms) in enumerate(self.pieces):
+                flying[level, i] = copy
+            for i in members:
+                a, c, n, *ms = self.pieces[i]
+                m = ms[which]
                 cols = slice(c, c + n)
+                off = self.bit[m] * count
+                bases[i] = bases[i] + off
                 if level == 1:
-                    m = ms[which]
-                    got = self.r_core[a, pl.ds(pl.multiple_of(self.bit[m] * count, 16), count), cols]
-                    add(a, cols, new[i], count, got)
-            for i, (a, c, n, *ms) in enumerate(self.pieces):
-                sent[i].wait()
+                    add(a, cols, bases[i], count, self.r_core[a, self.rows(off, count), cols])
+
+        def end_half(level, members, boxes):
+            for i in members:
+                a, c, n, *ms = self.pieces[i]
                 cols = slice(c, c + n)
-                add(a, cols, new[i], count, boxes[a, :, cols])
-            return new
-
+                flying[level, i].wait()
+                add(a, cols, bases[i], halves[level], boxes[a, :, cols])
+
+        trading = exchange_small({"clip": self.across[1]})
+        wait_core((1, 2))
+        start_half(1, groups[0], self.r_one, 0)
+        wait_core((0,))
+        start_half(1, groups[1], self.r_one, 0)
+        join_small(trading)
         trading = exchange_small({"clip": self.across[self.masks[1]]})
-        bases = half_step(1, [base] * 4, self.r_one, 0)
+        between(0)
+        end_half(1, groups[0], self.r_one)
+        start_half(2, groups[0], self.r_two, 1)
+        end_half(1, groups[1], self.r_one)
+        start_half(2, groups[1], self.r_two, 1)
         join_small(trading)
         trading = exchange_small({"clip": self.across[self.pieces[0][4]]})
-        bases = half_step(2, bases, self.r_two, 1)
+        between(1)
+        end_half(2, groups[0], self.r_two)
+        if not self.extra:
+            self.start_quarters(0, bases)
+        end_half(2, groups[1], self.r_two)
+        if not self.extra:
+            self.start_quarters(1, bases)
         join_small(trading)
         count = halves[2]
         for n_extra, m in enumerate(self.extra):
@@ -179,92 +201,119 @@
                 here = self.rows(bases[i], count)
                 self.sums[a][here, cols] = self.sends[a][here, cols].astype(F32) + box[...].astype(F32)
             join_small(trading)
-
-        chunks = []
-        for first in (0, 2):
-            for q in range(4):
-                a, c, n = self.pieces[first + q // 2][:3]
-                cols = slice(c + (q % 2) * (n // 2), c + (q % 2) * (n // 2) + n // 2)
-                chunks.append((first // 2, q, a, cols, bases[first + q // 2], n // 2))
-        parts = self.tm_count
-        arrival = {0: self.sem(parts), 1: self.sem(parts)}
-        departure = {}
-        for which, q, a, cols, at, n in chunks:
-            departure[which, q] = self.sem()
-            here = self.rows(at, count)
+        if self.extra:
+            self.start_quarters(0, bases)
+            self.start_quarters(1, bases)
+        trading = exchange_small({"tm": self.tm + 1 - 2 * (self.tm % 2)})
+        between(2)
+        join_small(trading)
+        trading = exchange_small({"tm": self.tm + 2 - 4 * (self.tm // 2)})
+        self.settle_quarters(0)
+        self.settle_quarters(1)
+        join_small(trading)
+        between(3)
+
+        def start_back(level, members, which):
+            count = halves[level]
+            for i in members:
+                a, c, n, *ms = self.pieces[i]
+                m = ms[which]
+                place = self.gathered.at[a, self.rows(bases[i], count), slice(c, c + n)]
+                copy = self.copy(place, place, self.sem(), {"clip": self.across[m]})
+                copy.start()
+                flying[level, i] = copy
+                bases[i] = bases[i] - self.bit[m] * count
+
+        def end_back(level, members):
+            for i in members:
+                flying[level, i].wait()
+
+        def start_core_back(arrays):
+            for a in arrays:
+                place = self.gathered.at[a, self.rows(base, halves[0]), :]
+                copy = self.copy(place, place, self.sem(), {"clip": self.across[1]})
+                copy.start()
+                flying[0, a] = copy
+
+        self.end_quarters(0)
+        start_back(2, groups[0], 1)
+        self.end_quarters(1)
+        start_back(2, groups[1], 1)
+        between(4)
+        end_back(2, groups[0])
+        start_back(1, groups[0], 0)
+        end_back(2, groups[1])
+        start_back(1, groups[1], 0)
+        between(5)
+        end_back(1, groups[0])
+        start_core_back((1, 2))
+        end_back(1, groups[1])
+        start_core_back((0,))
+        between(6)
+        for a in range(3):
+            flying[0, a].wait()
+
+    def start_quarters(self, which, bases):
+        if which == 0:
+            self.chunks, self.departure = {}, {}
+            parts = self.tm_count
+            self.arrival = [self.sem(parts), self.sem(parts)]
+            self.back = [self.sem(parts), self.sem(parts)]
+            self.outgoing = [self.sem(parts), self.sem(parts)]
+        for q in range(4):
+            i = 2 * which + q // 2
+            a, c, n = self.pieces[i][:3]
+            n = n // 2
+            cols = slice(c + (q % 2) * n, c + (q % 2) * n + n)
+            here = self.rows(bases[i], self.f // 8)
+            self.chunks[which, q] = (a, cols, here, n)
+            self.departure[which, q] = self.sem()
 
             def send(which=which, q=q, a=a, cols=cols, here=here, n=n):
                 self.sends[a][here, cols] = self.sums[a][here, cols].astype(BF16)
-                self.chunk_copy(which, q, a, cols, here, n, departure, arrival).start()
+                self.chunk_copy(which, q, a, cols, here, n).start()
 
             pl.when(self.tm != q)(send)
-        trading = exchange_small({"tm": self.tm + 1 - 2 * (self.tm % 2)})
-        join_small(trading)
-        trading = exchange_small({"tm": self.tm + 2 - 4 * (self.tm // 2)})
-        join_small(trading)
-        back = {0: self.sem(parts), 1: self.sem(parts)}
-        outgoing = self.sem(2 * parts)
-        for which, q, a, cols, at, n in chunks:
-            here = self.rows(at, count)
-
-            def settle(which=which, q=q, a=a, cols=cols, here=here, n=n):
+
+    def settle_quarters(self, which):
+        for q in range(4):
+            a, cols, here, n = self.chunks[which, q]
+
+            def settle(q=q, a=a, cols=cols, here=here, n=n):
                 total = self.sums[a][here, cols]
-                for other in range(parts):
+                for other in range(self.tm_count):
                     if other != q:
-                        pltpu.make_async_copy(
-                            self.r_tm.at[which, other, :, pl.ds(0, n)], self.r_tm.at[which, other, :, pl.ds(0, n)],
-                            self.recv_sems.at[arrival[which] + other],
-                        ).wait()
-                        total += self.r_tm[which, other, :, :n].astype(F32)
+                        box = self.r_tm.at[which, other, :, pl.ds(0, n)]
+                        pltpu.make_async_copy(box, box, self.recv_sems.at[self.arrival[which] + other]).wait()
+                        total += box[...].astype(F32)
                 self.own_chunk[0, which, :, :n] = total.astype(BF16)
-                self.publish(which, q, a, cols, here, n, back, outgoing, "start")
+                self.publish(which, q, a, cols, here, n, "start")
 
             pl.when(self.tm == q)(settle)
-        for which, q, a, cols, at, n in chunks:
-            here = self.rows(at, count)
-
-            def arrive(which=which, q=q, a=a, cols=cols, here=here, n=n):
-                self.chunk_copy(which, q, a, cols, here, n, departure, arrival).wait_send()
+
+    def end_quarters(self, which):
+        for q in range(4):
+            a, cols, here, n = self.chunks[which, q]
+
+            def arrive(q=q, a=a, cols=cols, here=here, n=n):
+                self.chunk_copy(which, q, a, cols, here, n).wait_send()
                 place = self.gathered.at[a, here, cols]
-                pltpu.make_async_copy(place, place, self.recv_sems.at[back[which] + q]).wait()
-
-            def left(which=which, q=q, a=a, cols=cols, here=here, n=n):
-                self.publish(which, q, a, cols, here, n, back, outgoing, "wait")
+                pltpu.make_async_copy(place, place, self.recv_sems.at[self.back[which] + q]).wait()
+
+            def left(q=q, a=a, cols=cols, here=here, n=n):
+                self.publish(which, q, a, cols, here, n, "wait")
 
             pl.when(self.tm != q)(arrive)
             pl.when(self.tm == q)(left)
 
-        for level, which in ((2, 1), (1, 0)):
-            count = halves[level]
-            sent = []
-            for i, (a, c, n, *ms) in enumerate(self.pieces):
-                m = ms[which]
-                cols = slice(c, c + n)
-                place = self.gathered.at[a, self.rows(bases[i], count), cols]
-                copy = self.copy(place, place, self.sem(), {"clip": self.across[m]})
-                copy.start()
-                sent.append((copy, self.gathered.at[a, self.rows(bases[i] + (1 - 2 * self.bit[m]) * count, count), cols]))
-                bases[i] = bases[i] - self.bit[m] * count
-            for copy, theirs in sent:
-                copy.wait_send()
-                copy.wait_recv()
-        sent = []
-        for a in range(3):
-            place = self.gathered.at[a, self.rows(base, halves[0]), :]
-            copy = self.copy(place, place, self.sem(), {"clip": self.across[1]})
-            copy.start()
-            sent.append(copy)
-        for copy in sent:
-            copy.wait()
-
-    def chunk_copy(self, which, q, a, cols, here, n, departure, arrival):
+    def chunk_copy(self, which, q, a, cols, here, n):
         return pltpu.make_async_remote_copy(
             src_ref=self.sends[a].at[here, cols], dst_ref=self.r_tm.at[which, self.tm, :, pl.ds(0, n)],
-            send_sem=self.send_sems.at[departure[which, q]], recv_sem=self.recv_sems.at[arrival[which] + self.tm],
+            send_sem=self.send_sems.at[self.departure[which, q]], recv_sem=self.recv_sems.at[self.arrival[which] + self.tm],
             device_id={"tm": q}, device_id_type=MESH,
         )
 
-    def publish(self, which, q, a, cols, here, n, back, outgoing, do):
+    def publish(self, which, q, a, cols, here, n, do):
         place = self.gathered.at[a, here, cols]
         chunk = self.own_chunk.at[0, which, :, pl.ds(0, n)]
         local = pltpu.make_async_copy(chunk, place, self.local_sems.at[which])
@@ -272,22 +321,22 @@
         for other in range(self.tm_count):
             if other != q:
                 copy = pltpu.make_async_remote_copy(
-                    src_ref=chunk, dst_ref=place, send_sem=self.send_sems.at[outgoing + which * self.tm_count + other],
-                    recv_sem=self.recv_sems.at[back[which] + q], device_id={"tm": other}, device_id_type=MESH,
+                    src_ref=chunk, dst_ref=place, send_sem=self.send_sems.at[self.outgoing[which] + other],
+                    recv_sem=self.recv_sems.at[self.back[which] + q], device_id={"tm": other}, device_id_type=MESH,
                 )
                 copy.start() if do == "start" else copy.wait_send()
 
 
 def layer_kernel(
     lanes, spatial, features, hidden, tm_count, clip_count,
-    frames_ref, tok_hbm, tok_ref, cot_ref,
+    frames_ref, tok_ref, cot_ref,
     pre_gain_ref, pre_bias_ref, w_project_ref, query_bias_ref, value_bias_ref,
     w_out_ref, out_bias_ref, mid_gain_ref, mid_bias_ref, w_up_ref, up_bias_ref, w_down_ref, down_bias_ref,
-    out_ref, own_ref, above_ref, below_ref, gathered_ref, total_small_ref,
-    a_w, a_up, a_down, a_small, a_upb, low_s, up_s, gl_s, gu_s, n1_s, k_s, v_s, kt_s, vt_s, qt_s, p_s, inv_s, att_s, attt_s, res_s, n2_s, act_s, gh_s,
+    out_ref, own_ref, gathered_ref, total_small_ref,
+    a_w, a_up, a_down, a_small, a_upb, low_s, up_s, gl_s, gu_s, above_s, below_s, n1_s, k_s, v_s, kt_s, vt_s, qt_s, p_s, inv_s, att_s, attt_s, res_s, n2_s, act_s, gh_s,
     dao_s, dres_s, dq_s, dkv_s, dt_s,
     send_up, send_down, recv_low, recv_up, send_gl, send_gu, recv_above, recv_below,
-    s_w, s_up, s_down, r_core, r_one, r_two, r_tm, own_chunk, r_small, ar_send, ar_recv, ar_local,
+    s_w, r_core, r_one, r_two, r_tm, own_chunk, r_small, ar_send, ar_recv, ar_local,
 ):
     f = features
     pad = n1_s.shape[1] // GROUP
@@ -326,16 +375,16 @@
         )
 
     def rising(l):
-        return copy(tok_hbm.at[0, l], low_s.at[l + step_up], send_up.at[l], recv_low.at[l + step_up], higher)
+        return copy(gl_s.at[l], low_s.at[l + step_up], send_up.at[l], recv_low.at[l + step_up], higher)
 
     def falling(l):
-        return copy(tok_hbm.at[0, l], up_s.at[l - step_down], send_down.at[l], recv_up.at[l - step_down], lower)
+        return copy(gl_s.at[l], up_s.at[l - step_down], send_down.at[l], recv_up.at[l - step_down], lower)
 
     def returning_low(l):
-        return copy(gl_s.at[l], above_ref.at[0, l - step_down], send_gl.at[l], recv_above.at[l - step_down], lower)
+        return copy(gl_s.at[l], above_s.at[l - step_down], send_gl.at[l], recv_above.at[l - step_down], lower)
 
     def returning_up(l):
-        return copy(gu_s.at[l], below_ref.at[0, l + step_up], send_gu.at[l], recv_below.at[l + step_up], higher)
+        return copy(gu_s.at[l], below_s.at[l + step_up], send_gu.at[l], recv_below.at[l + step_up], higher)
 
     clip = lax.axis_index("clip")
     masks = [1 << i for i in range((clip_count - 1).bit_length())]
@@ -351,6 +400,8 @@
     pl.semaphore_wait(barrier, len(others) + len(masks))
 
     def start_tokens(l, carry):
+        xhat, _ = normalise(tok_ref[0, l].astype(F32))
+        gl_s[l] = (xhat * pre_gain + pre_bias).astype(BF16)
         pl.when(has_up(l))(lambda: rising(l).start())
         pl.when(has_low(l))(lambda: falling(l).start())
         return carry
@@ -361,10 +412,12 @@
         @pl.when(jnp.logical_not(has_low(l)))
         def _():
             low_s[l] = jnp.zeros(low_s.shape[1:], BF16)
+            below_s[l] = jnp.zeros(low_s.shape[1:], BF16)
 
         @pl.when(jnp.logical_not(has_up(l)))
         def _():
             up_s[l] = jnp.zeros(up_s.shape[1:], BF16)
+            above_s[l] = jnp.zeros(up_s.shape[1:], BF16)
 
         return carry
 
@@ -384,7 +437,7 @@
                 ref[pl.ds(j * pad + pad - 16, 16), :] = jnp.zeros((16, ref.shape[1]), ref.dtype)
 
     sums = Reduction(
-        f, hidden, tm, tm_count, masks, bit, across, others, (a_w, a_up, a_down), (s_w, s_up, s_down),
+        f, hidden, tm, tm_count, masks, bit, across, others, (a_w, a_up, a_down), (s_w, act_s.at[pl.ds(0, f), :], gh_s.at[pl.ds(0, f), :]),
         r_core, r_one, r_two, r_tm, own_chunk, gathered_ref, a_small, r_small, ar_send, ar_recv, ar_local,
     )
 
@@ -393,17 +446,14 @@
 
         def arrive(j, carry):
             l = base + j
-            pl.when(has_low(l))(lambda: copy(tok_hbm.at[0, l], low_s.at[l], send_up.at[l], recv_low.at[l], lower).wait_recv())
-            pl.when(has_up(l))(lambda: copy(tok_hbm.at[0, l], up_s.at[l], send_down.at[l], recv_up.at[l], higher).wait_recv())
+            pl.when(has_low(l))(lambda: copy(gl_s.at[l], low_s.at[l], send_up.at[l], recv_low.at[l], lower).wait_recv())
+            pl.when(has_up(l))(lambda: copy(gl_s.at[l], up_s.at[l], send_down.at[l], recv_up.at[l], higher).wait_recv())
             return carry
 
         lax.fori_loop(0, GROUP, arrive, 0)
 
         def forward(j, carry):
-            below, above = low_s[base + j].astype(F32), up_s[base + j].astype(F32)
-            for s, x in enumerate((below, tok_ref[0, base + j].astype(F32), above)):
-                xhat, _ = normalise(x)
-                n1 = (xhat * pre_gain + pre_bias).astype(BF16)
+            for s, n1 in enumerate((low_s[base + j], gl_s[base + j], up_s[base + j])):
                 n1_s[s, rows_of(j), :] = n1
                 kv = dot(n1, w_project_ref[:, f:])
                 k = kv[:, :f].astype(BF16)
@@ -476,9 +526,9 @@
             mlp(c, 0)
         a_up[...] += dot(n2_s[...], gh_s[...], TN)
         a_down[...] += dot(dao_s[...], act_s[...], TN)
-        pl.when(index == lanes // GROUP - 1)(lambda: sums.start_core((1, 2)))
         total_out = dot(act_s[...], w_down_ref[...]) + down_bias + res_s[...]
         grad_n2 = dot(gh_s[...], w_up_ref[...], NT)
+        pl.when(index == lanes // GROUP - 1)(lambda: sums.start_core((1, 2)))
         for j in range(GROUP):
             full = full_lane(base + j)
             mine = total_out[j * pad : j * pad + spatial]
@@ -538,26 +588,23 @@
         dq = dq_s[...]
         a_w[:, :f] += dot(n1_s[1], dq, TN)
         a_small[2:3, :] += column_sum(dq.astype(F32))
-        for s in range(3):
-            dkv = dkv_s[s]
-            a_w[:, f : 3 * f] += dot(n1_s[s], dkv, TN)
-            a_small[7:8, :] += column_sum(dkv[:, f:].astype(F32))
+        dkv = dkv_s[...].reshape(3 * GROUP * pad, 2 * f)
+        a_w[:, f : 3 * f] += dot(n1_s[...].reshape(3 * GROUP * pad, f), dkv, TN)
+        a_small[7:8, :] += column_sum(dkv[:, f:].astype(F32))
 
         def finish(j, carry):
-            below, above = low_s[base + j].astype(F32), up_s[base + j].astype(F32)
-            for s, x in enumerate((below, tok_ref[0, base + j].astype(F32), above)):
+            l = base + j
+            pl.when(has_up(l))(lambda: rising(l).wait_send())
+            pl.when(has_low(l))(lambda: falling(l).wait_send())
+            for s, box in enumerate((gl_s, low_s, gu_s)):
                 grad = dot(dkv_s[s, rows_of(j), :], w_project_ref[:, f:], NT)
                 if s == 1:
                     grad += dot(dq_s[rows_of(j), :], w_project_ref[:, :f], NT)
-                xhat, rate = normalise(x)
-                a_small[0:1, :] += column_sum(grad * xhat)
+                a_small[0:1, :] += column_sum(grad * n1_s[s, rows_of(j), :].astype(F32))
                 a_small[1:2, :] += column_sum(grad)
-                back = norm_back(grad, xhat, rate, pre_gain)
-                if s == 1:
-                    straight = jnp.where(full_lane(base + j), 0.0, cot_ref[0, base + j].astype(F32))
-                    own_ref[0, base + j] = (back + dres_s[rows_of(j), :] + straight).astype(BF16)
-                else:
-                    (gl_s if s == 0 else gu_s)[base + j] = back.astype(BF16)
+                box[l] = grad.astype(BF16)
+            straight = jnp.where(full_lane(l), 0.0, cot_ref[0, l].astype(F32))
+            own_ref[0, l] = (dres_s[rows_of(j), :] + straight).astype(BF16)
             return carry
 
         for j in range(GROUP):
@@ -573,38 +620,34 @@
         return carry
 
     lax.fori_loop(0, lanes // GROUP, group, 0)
+    def conclude(l, carry):
+        @pl.when(has_up(l))
+        def _():
+            returning_up(l).wait_send()
+            copy(gl_s.at[l], above_s.at[l], send_gl.at[l], recv_above.at[l], higher).wait_recv()
+
+        @pl.when(has_low(l))
+        def _():
+            returning_low(l).wait_send()
+            copy(gu_s.at[l], below_s.at[l], send_gu.at[l], recv_below.at[l], lower).wait_recv()
+
+        grad = low_s[l].astype(F32) + above_s[l].astype(F32) + below_s[l].astype(F32)
+        xhat, rate = normalise(tok_ref[0, l].astype(F32))
+        own_ref[0, l] = (norm_back(grad, xhat, rate, pre_gain) + own_ref[0, l].astype(F32)).astype(BF16)
+        return carry
+
+    bounds = [0] + [lanes * k // 16 for k in (4, 6, 8, 10, 12, 13, 14)] + [lanes]
+
+    def between(step):
+        lax.fori_loop(bounds[step], bounds[step + 1], conclude, 0)
+
     for i in range(hidden // f):
         a_small[8 + i : 9 + i, :] = a_upb[:, i * f : (i + 1) * f]
     sums.start_core((0,))
-    sums.run()
+    sums.run(between)
+    between(7)
     total_small_ref[...] = a_small[...]
-
-    def settle(l, carry):
-        @pl.when(has_up(l))
-        def _():
-            rising(l).wait_send()
-            returning_up(l).wait_send()
-            copy(gl_s.at[l], above_ref.at[0, l], send_gl.at[l], recv_above.at[l], higher).wait_recv()
-
-        @pl.when(has_low(l))
-        def _():
-            falling(l).wait_send()
-            returning_low(l).wait_send()
-            copy(gu_s.at[l], below_ref.at[0, l], send_gu.at[l], recv_below.at[l], lower).wait_recv()
-
-        return carry
-
-    lax.fori_loop(0, lanes, settle, 0)
-
-
-def finish_kernel(tm_ref, own_ref, above_ref, below_ref, out_ref):
-    tm, last = tm_ref[0], tm_ref[1]
-    for lane in range(WRAP):
-        total = own_ref[0, lane].astype(F32)
-        above, below = above_ref[0, lane].astype(F32), below_ref[0, lane].astype(F32)
-        total += above if lane < WRAP - 1 else jnp.where(tm < last, above, 0.0)
-        total += below if lane > 0 else jnp.where(tm > 0, below, 0.0)
-        out_ref[0, lane] = total.astype(BF16)
+    total_small_ref[0:1, :] = (a_small[0:1, :] - pre_bias * a_small[1:2, :]) / pre_gain
 
 
 def unpack_kernel(in_ref, project_ref, out_ref, up_ref, down_ref):
@@ -629,6 +672,7 @@
     dma = pltpu.SemaphoreType.DMA((lanes,))
     scratch = sums + [
         lane(lanes, spatial, f), lane(lanes, spatial, f), lane(lanes, spatial, f), lane(lanes, spatial, f),
+        lane(lanes, spatial, f), lane(lanes, spatial, f),
         lane(3, rows, f), lane(3, GROUP, spatial, f), lane(3, GROUP, spatial, f),
         lane(3, GROUP, f, spatial), lane(3, GROUP, f, spatial), lane(GROUP, f, spatial),
         lane(GROUP, f // HEAD_DIM, 3, spatial, spatial), pltpu.VMEM((GROUP, 8, spatial), F32),
@@ -638,22 +682,22 @@
     ] + [dma] * 8
     sems = pltpu.SemaphoreType.DMA((96,))
     scratch += [
-        lane(f, hidden), lane(f, hidden), lane(f, hidden), lane(3, f // 2, hidden), lane(3, f // 4, hidden),
+        lane(f, hidden), lane(3, f // 2, hidden), lane(3, f // 4, hidden),
         lane(3, f // 8, hidden), lane(2, tm_count, f // 8, hidden // 2), lane(1 + extra, 3, f // 8, hidden),
         pltpu.VMEM((masks + 2, 16, f), F32), sems, sems, pltpu.SemaphoreType.DMA((2,)),
     ]
     return pl.pallas_call(
         functools.partial(layer_kernel, lanes, spatial, f, hidden, tm_count, clip_count),
-        in_specs=[smem, hbm] + [vmem] * (2 + len(weights)),
-        out_specs=[vmem, vmem, hbm, hbm, hbm, vmem],
-        out_shape=[whole] * 4 + [jax.ShapeDtypeStruct((3, f, hidden), BF16), jax.ShapeDtypeStruct((16, f), F32)],
+        in_specs=[smem] + [vmem] * (2 + len(weights)),
+        out_specs=[vmem, vmem, hbm, vmem],
+        out_shape=[whole] * 2 + [jax.ShapeDtypeStruct((3, f, hidden), BF16), jax.ShapeDtypeStruct((16, f), F32)],
         scratch_shapes=scratch,
         name="layer",
         compiler_params=pltpu.CompilerParams(
             vmem_limit_bytes=63 * 1024 * 1024, collective_id=0, has_side_effects=True
         ),
         cost_estimate=pl.CostEstimate(flops=100 * 10**9, bytes_accessed=40 * 10**6, transcendentals=0),
-    )(frames, tokens, tokens, cotangent, *weights)
+    )(frames, tokens, cotangent, *weights)
 
 
 def body(
@@ -663,25 +707,13 @@
     lanes, spatial, f = tokens.shape[1:]
     hidden = w_up.shape[1]
     tm_count = lax.axis_size("tm")
-    tm_index = lax.axis_index("tm")
     weights = (
         pre_gain, pre_bias, w_project, query_bias, value_bias, w_out, out_bias,
         mid_gain, mid_bias, w_up, up_bias, w_down, down_bias,
     )
-    out, own, above, below, gathered, small = layer_call(
+    out, input_grad, gathered, small = layer_call(
         lanes, spatial, f, hidden, tm_count, lax.axis_size("clip"), lane_frames, tokens, cotangent, weights
     )
-    block = pl.BlockSpec((1, WRAP, spatial, f), lambda i: (0, i, 0, 0))
-    tm_arr = jnp.stack([tm_index, jnp.asarray(tm_count - 1, tm_index.dtype)]).astype(jnp.int32)
-    input_grad = pl.pallas_call(
-        finish_kernel,
-        grid=(lanes // WRAP,),
-        in_specs=[pl.BlockSpec(memory_space=pltpu.SMEM), block, block, block],
-        out_specs=block,
-        out_shape=jax.ShapeDtypeStruct(tokens.shape, BF16),
-        name="finish",
-    )(tm_arr, own, above, below)
-
     tall = 128
     wide_block = lambda n: pl.BlockSpec((tall, n), lambda i: (i, 0))
     g_project, g_out, g_up, g_down = pl.pallas_call(

time: 265 us -> 254 us (0.958)
  Pallas kernels: 251 us -> 241 us
    pallas_call x1 -> x0, Pallas kernels: 5.37 us -> none  [body(): pl.pallas_call(finish_kernel, grid=(lanes // WRAP,), in_specs=[pl.BlockSp...]
    pallas_call x1, Pallas kernels: 241 us -> 236 us  [layer_call(): pl.pallas_call(functools.partial(layer_kernel, lanes, spatial, f, hidden,...]
where the time goes in v5:
time: 254 us
  Pallas kernels  241 us (95%)
  local copies, waits for them, and re-layouts  12.3 us (5%)
    pallas_call x1, Pallas kernels, layer_call(): pl.pallas_call(functools.partial(layer_kernel, lanes, spatial, f, hidden,...  236 us
    unnamed x10, local copies, waits for them, and re-layouts  11.1 us
    pallas_call x1, Pallas kernels, body(): pl.pallas_call(unpack_kernel, grid=(f // tall,), in_specs=[pl.BlockSpec((...  5.23 us

profile of v5, /device:TPU:0, one launch (start us, length us, event | category | flops | bytes accessed | tf_op | source)
XLA Modules:
  0.0 253.9 jit_solution(15710972864222886465)
XLA Ops:
  0.6 0.0 copy-start.1
  0.7 3.8 %copy.31.tok_ref = bf16[1,16,196,384]{3,2,1,0:T(8,128)(2,1)} copy(bf16[1,16,196,384]{3,1,2,0:T(8,128)(2,1)} %param.16) | data formatting | bytes 4816896 | tf_op args[0]
  4.5 0.0 copy-done.1
  4.5 2.0 copy.32.cot_ref
  6.4 235.7 %layer.1 = (bf16[1,16,196,384]{3,2,1,0:T(8,128)(2,1)}, bf16[1,16,196,384]{3,2,1,0:T(8,128)(2,1)}, bf16[3,384,1536]{2,1,0:T(8,128)(2,1)}, f32[16,384]{1,0:T(8,128)}) custom-call(s32[16]{0:T(128)} %frames_ref.1, bf16[1,16,196,384]{3,2,1,0:T(8,128)(2,1)} %copy.31.tok_ref, bf16[1,16,196,384]{3,2,1,0:T(8,128)(2,1)} %copy.32.cot_ref, bf16[384]{0:T(512)(128)(2,1)} %pre_gain_ref.1, ...), custom_call_target="tpu_custom_call" | custom-call | flops 99999997952 | bytes 40000000 | tf_op jit(solution)/shard_map/layer/pallas_call | solution.py:689
  242.1 0.0 copy-start.2
  242.1 0.0 copy-start
  242.1 3.6 %copy.33 = bf16[1,16,196,384]{3,1,2,0:T(8,128)(2,1)} copy(bf16[1,16,196,384]{3,2,1,0:T(8,128)(2,1)} %get-tuple-element.31) | data formatting | bytes 4816896
  245.7 0.0 copy-done.2
  245.7 0.6 slice_reduce_fusion
  246.3 0.6 reshape.33
  247.0 0.0 copy-done
  247.0 1.7 copy.34
  248.7 5.2 %unpack.1 = (f32[384,1152]{1,0:T(8,128)}, f32[384,384]{1,0:T(8,128)}, f32[384,1536]{1,0:T(8,128)}, f32[1536,384]{1,0:T(8,128)}) custom-call(bf16[3,384,1536]{2,1,0:T(8,128)(2,1)} %get-tuple-element.26.in_ref), custom_call_target="tpu_custom_call" | custom-call | tf_op jit(solution)/shard_map/unpack/pallas_call | solution.py:719
  (1 shorter events, 0.0 us)
Async XLA Ops:
  0.6 3.8 %copy-start.1 = (bf16[1,16,196,384]{3,1,2,0:T(8,128)(2,1)S(1)}, bf16[1,16,196,384]{3,1,2,0:T(8,128)(2,1)}, u32[]{:S(2)}) copy-start(bf16[1,16,196,384]{3,1,2,0:T(8,128)(2,1)} %param.17) | copy-start | bytes 7225348
  242.1 3.6 %copy-start.2 = (f32[16,384]{1,0:T(8,128)S(1)}, f32[16,384]{1,0:T(8,128)}, u32[]{:S(2)}) copy-start(f32[16,384]{1,0:T(8,128)} %get-tuple-element.25) | copy-start | bytes 73732
  242.1 4.8 %copy-start = (bf16[1,16,196,384]{3,2,1,0:T(8,128)(2,1)S(1)}, bf16[1,16,196,384]{3,2,1,0:T(8,128)(2,1)}, u32[]{:S(2)}) copy-start(bf16[1,16,196,384]{3,2,1,0:T(8,128)(2,1)} %get-tuple-element.32) | copy-start | bytes 7225348

commit v6 on v2

v6 whole, which is shorter than its diff:
```python
import functools

import jax
import jax.numpy as jnp
from jax import lax
from jax.experimental import pallas as pl
from jax.experimental.pallas import tpu as pltpu
from jax.sharding import PartitionSpec as P

HEAD_DIM = 64
GROUP = 2
WRAP = 4
MESH = pl.DeviceIdType.MESH
EPSILON = 1e-06
FAR = 1e30
F32 = jnp.float32
BF16 = jnp.bfloat16
NN = (((1,), (0,)), ((), ()))
NT = (((1,), (1,)), ((), ()))
TN = (((0,), (0,)), ((), ()))


def dot(a, b, dims=NN):
    return lax.dot_general(a, b, dims, preferred_element_type=F32)


def row_mean(value):
    return jnp.sum(value, -1, keepdims=True) * (1.0 / value.shape[-1])


def normalise(x):
    center = x - row_mean(x)
    rate = lax.rsqrt(row_mean(center * center) + EPSILON)
    return center * rate, rate


def norm_back(grad, xhat, rate, gain):
    e = grad * gain
    return rate * (e - row_mean(e) - xhat * row_mean(e * xhat))


def gelu_parts(h):
    size = jnp.abs(h)
    bell = jnp.exp(-0.5 * (h * h))
    whole = 1.0 + 0.23164190 * size
    t = pl.reciprocal(whole, approx=True)
    t = t * (2.0 - whole * t)
    poly = t * (0.127414796 + t * (-0.142248368 + t * (0.7107068705 + t * (-0.7265760135 + t * 0.5307027145))))
    tail = poly * bell
    phi = jnp.where(h >= 0.0, 1.0 - tail, tail)
    return jnp.maximum(h, 0.0) - size * tail, phi + h * (bell * 0.3989422804014327)


def column_sum(value):
    return jnp.sum(value, 0, keepdims=True)


UP, DOWN, W = 1, 2, 0
LATE = 1
TALL = 128
TAIL = [(W, 0), ("trade", 0), ("lanes", 2), (UP, 3), (DOWN, 3), ("give",), (W, 1), ("trade", 1), ("lanes", 3), (W, 2), ("trade", 2), (UP, 4), (DOWN, 4), (W, 3), ("trade", 3), (UP, 5), (DOWN, 5), (W, 4), ("trade", 4), ("lanes", 4), (UP, 6), (DOWN, 6), ("trade", 5), (W, 5), (UP, 7), (DOWN, 7), (W, 6), (W, 7), ("lanes", 6), (UP, 8), (DOWN, 8), (W, 8)]


class Reduction:
    def __init__(
        self, f, hidden, tm, tm_count, masks, bit, across, sums, sends,
        r_core, r_one, r_two, r_more, r_tm, own_chunk, gathered, small, r_small, send_sems, recv_sems, local_sems,
    ):
        self.f, self.hidden, self.tm, self.tm_count = f, hidden, tm, tm_count
        self.masks, self.bit, self.across = masks, bit, across
        self.sums, self.sends = sums, sends
        self.r_core, self.r_one, self.r_two, self.r_more, self.r_tm = r_core, r_one, r_two, r_more, r_tm
        self.own_chunk, self.gathered, self.small, self.r_small = own_chunk, gathered, small, r_small
        self.send_sems, self.recv_sems, self.local_sems = send_sems, recv_sems, local_sems
        half = (len(masks) - 1) // 2
        self.more = masks[2 : 1 + half] + masks[2 + half :]
        one, two = masks[1], masks[1 + half]
        wide = hidden // 2
        self.pieces = [(slice(0, wide), one, two), (slice(wide, hidden), two, one)]
        self.core = bit[1] * (f // 2)
        self.level_one = [self.core + bit[m] * (f // 4) for _, m, _ in self.pieces]
        self.level_two = [at + bit[m] * (f // 8) for at, (_, _, m) in zip(self.level_one, self.pieces)]
        self.used, self.known, self.flying = 0, {}, {}

    def sem(self, name, n=1):
        if name not in self.known:
            self.known[name] = self.used
            self.used += n
        return self.known[name]

    def copy(self, name, src, dst, device):
        at = self.sem(name)
        return pltpu.make_async_remote_copy(
            src_ref=src, dst_ref=dst, send_sem=self.send_sems.at[at], recv_sem=self.recv_sems.at[at],
            device_id=device, device_id_type=MESH,
        )

    def rows(self, at, count):
        return pl.ds(pl.multiple_of(at, 16), count)

    def add(self, a, cols, at, count, got):
        where = self.rows(at, count)
        self.sums[a][where, cols] += got.astype(F32)

    def core_copy(self, a):
        count = self.f // 2
        away = self.rows((1 - self.bit[1]) * count, count)
        return self.copy(("core", a), self.sends[a].at[away, :], self.r_core.at[a], {"clip": self.across[1]})

    def half_copy(self, level, a, i):
        cols, *ms = self.pieces[i]
        count = self.f // (4 * level)
        m = ms[level - 1]
        start = self.core if level == 1 else self.level_one[i]
        away = self.rows(start + (1 - self.bit[m]) * count, count)
        box = (self.r_one, self.r_two)[level - 1]
        return self.copy(
            ("half", level, a, i), self.sends[a].at[away, cols], box.at[a, :, cols], {"clip": self.across[m]}
        )

    def start_half(self, level, a):
        count = self.f // (4 * level)
        for i, (cols, *ms) in enumerate(self.pieces):
            m = ms[level - 1]
            off = (1 - self.bit[m]) * count
            start = self.core if level == 1 else self.level_one[i]
            if level == 1:
                self.add(a, cols, start + off, count, self.r_core[a, self.rows(off, count), cols])
            away = self.rows(start + off, count)
            self.sends[a][away, cols] = self.sums[a][away, cols].astype(BF16)
            self.half_copy(level, a, i).start()
        if level == 1:
            for i, (cols, m, _) in enumerate(self.pieces):
                off = self.bit[m] * count
                self.add(a, cols, self.core + off, count, self.r_core[a, self.rows(off, count), cols])

    def end_half(self, level, a):
        count = self.f // (4 * level)
        for i, (cols, *_) in enumerate(self.pieces):
            self.half_copy(level, a, i).wait()
            at = (self.level_one, self.level_two)[level - 1][i]
            self.add(a, cols, at, count, (self.r_one, self.r_two)[level - 1][a, :, cols])

    def chunk(self, q):
        n = self.hidden // 4
        return slice(q * n, (q + 1) * n), self.rows(self.level_two[q // 2], self.f // 8)

    def chunk_copy(self, a, q):
        cols, here = self.chunk(q)
        return pltpu.make_async_remote_copy(
            src_ref=self.sends[a].at[here, cols], dst_ref=self.r_tm.at[a, self.tm],
            send_sem=self.send_sems.at[self.sem(("leave", a, q))],
            recv_sem=self.recv_sems.at[self.sem(("meet", a), self.tm_count) + self.tm],
            device_id={"tm": q}, device_id_type=MESH,
        )

    def publish(self, a, q, do):
        cols, here = self.chunk(q)
        place, mine = self.gathered.at[a, here, cols], self.own_chunk.at[a]
        local = pltpu.make_async_copy(mine, place, self.local_sems.at[a])
        local.start() if do == "start" else local.wait()
        for other in range(self.tm_count):
            if other != q:
                copy = pltpu.make_async_remote_copy(
                    src_ref=mine, dst_ref=place, send_sem=self.send_sems.at[self.sem(("out", a), self.tm_count) + other],
                    recv_sem=self.recv_sems.at[self.sem(("back", a), self.tm_count) + q],
                    device_id={"tm": other}, device_id_type=MESH,
                )
                copy.start() if do == "start" else copy.wait_send()

    def back_copy(self, level, a, i):
        cols, *ms = self.pieces[i]
        at, count = (self.level_two, self.level_one)[2 - level][i], self.f // (4 * level)
        place = self.gathered.at[a, self.rows(at, count), cols]
        return self.copy(("return", level, a, i), place, place, {"clip": self.across[ms[level - 1]]})

    def core_back(self, a):
        place = self.gathered.at[a, self.rows(self.core, self.f // 2), :]
        return self.copy(("core back", a), place, place, {"clip": self.across[1]})

    def step(self, a, n):
        if n == 0:
            count = self.f // 2
            away = self.rows((1 - self.bit[1]) * count, count)
            self.sends[a][away, :] = self.sums[a][away, :].astype(BF16)
            self.core_copy(a).start()
        elif n == 1:
            self.core_copy(a).wait()
            self.start_half(1, a)
        elif n == 2:
            self.end_half(1, a)
            self.start_half(2, a)
        elif n == 3:
            self.end_half(2, a)
            count = self.f // 8
            for k, m in enumerate(self.more):
                for i, (cols, *_) in enumerate(self.pieces):
                    here = self.rows(self.level_two[i], count)
                    box = self.r_more.at[k, a, :, cols]
                    self.sends[a][here, cols] = self.sums[a][here, cols].astype(BF16)
                    copy = self.copy(("more", k, a, i), self.sends[a].at[here, cols], box, {"clip": self.across[m]})
                    copy.start()
                    copy.wait()
                    self.sums[a][here, cols] = self.sends[a][here, cols].astype(F32) + box[...].astype(F32)
            for q in range(4):

                def send(q=q):
                    cols, here = self.chunk(q)
                    self.sends[a][here, cols] = self.sums[a][here, cols].astype(BF16)
                    self.chunk_copy(a, q).start()

                pl.when(self.tm != q)(send)
        elif n == 4:
            for q in range(4):

                def settle(q=q):
                    cols, here = self.chunk(q)
                    total = self.sums[a][here, cols]
                    for other in range(self.tm_count):
                        if other != q:
                            box = self.r_tm.at[a, other]
                            at = self.sem(("meet", a), self.tm_count) + other
                            pltpu.make_async_copy(box, box, self.recv_sems.at[at]).wait()
                            total += box[...].astype(F32)
                    self.own_chunk[a] = total.astype(BF16)
                    self.publish(a, q, "start")

                pl.when(self.tm == q)(settle)
        elif n == 5:
            for q in range(4):

                def arrive(q=q):
                    self.chunk_copy(a, q).wait_send()
                    cols, here = self.chunk(q)
                    place = self.gathered.at[a, here, cols]
                    at = self.sem(("back", a), self.tm_count) + q
                    pltpu.make_async_copy(place, place, self.recv_sems.at[at]).wait()

                pl.when(self.tm != q)(arrive)
                pl.when(self.tm == q)(functools.partial(self.publish, a, q, "wait"))
            for i in range(2):
                self.back_copy(2, a, i).start()
        elif n == 6:
            for i in range(2):
                self.back_copy(2, a, i).wait()
            for i in range(2):
                self.back_copy(1, a, i).start()
        elif n == 7:
            for i in range(2):
                self.back_copy(1, a, i).wait()
            self.core_back(a).start()
        else:
            self.core_back(a).wait()

    def trade(self, k, do):
        if k < len(self.masks):
            device = {"clip": self.across[self.masks[k]]}
        else:
            m = 1 << (k - len(self.masks))
            device = {"tm": self.tm + m - 2 * m * ((self.tm // m) % 2)}
        copy = self.copy(("small", k), self.small, self.r_small.at[k], device)
        if do == "start":
            copy.start()
        else:
            copy.wait()
            self.small[...] += self.r_small[k]

    def trades(self):
        return len(self.masks) + (self.tm_count - 1).bit_length()


def layer_kernel(
    lanes, spatial, features, hidden, tm_count, clip_count,
    frames_ref, tok_hbm, cot_hbm,
    pre_gain_ref, pre_bias_ref, w_project_hbm, query_bias_ref, value_bias_ref,
    w_out_hbm, out_bias_ref, mid_gain_ref, mid_bias_ref, w_up_hbm, up_bias_ref, w_down_hbm, down_bias_ref,
    out_hbm, own_ref, gathered_ref, total_small_ref,
    a_w, a_up, a_down, a_small, a_upb, low_s, up_s, gl_s, above_s, below_s, raw_s, tok_s, cot_s, out_s,
    w_project_ref, w_out_ref, w_up_ref, w_down_ref, n1_s, k_s, v_s, kt_s, vt_s, qt_s, p_s, inv_s, att_s, attt_s, res_s, n2_s, act_s, gh_s,
    dao_s, dq_s, dkv_s, dt_s,
    send_up, send_down, recv_low, recv_up, send_gl, send_gu, recv_above, recv_below,
    raw_sems, weight_sems, out_sems, s_w, r_core, r_one, r_two, r_more, r_tm, own_chunk, r_small, ar_send, ar_recv, ar_local,
):
    f = features
    pad = n1_s.shape[2] // GROUP
    heads = f // HEAD_DIM
    tm = lax.axis_index("tm")
    last = tm_count - 1
    at_low, at_high = tm == 0, tm == last
    higher, lower = lax.rem(tm + 1, tm_count), lax.rem(tm + last, tm_count)
    step_up, step_down = (tm + 1) // tm_count, (tm_count - tm) // tm_count

    def row(ref):
        return ref[...].astype(F32).reshape(1, -1)

    pre_gain, pre_bias, mid_gain, mid_bias = row(pre_gain_ref), row(pre_bias_ref), row(mid_gain_ref), row(mid_bias_ref)
    out_bias, down_bias, up_bias = row(out_bias_ref), row(down_bias_ref), row(up_bias_ref)
    query_bias, value_bias = row(query_bias_ref), row(value_bias_ref)

    def full_lane(l):
        return frames_ref[l] > 0

    def joined(l):
        frames = frames_ref[l]
        inner_low = ((frames == 4 * tm_count) & (l % 2 > 0)) | ((frames == 8 * tm_count) & (l % 4 > 0))
        inner_up = ((frames == 4 * tm_count) & (l % 2 < 1)) | ((frames == 8 * tm_count) & (l % 4 < 3))
        return (frames > 0) & (inner_low | (tm > 0)), (frames > 0) & (inner_up | (tm < last))

    def has_low(l):
        return jnp.logical_or(tm > 0, lax.rem(l, WRAP) != 0)

    def has_up(l):
        return jnp.logical_or(tm < last, lax.rem(l, WRAP) != WRAP - 1)

    def copy(src, dst, send, recv, device):
        return pltpu.make_async_remote_copy(
            src_ref=src, dst_ref=dst, send_sem=send, recv_sem=recv, device_id={"tm": device}, device_id_type=MESH
        )

    def rising(l):
        return copy(gl_s.at[l], low_s.at[l + step_up], send_up.at[l], recv_low.at[l + step_up], higher)

    def falling(l):
        return copy(gl_s.at[l], up_s.at[l - step_down], send_down.at[l], recv_up.at[l - step_down], lower)

    def returning_low(l):
        return copy(gl_s.at[l], above_s.at[l - step_down], send_gl.at[l], recv_above.at[l - step_down], lower)

    def returning_up(l):
        return copy(up_s.at[l], below_s.at[l + step_up], send_gu.at[l], recv_below.at[l + step_up], higher)

    clip = lax.axis_index("clip")
    masks = [1 << i for i in range((clip_count - 1).bit_length())]
    bit = {m: (clip // m) % 2 for m in masks}
    across = {m: clip + m * (1 - 2 * bit[m]) for m in masks}
    others = [lax.rem(tm + i, tm_count) for i in range(1, tm_count)]

    third = spatial // 3 // 16 * 16
    cuts = [(0, third), (third, third), (2 * third, spatial - 2 * third)]

    def raw_copy(hbm, start, count):
        place = pl.ds(start, count)
        return pltpu.make_async_copy(hbm.at[0, place], raw_s.at[place], raw_sems.at[start // third])

    moved = ((w_project_hbm, w_project_ref), (w_out_hbm, w_out_ref), (w_up_hbm, w_up_ref), (w_down_hbm, w_down_ref))
    for start, count in cuts:
        raw_copy(tok_hbm, start, count).start()
    for i, (hbm, ref) in enumerate(moved):
        pltpu.make_async_copy(hbm, ref, weight_sems.at[i]).start()

    barrier = pltpu.get_barrier_semaphore()
    for device in others:
        pl.semaphore_signal(barrier, inc=1, device_id={"tm": device}, device_id_type=MESH)
    for m in masks:
        pl.semaphore_signal(barrier, inc=1, device_id={"clip": across[m]}, device_id_type=MESH)
    pl.semaphore_wait(barrier, len(others) + len(masks))

    def store(g):
        return pltpu.make_async_copy(out_s.at[g % 2], out_hbm.at[0, pl.ds(g * GROUP, GROUP)], out_sems.at[g % 2])

    for start, count in cuts:
        raw_copy(tok_hbm, start, count).wait()
        tok_s[:, start : start + count, :] = jnp.transpose(raw_s[start : start + count], (1, 0, 2))
    for start, count in cuts:
        raw_copy(cot_hbm, start, count).start()

    def start_tokens(pair, carry):
        for l in (2 * pair, 2 * pair + 1):
            xhat, _ = normalise(tok_s[l].astype(F32))
            gl_s[l] = (xhat * pre_gain + pre_bias).astype(BF16)
        for l in (2 * pair, 2 * pair + 1):
            pl.when(has_up(l))(lambda: rising(l).start())
            pl.when(has_low(l))(lambda: falling(l).start())
        return carry

    lax.fori_loop(0, lanes // 2, start_tokens, 0)
    for start, count in cuts:
        raw_copy(cot_hbm, start, count).wait()
        cot_s[:, start : start + count, :] = jnp.transpose(raw_s[start : start + count], (1, 0, 2))
    for i, (hbm, ref) in enumerate(moved):
        pltpu.make_async_copy(hbm, ref, weight_sems.at[i]).wait()

    def fill(l, carry):
        @pl.when(jnp.logical_not(has_low(l)))
        def _():
            low_s[l] = jnp.zeros(low_s.shape[1:], BF16)
            below_s[l] = jnp.zeros(low_s.shape[1:], BF16)

        @pl.when(jnp.logical_not(has_up(l)))
        def _():
            up_s[l] = jnp.zeros(up_s.shape[1:], BF16)
            above_s[l] = jnp.zeros(up_s.shape[1:], BF16)

        return carry

    lax.fori_loop(0, lanes, fill, 0)

    for new in (a_w, a_up, a_down, a_small, a_upb):
        new[...] = jnp.zeros_like(new)

    vt_s[:, :, :, HEAD_DIM:, :] = jnp.ones((3, GROUP, heads, 16, spatial), BF16)

    def rows_of(j):
        return pl.ds(pl.multiple_of(j * pad, pad), spatial)

    for ref in (n1_s, dq_s, dkv_s):
        ref[...] = jnp.zeros_like(ref)
    for ref in (att_s, dao_s, res_s):
        for j in range(GROUP):
            ref[pl.ds(j * pad + pad - 16, 16), :] = jnp.zeros((16, ref.shape[1]), ref.dtype)

    sums = Reduction(
        f, hidden, tm, tm_count, masks, bit, across, (a_w, a_up, a_down),
        (s_w, act_s.at[pl.ds(0, f), :], gh_s.at[pl.ds(0, f), :]),
        r_core, r_one, r_two, r_more, r_tm, own_chunk, gathered_ref, a_small, r_small, ar_send, ar_recv, ar_local,
    )

    groups = lanes // GROUP

    def in_last(index, *steps):
        @pl.when(index == lanes // GROUP - 1)
        def _():
            for a, n in steps:
                sums.step(a, n)

    def group(index, carry):
        base = index * GROUP
        slot = index % 2
        pl.when(index >= 2)(lambda: store(index - 2).wait())

        def arrive(j, carry):
            l = base + j
            pl.when(has_low(l))(lambda: copy(gl_s.at[l], low_s.at[l], send_up.at[l], recv_low.at[l], lower).wait_recv())
            pl.when(has_up(l))(lambda: copy(gl_s.at[l], up_s.at[l], send_down.at[l], recv_up.at[l], higher).wait_recv())
            return carry

        lax.fori_loop(0, GROUP, arrive, 0)

        zero_half = jnp.zeros((HEAD_DIM, spatial), BF16)

        def pair_of(h):
            return slice(h // 2 * 2 * HEAD_DIM, (h // 2 + 1) * 2 * HEAD_DIM)

        def mine_of(h):
            return slice(h * HEAD_DIM, (h + 1) * HEAD_DIM)

        def in_pair(h, value):
            return jnp.concatenate([value, zero_half] if h % 2 == 0 else [zero_half, value], 0)

        def project(j, s):
            n1 = (low_s, gl_s, up_s)[s][base + j]
            n1_s[slot, s, rows_of(j), :] = n1
            kv = dot(n1, w_project_ref[:, f:])
            k = kv[:, :f].astype(BF16)
            v = (kv[:, f:] + value_bias).astype(BF16)
            k_s[s, j] = k
            v_s[s, j] = v
            kt_s[s, j] = k.T
            vt_s[s, j, :, :HEAD_DIM, :] = v.T.reshape(heads, HEAD_DIM, spatial)
            if s == 1:
                q = (dot(n1, w_project_ref[:, :f]) + query_bias).astype(BF16)
                qt_s[j] = (q * jnp.asarray(HEAD_DIM ** (-0.5), BF16)).T

        def get_scores(j, h):
            qz = in_pair(h, qt_s[j, mine_of(h), :])
            return [dot(k_s[s, j, :, pair_of(h)], qz) for s in range(3)]

        def attend(j, h, scores):
            low_ok, up_ok = joined(base + j)
            low_far, up_far = jnp.where(low_ok, 0.0, FAR), jnp.where(up_ok, 0.0, FAR)
            tops = [jnp.max(x, 0, keepdims=True) for x in scores]
            top = jnp.maximum(jnp.maximum(tops[0] - low_far, tops[2] - up_far), tops[1])
            attended = None
            for s, shift in enumerate((top + low_far, top, top + up_far)):
                low_prob = jnp.exp(scores[s] - shift).astype(BF16)
                p_s[j, h, s] = low_prob
                got = dot(vt_s[s, j, h], low_prob)
                attended = got if attended is None else attended + got
            inverse = 1.0 / attended[HEAD_DIM : HEAD_DIM + 1, :]
            inv_s[j, h : h + 1, :] = inverse
            attt_s[j, mine_of(h), :] = (attended[:HEAD_DIM, :] * inverse).astype(BF16)

        for s in (1, 0, 2):
            project(0, s)
        steps = [(j, h) for j in range(GROUP) for h in range(heads)]
        beside = {(j, h): [] for j, h in steps}
        for j in range(1, GROUP):
            for s, h in ((1, 0), (0, 2), (2, 4)):
                beside[j - 1, h].append(functools.partial(project, j, s))
        later = get_scores(0, 0)
        for i, (j, h) in enumerate(steps):
            scores = later
            for work in beside[j, h]:
                work()
            if i + 1 < len(steps):
                later = get_scores(*steps[i + 1])
            attend(j, h, scores)
            if h == heads - 1:
                att_s[rows_of(j), :] = attt_s[j].T
                res_s[rows_of(j), :] = tok_s[base + j].astype(F32)

        def sent(j, carry):
            l = base + j
            pl.when(has_up(l))(lambda: rising(l).wait_send())
            pl.when(has_low(l))(lambda: falling(l).wait_send())
            return carry

        lax.fori_loop(0, GROUP, sent, 0)

        residual = res_s[...] + dot(att_s[...], w_out_ref[...]) + out_bias
        res_s[...] = residual
        xhat2, rate2 = normalise(residual)
        n2_s[...] = (xhat2 * mid_gain + mid_bias).astype(BF16)
        for j in range(GROUP):
            full = full_lane(base + j)
            g = cot_s[base + j]
            dao_s[pl.ds(j * pad, spatial), :] = jnp.where(full, g.astype(F32), 0.0).astype(BF16)

        wide = 256

        def mlp(c, carry):
            cols = pl.ds(pl.multiple_of(c * wide, wide), wide)
            h = dot(n2_s[...], w_up_ref[:, cols]) + up_bias[:, c * wide : (c + 1) * wide]
            act, slope = gelu_parts(h)
            act_s[:, cols] = act.astype(BF16)
            gh = dot(dao_s[...], w_down_ref[cols, :], NT) * slope
            gh_s[:, cols] = gh.astype(BF16)
            a_upb[:, cols] += column_sum(gh)
            return carry

        before = project_back(1 - slot, jnp.maximum(base - GROUP, 0))
        chunks = hidden // wide
        for c in range(chunks):
            mlp(c, 0)
            for work in before[len(before) * c // chunks : len(before) * (c + 1) // chunks]:
                work()
        a_up[...] += dot(n2_s[...], gh_s[...], TN)
        a_down[...] += dot(dao_s[...], act_s[...], TN)
        total_out = dot(act_s[...], w_down_ref[...]) + down_bias + res_s[...]
        grad_n2 = dot(gh_s[...], w_up_ref[...], NT)
        in_last(index, (1, 0), (2, 0))
        for j in range(GROUP):
            full = full_lane(base + j)
            mine = total_out[j * pad : j * pad + spatial]
            out_s[slot, j] = jnp.where(full, mine, tok_s[base + j].astype(F32)).astype(BF16)
        store(index).start()
        g = dao_s[...].astype(F32)
        xhat2, rate2 = normalise(res_s[...])
        dres = g + norm_back(grad_n2, xhat2, rate2, mid_gain)
        for j in range(GROUP):
            straight = jnp.where(full_lane(base + j), 0.0, cot_s[base + j].astype(F32))
            own_ref[0, base + j] = (dres[j * pad : j * pad + spatial] + straight).astype(BF16)
        dao = dres.astype(BF16)
        dao_s[...] = dao
        a_small[3:4, :] += column_sum(dao.astype(F32))
        a_small[4:5, :] += column_sum(grad_n2 * xhat2)
        a_small[5:6, :] += column_sum(grad_n2)
        a_small[6:7, :] += column_sum(g)
        a_w[:, 3 * f :] += dot(att_s[...], dao, TN)

        def start_back(j):
            return dot(w_out_ref[...], dao_s[rows_of(j), :], NT).astype(BF16)

        def prepare(j, h, dt):
            dh = dt[mine_of(h), :].astype(F32) * inv_s[j, h : h + 1, :]
            delta = column_sum(dh * attt_s[j, mine_of(h), :].astype(F32))
            dh = dh.astype(BF16)
            dz = in_pair(h, dh)
            return dh, delta, [dot(v_s[s, j, :, pair_of(h)], dz) for s in range(3)]

        def attend_back(j, h, dh, delta, grad_probs):
            mine = mine_of(h)
            qh = qt_s[j, mine, :]
            probs = [p_s[j, h, s] for s in range(3)]
            for s in range(3):
                dt_s[4 + s, mine, :] = dot(dh, probs[s], NT).astype(BF16)
            ds = [(probs[s].astype(F32) * (grad_probs[s] - delta)).astype(BF16) for s in range(3)]
            for s in range(3):
                dt_s[1 + s, mine, :] = dot(qh, ds[s], NT).astype(BF16)
            grad_q = None
            for s in range(3):
                got = dot(kt_s[s, j, mine, :], ds[s])
                grad_q = got if grad_q is None else grad_q + got
            dt_s[0, mine, :] = (grad_q * HEAD_DIM ** (-0.5)).astype(BF16)

        dts = [start_back(j) for j in range(GROUP)]
        later = prepare(0, 0, dts[0])
        for i, (j, h) in enumerate(steps):
            now = later
            if i + 1 < len(steps):
                later = prepare(*steps[i + 1], dts[steps[i + 1][0]])
            attend_back(j, h, *now)
            if (j, h) == steps[len(steps) // 2 - 1]:
                in_last(index, (1, 1), (2, 1))
            if h == heads - 1:
                dq_s[slot, rows_of(j), :] = dt_s[0].T
                for s in range(3):
                    dkv_s[slot, s, rows_of(j), :f] = dt_s[1 + s].T
                    dkv_s[slot, s, rows_of(j), f:] = dt_s[4 + s].T

        in_last(index, (1, 2), (2, 2))
        pl.when(jnp.logical_and(index > 0, index < groups - LATE + 1))(lambda: give_back(base - GROUP))
        return carry

    def project_back(side, base):
        def weights_q():
            dq = dq_s[side]
            a_w[:, :f] += dot(n1_s[side, 1], dq, TN)
            a_small[2:3, :] += column_sum(dq.astype(F32))

        def weights_kv():
            dkv = dkv_s[side].reshape(3 * GROUP * pad, 2 * f)
            a_w[:, f : 3 * f] += dot(n1_s[side].reshape(3 * GROUP * pad, f), dkv, TN)
            a_small[7:8, :] += column_sum(dkv[:, f:].astype(F32))

        def rows_back(j, s):
            grad = dot(dkv_s[side, s, rows_of(j), :], w_project_ref[:, f:], NT)
            if s == 1:
                grad += dot(dq_s[side, rows_of(j), :], w_project_ref[:, :f], NT)
            a_small[0:1, :] += column_sum(grad * n1_s[side, s, rows_of(j), :].astype(F32))
            a_small[1:2, :] += column_sum(grad)
            (gl_s, low_s, up_s)[s][base + j] = grad.astype(BF16)

        rows_work = [functools.partial(rows_back, j, s) for j in range(GROUP) for s in range(3)]
        return [weights_q] + rows_work[:3] + [weights_kv] + rows_work[3:]

    def give_back(base):
        def one(j, carry):
            l = base + j
            pl.when(has_low(l))(lambda: returning_low(l).start())
            pl.when(has_up(l))(lambda: returning_up(l).start())
            return carry

        lax.fori_loop(0, GROUP, one, 0)

    lax.fori_loop(0, lanes // GROUP, group, 0)
    for work in project_back((lanes // GROUP - 1) % 2, lanes - GROUP):
        work()

    def conclude(pair, carry):
        for l in (2 * pair, 2 * pair + 1):

            @pl.when(has_up(l))
            def _(l=l):
                returning_up(l).wait_send()
                copy(gl_s.at[l], above_s.at[l], send_gl.at[l], recv_above.at[l], higher).wait_recv()

            @pl.when(has_low(l))
            def _(l=l):
                returning_low(l).wait_send()
                copy(up_s.at[l], below_s.at[l], send_gu.at[l], recv_below.at[l], lower).wait_recv()

        for l in (2 * pair, 2 * pair + 1):
            grad = low_s[l].astype(F32) + above_s[l].astype(F32) + below_s[l].astype(F32)
            xhat, rate = normalise(tok_s[l].astype(F32))
            own_ref[0, l] = (norm_back(grad, xhat, rate, pre_gain) + own_ref[0, l].astype(F32)).astype(BF16)
        return carry

    for i in range(hidden // f):
        a_small[8 + i : 9 + i, :] = a_upb[:, i * f : (i + 1) * f]
    for g in range(max(lanes // GROUP - 2, 0), lanes // GROUP):
        store(g).wait()
    done = 0
    for what in TAIL:
        if what[0] == "lanes":
            until = lanes // 2 * what[1] // 8
            lax.fori_loop(done, until, conclude, 0)
            done = until
        elif what[0] == "give":
            for i in range(LATE, 0, -1):
                give_back(lanes - i * GROUP)
        elif what[0] == "trade":
            k = what[1]
            if k > 0:
                sums.trade(k - 1, "join")
            if k < 5:
                sums.trade(k, "start")
        else:
            sums.step(*what)
    lax.fori_loop(done, lanes // 2, conclude, 0)
    for k in range(5, sums.trades()):
        sums.trade(k, "start")
        sums.trade(k, "join")
    total_small_ref[...] = a_small[...]
    total_small_ref[0:1, :] = (a_small[0:1, :] - pre_bias * a_small[1:2, :]) / pre_gain


def finish_kernel(
    out_in, grad_in, sums_ref, small_ref,
    out_ref, grad_ref, project_ref, w_out_ref, up_ref, down_ref,
    pre_gain_ref, pre_bias_ref, query_bias_ref, value_bias_ref, out_bias_ref, mid_gain_ref, mid_bias_ref, up_bias_ref,
    down_bias_ref,
):
    f = w_out_ref.shape[1]
    step = pl.program_id(0)
    out_ref[0] = jnp.transpose(out_in[0], (1, 0, 2))
    grad_ref[0] = jnp.transpose(grad_in[0], (1, 0, 2))

    @pl.when(jnp.logical_and(step % 2 == 0, step < 2 * f // TALL))
    def _():
        project_ref[...] = sums_ref[0, :, : 3 * f].astype(F32)
        w_out_ref[...] = sums_ref[0, :, 3 * f :].astype(F32)
        up_ref[...] = sums_ref[1].astype(F32)
        down_ref[...] = sums_ref[2].astype(F32).T

    @pl.when(step == 0)
    def _():
        vectors = (
            pre_gain_ref, pre_bias_ref, query_bias_ref, out_bias_ref, mid_gain_ref, mid_bias_ref, down_bias_ref,
            value_bias_ref,
        )
        for i, ref in enumerate(vectors):
            ref[...] = small_ref[i]
        for i in range(up_bias_ref.shape[0] // f):
            up_bias_ref[pl.ds(i * f, f)] = small_ref[8 + i]


def layer_call(lanes, spatial, f, hidden, tm_count, clip_count, frames, tokens, cotangent, weights):
    pad = -(-spatial // 16) * 16
    rows = GROUP * pad
    smem = pl.BlockSpec(memory_space=pltpu.SMEM)
    vmem = pl.BlockSpec(memory_space=pltpu.VMEM)
    hbm = pl.BlockSpec(memory_space=pl.ANY)
    masks = (clip_count - 1).bit_length()
    sums = [pltpu.VMEM(s, F32) for s in [(f, hidden)] * 3 + [(16, f), (1, hidden)]]
    whole = jax.ShapeDtypeStruct((1, lanes, spatial, f), BF16)
    lane = lambda *s: pltpu.VMEM(s, BF16)
    dma = pltpu.SemaphoreType.DMA((lanes,))
    scratch = sums + [
        lane(lanes, spatial, f), lane(lanes, spatial, f), lane(lanes, spatial, f), lane(lanes, spatial, f),
        lane(lanes, spatial, f),
        lane(spatial, lanes, f), lane(lanes, spatial, f), lane(lanes, spatial, f), lane(2, GROUP, spatial, f),
        lane(f, 3 * f), lane(f, f), lane(f, hidden), lane(hidden, f),
        lane(2, 3, rows, f), lane(3, GROUP, spatial, f), lane(3, GROUP, spatial, f),
        lane(3, GROUP, f, spatial), lane(3, GROUP, f // HEAD_DIM, HEAD_DIM + 16, spatial), lane(GROUP, f, spatial),
        lane(GROUP, f // HEAD_DIM, 3, spatial, spatial), pltpu.VMEM((GROUP, 8, spatial), F32),
        lane(rows, f), lane(GROUP, f, spatial), pltpu.VMEM((rows, f), F32), lane(rows, f),
        lane(rows, hidden), lane(rows, hidden), lane(rows, f),
        lane(2, rows, f), lane(2, 3, rows, 2 * f), lane(7, f, spatial),
    ] + [dma] * 8 + [pltpu.SemaphoreType.DMA((n,)) for n in (3, 4, 2)]
    sems = pltpu.SemaphoreType.DMA((96,))
    scratch += [
        lane(f, hidden), lane(3, f // 2, hidden), lane(3, f // 4, hidden),
        lane(3, f // 8, hidden), lane(max(masks - 3, 1), 3, f // 8, hidden), lane(3, tm_count, f // 8, hidden // 4),
        lane(3, f // 8, hidden // 4), pltpu.VMEM((masks + 2, 16, f), F32), sems, sems, pltpu.SemaphoreType.DMA((3,)),
    ]
    return pl.pallas_call(
        functools.partial(layer_kernel, lanes, spatial, f, hidden, tm_count, clip_count),
        in_specs=[smem, hbm, hbm] + [hbm if w.ndim == 2 else vmem for w in weights],
        out_specs=[hbm, vmem, hbm, vmem],
        out_shape=[whole] * 2 + [jax.ShapeDtypeStruct((3, f, hidden), BF16), jax.ShapeDtypeStruct((16, f), F32)],
        scratch_shapes=scratch,
        name="layer",
        compiler_params=pltpu.CompilerParams(
            vmem_limit_bytes=63 * 1024 * 1024, collective_id=0, has_side_effects=True
        ),
        cost_estimate=pl.CostEstimate(flops=100 * 10**9, bytes_accessed=40 * 10**6, transcendentals=0),
    )(frames, tokens, cotangent, *weights)


def body(
    tokens, cotangent, lane_frames, pre_gain, pre_bias, w_project, query_bias, value_bias,
    w_out, out_bias, mid_gain, mid_bias, w_up, up_bias, w_down, down_bias,
):
    lanes, spatial, f = tokens.shape[1:]
    hidden = w_up.shape[1]
    tm_count = lax.axis_size("tm")
    weights = (
        pre_gain, pre_bias, w_project, query_bias, value_bias, w_out, out_bias,
        mid_gain, mid_bias, w_up, up_bias, w_down, down_bias,
    )
    out, input_grad, gathered, small = layer_call(
        lanes, spatial, f, hidden, tm_count, lax.axis_size("clip"), lane_frames,
        tokens.transpose(0, 2, 1, 3), cotangent.transpose(0, 2, 1, 3), weights,
    )
    part = 32
    steps = max(-(-spatial // part), 2 * f // TALL)
    turn = lambda i: jnp.minimum(i, -(-spatial // part) - 1)
    tall = lambda i: jnp.minimum(i // 2, f // TALL - 1)
    lane_block = pl.BlockSpec((1, lanes, part, f), lambda i: (0, 0, turn(i), 0))
    token_block = pl.BlockSpec((1, part, lanes, f), lambda i: (0, turn(i), 0, 0))
    row_block = lambda n: pl.BlockSpec((TALL, n), lambda i: (tall(i), 0))
    vector = lambda n: pl.BlockSpec((n,), lambda i: (0,))
    sizes = [f] * 7 + [hidden, f]
    got = pl.pallas_call(
        finish_kernel,
        grid=(steps,),
        in_specs=[
            lane_block, lane_block, pl.BlockSpec((3, TALL, hidden), lambda i: (0, tall(i), 0)),
            pl.BlockSpec((16, f), lambda i: (0, 0)),
        ],
        out_specs=[
            token_block, token_block, row_block(3 * f), row_block(f), row_block(hidden),
            pl.BlockSpec((hidden, TALL), lambda i: (0, tall(i))),
        ] + [vector(n) for n in sizes],
        out_shape=[jax.ShapeDtypeStruct((1, spatial, lanes, f), BF16)] * 2
        + [jax.ShapeDtypeStruct(n, F32) for n in ((f, 3 * f), (f, f), (f, hidden), (hidden, f))]
        + [jax.ShapeDtypeStruct((n,), F32) for n in sizes],
        name="finish",
    )(out, input_grad, gathered, small)
    out, input_grad = (v.transpose(0, 2, 1, 3) for v in got[:2])
    g_project, g_out, g_up, g_down = got[2:6]
    pre_gain, pre_bias, query_bias, value_bias, out_bias, mid_gain, mid_bias, up_bias, down_bias = got[6:]
    return (
        out, input_grad, pre_gain, pre_bias, g_project, query_bias, value_bias, g_out, out_bias,
        mid_gain, mid_bias, g_up, up_bias, g_down, down_bias,
    )


def solution(mesh):
    spread = P("tm", "clip", None, None)
    return jax.shard_map(
        body,
        mesh=mesh,
        in_specs=(spread, spread, P("clip")) + (P(),) * 13,
        out_specs=(spread, spread) + (P(),) * 13,
        check_vma=False,
    )
```

time: 459 us -> 245 us (0.53)
  waiting for transfers between devices: 120 us -> 0 us
  local copies, waits for them, and re-layouts: 51.3 us -> 0 us
  Pallas kernels: 258 us -> 244 us
  other arithmetic: 13.6 us -> 0 us
  between operations: 14.2 us -> 0.84 us
    psum x1 -> x0, waiting for transfers between devices: 120 us -> none  [body(): packed = lax.psum(packed, ('tm', 'clip')).astype(F32)]
    reshape x17 -> x0, local copies, waits for them, and re-layouts: 24 us -> none  [the longest x8 4.55 us: body(): row = lambda v: v.astype(F32).reshape(1, -1)]
    unnamed x41 -> x0, local copies, waits for them, and re-layouts: 21.4 us -> none
    pallas_call x1, Pallas kernels: 247 us -> 233 us  [layer_call(): pl.pallas_call(functools.partial(layer_kernel, lanes, spatial, f, hidden,...]
    another operation x5 -> x0, other arithmetic: 8.48 us -> none
    slice x7 -> x0, local copies, waits for them, and re-layouts: 5.9 us -> none  [the longest x4 5.27 us: body(): parts.append(packed[at:at + n])]
  transfers between devices with their start and end apart: 1 -> 0, of which waited for: 1 -> 0; matrix products, arithmetic and copies ran while one was open for 2% -> 0% of each run, Pallas kernels for 2% -> 0%
where the time goes in v6:
time: 245 us
  Pallas kernels  244 us (100%)
    pallas_call x1, Pallas kernels, layer_call(): pl.pallas_call(functools.partial(layer_kernel, lanes, spatial, f, hidden,...  233 us
    pallas_call x1, Pallas kernels, body(): pl.pallas_call(finish_kernel, grid=(steps,), in_specs=[lane_block, lane_b...  11.8 us

profile of v6, /device:TPU:0, one launch (start us, length us, event | category | flops | bytes accessed | tf_op | source)
XLA Modules:
  0.0 245.1 jit_solution(1613657147000510864)
XLA Ops:
  0.7 232.5 %layer.1 = (bf16[1,16,196,384]{3,2,1,0:T(8,128)(2,1)}, bf16[1,16,196,384]{3,2,1,0:T(8,128)(2,1)}, bf16[3,384,1536]{2,1,0:T(8,128)(2,1)}, f32[16,384]{1,0:T(8,128)}) custom-call(s32[16]{0:T(128)} %frames_ref.1, bf16[1,196,16,384]{3,2,1,0:T(8,128)(2,1)} %bitcast.4, bf16[1,196,16,384]{3,2,1,0:T(8,128)(2,1)} %bitcast.5, bf16[384]{0:T(512)(128)(2,1)} %pre_gain_ref.1, ...), custom_call_target="tpu_custom_call" | custom-call | flops 99999997952 | bytes 40000000 | tf_op jit(solution)/shard_map/layer/pallas_call | solution.py:747
  233.2 11.8 %finish.1 = (bf16[1,196,16,384]{3,2,1,0:T(8,128)(2,1)}, bf16[1,196,16,384]{3,2,1,0:T(8,128)(2,1)}, f32[384,1152]{1,0:T(8,128)}, f32[384,384]{1,0:T(8,128)}, f32[...) custom-call(bf16[1,16,196,384]{3,2,1,0:T(8,128)(2,1)} %get-tuple-ele, ...), custom_call_target="tpu_custom_call" | custom-call | tf_op jit(solution)/shard_map/finish/pallas_call | solution.py:785

commit v7 on v6

--- a/solution.py
+++ b/solution.py
@@ -57,8 +57,12 @@
 
 UP, DOWN, W = 1, 2, 0
 LATE = 1
-TALL = 128
-TAIL = [(W, 0), ("trade", 0), ("lanes", 2), (UP, 3), (DOWN, 3), ("give",), (W, 1), ("trade", 1), ("lanes", 3), (W, 2), ("trade", 2), (UP, 4), (DOWN, 4), (W, 3), ("trade", 3), (UP, 5), (DOWN, 5), (W, 4), ("trade", 4), ("lanes", 4), (UP, 6), (DOWN, 6), ("trade", 5), (W, 5), (UP, 7), (DOWN, 7), (W, 6), (W, 7), ("lanes", 6), (UP, 8), (DOWN, 8), (W, 8)]
+TAIL = [
+    (W, 0), ("rows", 0, 6), (UP, 3), (DOWN, 3), ("trade", 0, "start"), ("lanes", 2), ("trade", 0, "join"), ("trade", 1, "start"), (W, 1), ("trade", 1, "join"), ("trade", 2, "start"), (W, 2),
+    ("lanes", 3), ("trade", 2, "join"), ("trade", 3, "start"), (W, 3), (UP, 4), (DOWN, 4), ("trade", 3, "join"), ("trade", 4, "start"), (W, 4), ("give",), (UP, 5), (DOWN, 5),
+    (W, 5), (UP, 6), (DOWN, 6), (W, 6), (UP, 7), (DOWN, 7), (W, 7), ("trade", 4, "join"), ("lanes", 4), ("lanes", 5), (UP, 8), (DOWN, 8),
+    (W, 8),
+]
 
 
 class Reduction:
@@ -274,12 +278,12 @@
     frames_ref, tok_hbm, cot_hbm,
     pre_gain_ref, pre_bias_ref, w_project_hbm, query_bias_ref, value_bias_ref,
     w_out_hbm, out_bias_ref, mid_gain_ref, mid_bias_ref, w_up_hbm, up_bias_ref, w_down_hbm, down_bias_ref,
-    out_hbm, own_ref, gathered_ref, total_small_ref,
-    a_w, a_up, a_down, a_small, a_upb, low_s, up_s, gl_s, above_s, below_s, raw_s, tok_s, cot_s, out_s,
+    out_hbm, grad_hbm, gathered_ref, total_small_ref,
+    a_w, a_up, a_down, a_small, a_upb, low_s, up_s, gl_s, above_s, below_s, own_s, raw_s, tok_s, cot_s, out_s,
     w_project_ref, w_out_ref, w_up_ref, w_down_ref, n1_s, k_s, v_s, kt_s, vt_s, qt_s, p_s, inv_s, att_s, attt_s, res_s, n2_s, act_s, gh_s,
     dao_s, dq_s, dkv_s, dt_s,
     send_up, send_down, recv_low, recv_up, send_gl, send_gu, recv_above, recv_below,
-    raw_sems, weight_sems, out_sems, s_w, r_core, r_one, r_two, r_more, r_tm, own_chunk, r_small, ar_send, ar_recv, ar_local,
+    raw_sems, weight_sems, out_sems, own_sems, s_w, r_core, r_one, r_two, r_more, r_tm, own_chunk, r_small, ar_send, ar_recv, ar_local,
 ):
     f = features
     pad = n1_s.shape[2] // GROUP
@@ -353,7 +357,6 @@
         pl.semaphore_signal(barrier, inc=1, device_id={"tm": device}, device_id_type=MESH)
     for m in masks:
         pl.semaphore_signal(barrier, inc=1, device_id={"clip": across[m]}, device_id_type=MESH)
-    pl.semaphore_wait(barrier, len(others) + len(masks))
 
     def store(g):
         return pltpu.make_async_copy(out_s.at[g % 2], out_hbm.at[0, pl.ds(g * GROUP, GROUP)], out_sems.at[g % 2])
@@ -363,6 +366,7 @@
         tok_s[:, start : start + count, :] = jnp.transpose(raw_s[start : start + count], (1, 0, 2))
     for start, count in cuts:
         raw_copy(cot_hbm, start, count).start()
+    pl.semaphore_wait(barrier, len(others) + len(masks))
 
     def start_tokens(pair, carry):
         for l in (2 * pair, 2 * pair + 1):
@@ -528,7 +532,7 @@
             a_upb[:, cols] += column_sum(gh)
             return carry
 
-        before = project_back(1 - slot, jnp.maximum(base - GROUP, 0))
+        before, _, _ = project_back(1 - slot, jnp.maximum(base - GROUP, 0))
         chunks = hidden // wide
         for c in range(chunks):
             mlp(c, 0)
@@ -549,7 +553,7 @@
         dres = g + norm_back(grad_n2, xhat2, rate2, mid_gain)
         for j in range(GROUP):
             straight = jnp.where(full_lane(base + j), 0.0, cot_s[base + j].astype(F32))
-            own_ref[0, base + j] = (dres[j * pad : j * pad + spatial] + straight).astype(BF16)
+            own_s[base + j] = (dres[j * pad : j * pad + spatial] + straight).astype(BF16)
         dao = dres.astype(BF16)
         dao_s[...] = dao
         a_small[3:4, :] += column_sum(dao.astype(F32))
@@ -622,7 +626,7 @@
             (gl_s, low_s, up_s)[s][base + j] = grad.astype(BF16)
 
         rows_work = [functools.partial(rows_back, j, s) for j in range(GROUP) for s in range(3)]
-        return [weights_q] + rows_work[:3] + [weights_kv] + rows_work[3:]
+        return [weights_q] + rows_work[:3] + [weights_kv] + rows_work[3:], [weights_q, weights_kv], rows_work
 
     def give_back(base):
         def one(j, carry):
@@ -634,8 +638,17 @@
         lax.fori_loop(0, GROUP, one, 0)
 
     lax.fori_loop(0, lanes // GROUP, group, 0)
-    for work in project_back((lanes // GROUP - 1) % 2, lanes - GROUP):
+    _, final_weights, final_rows = project_back((lanes // GROUP - 1) % 2, lanes - GROUP)
+    for work in final_weights:
         work()
+
+    def hand_over(pair):
+        place = pl.ds(2 * pair, 2)
+        return pltpu.make_async_copy(own_s.at[place], grad_hbm.at[0, place], own_sems.at[pair])
+
+    def handed_over(pair, carry):
+        hand_over(pair).wait()
+        return carry
 
     def conclude(pair, carry):
         for l in (2 * pair, 2 * pair + 1):
@@ -653,7 +666,8 @@
         for l in (2 * pair, 2 * pair + 1):
             grad = low_s[l].astype(F32) + above_s[l].astype(F32) + below_s[l].astype(F32)
             xhat, rate = normalise(tok_s[l].astype(F32))
-            own_ref[0, l] = (norm_back(grad, xhat, rate, pre_gain) + own_ref[0, l].astype(F32)).astype(BF16)
+            own_s[l] = (norm_back(grad, xhat, rate, pre_gain) + own_s[l].astype(F32)).astype(BF16)
+        hand_over(pair).start()
         return carry
 
     for i in range(hidden // f):
@@ -666,53 +680,96 @@
             until = lanes // 2 * what[1] // 8
             lax.fori_loop(done, until, conclude, 0)
             done = until
+        elif what[0] == "rows":
+            for work in final_rows[what[1] : what[2]]:
+                work()
         elif what[0] == "give":
             for i in range(LATE, 0, -1):
                 give_back(lanes - i * GROUP)
         elif what[0] == "trade":
-            k = what[1]
-            if k > 0:
-                sums.trade(k - 1, "join")
-            if k < 5:
-                sums.trade(k, "start")
+            sums.trade(what[1], what[2])
         else:
             sums.step(*what)
     lax.fori_loop(done, lanes // 2, conclude, 0)
     for k in range(5, sums.trades()):
         sums.trade(k, "start")
         sums.trade(k, "join")
+    lax.fori_loop(0, lanes // 2, handed_over, 0)
     total_small_ref[...] = a_small[...]
     total_small_ref[0:1, :] = (a_small[0:1, :] - pre_bias * a_small[1:2, :]) / pre_gain
 
 
 def finish_kernel(
-    out_in, grad_in, sums_ref, small_ref,
-    out_ref, grad_ref, project_ref, w_out_ref, up_ref, down_ref,
+    out_hbm, grad_hbm, sums_hbm, small_ref,
+    out_to, grad_to, project_to, w_out_to, up_to, down_to,
     pre_gain_ref, pre_bias_ref, query_bias_ref, value_bias_ref, out_bias_ref, mid_gain_ref, mid_bias_ref, up_bias_ref,
     down_bias_ref,
+    lane_s, turned_s, sums_s, project_s, w_out_s, up_s, down_s, in_sems, sum_sems, out_sems, wide_sems,
 ):
-    f = w_out_ref.shape[1]
-    step = pl.program_id(0)
-    out_ref[0] = jnp.transpose(out_in[0], (1, 0, 2))
-    grad_ref[0] = jnp.transpose(grad_in[0], (1, 0, 2))
-
-    @pl.when(jnp.logical_and(step % 2 == 0, step < 2 * f // TALL))
-    def _():
-        project_ref[...] = sums_ref[0, :, : 3 * f].astype(F32)
-        w_out_ref[...] = sums_ref[0, :, 3 * f :].astype(F32)
-        up_ref[...] = sums_ref[1].astype(F32)
-        down_ref[...] = sums_ref[2].astype(F32).T
-
-    @pl.when(step == 0)
-    def _():
-        vectors = (
-            pre_gain_ref, pre_bias_ref, query_bias_ref, out_bias_ref, mid_gain_ref, mid_bias_ref, down_bias_ref,
-            value_bias_ref,
-        )
-        for i, ref in enumerate(vectors):
-            ref[...] = small_ref[i]
-        for i in range(up_bias_ref.shape[0] // f):
-            up_bias_ref[pl.ds(i * f, f)] = small_ref[8 + i]
+    f, spatial = w_out_s.shape[1], lane_s.shape[2]
+    third = spatial // 3 // 16 * 16
+    cuts = [(0, third), (third, third), (2 * third, spatial - 2 * third)]
+    sides = ((out_hbm, out_to), (grad_hbm, grad_to))
+
+    def load(i, k):
+        start, count = cuts[k]
+        place = pl.ds(start, count)
+        return pltpu.make_async_copy(sides[i][0].at[0, :, place], lane_s.at[i, :, place], in_sems.at[i, k])
+
+    def store(i, k):
+        start, count = cuts[k]
+        place = pl.ds(start, count)
+        return pltpu.make_async_copy(turned_s.at[i, place], sides[i][1].at[0, place], out_sems.at[i, k])
+
+    def load_sums(a):
+        return pltpu.make_async_copy(sums_hbm.at[a], sums_s.at[a], sum_sems.at[a])
+
+    wide = ((up_s, up_to), (down_s, down_to), (project_s, project_to), (w_out_s, w_out_to))
+
+    def store_wide(i):
+        return pltpu.make_async_copy(*wide[i], wide_sems.at[i])
+
+    def turn(i, k):
+        load(i, k).wait()
+        start, count = cuts[k]
+        turned_s[i, start : start + count] = jnp.transpose(lane_s[i, :, start : start + count], (1, 0, 2))
+        store(i, k).start()
+
+    load_sums(1).start()
+    for k in range(3):
+        load(0, k).start()
+    load_sums(2).start()
+    for k in range(3):
+        load(1, k).start()
+    load_sums(0).start()
+    load_sums(1).wait()
+    up_s[...] = sums_s[1].astype(F32)
+    store_wide(0).start()
+    for k in range(3):
+        turn(0, k)
+    load_sums(2).wait()
+    down_s[...] = sums_s[2].T.astype(F32)
+    store_wide(1).start()
+    for k in range(3):
+        turn(1, k)
+    load_sums(0).wait()
+    project_s[...] = sums_s[0, :, : 3 * f].astype(F32)
+    w_out_s[...] = sums_s[0, :, 3 * f :].astype(F32)
+    store_wide(2).start()
+    store_wide(3).start()
+    vectors = (
+        pre_gain_ref, pre_bias_ref, query_bias_ref, out_bias_ref, mid_gain_ref, mid_bias_ref, down_bias_ref,
+        value_bias_ref,
+    )
+    for i, ref in enumerate(vectors):
+        ref[...] = small_ref[i]
+    for i in range(up_bias_ref.shape[0] // f):
+        up_bias_ref[pl.ds(i * f, f)] = small_ref[8 + i]
+    for i in range(2):
+        for k in range(3):
+            store(i, k).wait()
+    for i in range(4):
+        store_wide(i).wait()
 
 
 def layer_call(lanes, spatial, f, hidden, tm_count, clip_count, frames, tokens, cotangent, weights):
@@ -729,7 +786,7 @@
     scratch = sums + [
         lane(lanes, spatial, f), lane(lanes, spatial, f), lane(lanes, spatial, f), lane(lanes, spatial, f),
         lane(lanes, spatial, f),
-        lane(spatial, lanes, f), lane(lanes, spatial, f), lane(lanes, spatial, f), lane(2, GROUP, spatial, f),
+        lane(lanes, spatial, f), lane(spatial, lanes, f), lane(lanes, spatial, f), lane(lanes, spatial, f), lane(2, GROUP, spatial, f),
         lane(f, 3 * f), lane(f, f), lane(f, hidden), lane(hidden, f),
         lane(2, 3, rows, f), lane(3, GROUP, spatial, f), lane(3, GROUP, spatial, f),
         lane(3, GROUP, f, spatial), lane(3, GROUP, f // HEAD_DIM, HEAD_DIM + 16, spatial), lane(GROUP, f, spatial),
@@ -737,7 +794,7 @@
         lane(rows, f), lane(GROUP, f, spatial), pltpu.VMEM((rows, f), F32), lane(rows, f),
         lane(rows, hidden), lane(rows, hidden), lane(rows, f),
         lane(2, rows, f), lane(2, 3, rows, 2 * f), lane(7, f, spatial),
-    ] + [dma] * 8 + [pltpu.SemaphoreType.DMA((n,)) for n in (3, 4, 2)]
+    ] + [dma] * 8 + [pltpu.SemaphoreType.DMA((n,)) for n in (3, 4, 2, lanes // 2)]
     sems = pltpu.SemaphoreType.DMA((96,))
     scratch += [
         lane(f, hidden), lane(3, f // 2, hidden), lane(3, f // 4, hidden),
@@ -747,7 +804,7 @@
     return pl.pallas_call(
         functools.partial(layer_kernel, lanes, spatial, f, hidden, tm_count, clip_count),
         in_specs=[smem, hbm, hbm] + [hbm if w.ndim == 2 else vmem for w in weights],
-        out_specs=[hbm, vmem, hbm, vmem],
+        out_specs=[hbm, hbm, hbm, vmem],
         out_shape=[whole] * 2 + [jax.ShapeDtypeStruct((3, f, hidden), BF16), jax.ShapeDtypeStruct((16, f), F32)],
         scratch_shapes=scratch,
         name="layer",
@@ -773,30 +830,23 @@
         lanes, spatial, f, hidden, tm_count, lax.axis_size("clip"), lane_frames,
         tokens.transpose(0, 2, 1, 3), cotangent.transpose(0, 2, 1, 3), weights,
     )
-    part = 32
-    steps = max(-(-spatial // part), 2 * f // TALL)
-    turn = lambda i: jnp.minimum(i, -(-spatial // part) - 1)
-    tall = lambda i: jnp.minimum(i // 2, f // TALL - 1)
-    lane_block = pl.BlockSpec((1, lanes, part, f), lambda i: (0, 0, turn(i), 0))
-    token_block = pl.BlockSpec((1, part, lanes, f), lambda i: (0, turn(i), 0, 0))
-    row_block = lambda n: pl.BlockSpec((TALL, n), lambda i: (tall(i), 0))
-    vector = lambda n: pl.BlockSpec((n,), lambda i: (0,))
+    vmem, hbm = pl.BlockSpec(memory_space=pltpu.VMEM), pl.BlockSpec(memory_space=pl.ANY)
     sizes = [f] * 7 + [hidden, f]
+    wide = ((f, 3 * f), (f, f), (f, hidden), (hidden, f))
+    dma = lambda *n: pltpu.SemaphoreType.DMA(n)
     got = pl.pallas_call(
         finish_kernel,
-        grid=(steps,),
-        in_specs=[
-            lane_block, lane_block, pl.BlockSpec((3, TALL, hidden), lambda i: (0, tall(i), 0)),
-            pl.BlockSpec((16, f), lambda i: (0, 0)),
-        ],
-        out_specs=[
-            token_block, token_block, row_block(3 * f), row_block(f), row_block(hidden),
-            pl.BlockSpec((hidden, TALL), lambda i: (0, tall(i))),
-        ] + [vector(n) for n in sizes],
+        in_specs=[hbm] * 3 + [vmem],
+        out_specs=[hbm] * 6 + [vmem] * len(sizes),
         out_shape=[jax.ShapeDtypeStruct((1, spatial, lanes, f), BF16)] * 2
-        + [jax.ShapeDtypeStruct(n, F32) for n in ((f, 3 * f), (f, f), (f, hidden), (hidden, f))]
+        + [jax.ShapeDtypeStruct(n, F32) for n in wide]
         + [jax.ShapeDtypeStruct((n,), F32) for n in sizes],
+        scratch_shapes=[
+            pltpu.VMEM((2, lanes, spatial, f), BF16), pltpu.VMEM((2, spatial, lanes, f), BF16),
+            pltpu.VMEM((3, f, hidden), BF16),
+        ] + [pltpu.VMEM(n, F32) for n in wide] + [dma(2, 3), dma(3), dma(2, 3), dma(4)],
         name="finish",
+        compiler_params=pltpu.CompilerParams(vmem_limit_bytes=63 * 1024 * 1024),
     )(out, input_grad, gathered, small)
     out, input_grad = (v.transpose(0, 2, 1, 3) for v in got[:2])
     g_project, g_out, g_up, g_down = got[2:6]

time: 245 us -> 233 us (0.951)
  Pallas kernels: 244 us -> 232 us
    pallas_call x1, Pallas kernels: 233 us -> 224 us  [layer_call(): pl.pallas_call(functools.partial(layer_kernel, lanes, spatial, f, hidden,...]
    pallas_call x1, Pallas kernels: 11.8 us -> 8.03 us  [body(): pl.pallas_call(finish_kernel, in_specs=[hbm] * 3 + [vmem], out_specs=[hbm...]
where the time goes in v7:
time: 233 us
  Pallas kernels  232 us (100%)
    pallas_call x1, Pallas kernels, layer_call(): pl.pallas_call(functools.partial(layer_kernel, lanes, spatial, f, hidden,...  224 us
    pallas_call x1, Pallas kernels, body(): pl.pallas_call(finish_kernel, in_specs=[hbm] * 3 + [vmem], out_specs=[hbm...  8.03 us

profile of v7, /device:TPU:0, one launch (start us, length us, event | category | flops | bytes accessed | tf_op | source)
XLA Modules:
  0.0 232.6 jit_solution(12025777542491442341)
XLA Ops:
  0.7 223.8 %layer.1 = (bf16[1,16,196,384]{3,2,1,0:T(8,128)(2,1)}, bf16[1,16,196,384]{3,2,1,0:T(8,128)(2,1)}, bf16[3,384,1536]{2,1,0:T(8,128)(2,1)}, f32[16,384]{1,0:T(8,128)}) custom-call(s32[16]{0:T(128)} %frames_ref.1, bf16[1,196,16,384]{3,2,1,0:T(8,128)(2,1)} %bitcast.4, bf16[1,196,16,384]{3,2,1,0:T(8,128)(2,1)} %bitcast.5, bf16[384]{0:T(512)(128)(2,1)} %pre_gain_ref.1, ...), custom_call_target="tpu_custom_call" | custom-call | flops 99999997952 | bytes 40000000 | tf_op jit(solution)/shard_map/layer/pallas_call | solution.py:804
  224.4 8.0 %finish.1 = (bf16[1,196,16,384]{3,2,1,0:T(8,128)(2,1)}, bf16[1,196,16,384]{3,2,1,0:T(8,128)(2,1)}, f32[384,1152]{1,0:T(8,128)}, f32[384,384]{1,0:T(8,128)}, f32[...) custom-call(bf16[1,16,196,384]{3,2,1,0:T(8,128)(2,1)} %get-tuple-ele, ...), custom_call_target="tpu_custom_call" | custom-call | tf_op jit(solution)/shard_map/finish/pallas_call | solution.py:837

commit v8 on v7

--- a/solution.py
+++ b/solution.py
@@ -63,6 +63,19 @@
     (W, 5), (UP, 6), (DOWN, 6), (W, 6), (UP, 7), (DOWN, 7), (W, 7), ("trade", 4, "join"), ("lanes", 4), ("lanes", 5), (UP, 8), (DOWN, 8),
     (W, 8),
 ]
+
+
+class Several:
+    def __init__(self, copies):
+        self.copies = list(copies)
+
+    def start(self):
+        for copy in self.copies:
+            copy.start()
+
+    def wait(self):
+        for copy in self.copies:
+            copy.wait()
 
 
 class Reduction:
@@ -301,6 +314,9 @@
     out_bias, down_bias, up_bias = row(out_bias_ref), row(down_bias_ref), row(up_bias_ref)
     query_bias, value_bias = row(query_bias_ref), row(value_bias_ref)
 
+    def lane_of(g, j):
+        return 4 * (g // 2) + (1 - g % 2) * 3 * j + g % 2 * (1 + j)
+
     def full_lane(l):
         return frames_ref[l] > 0
 
@@ -359,7 +375,10 @@
         pl.semaphore_signal(barrier, inc=1, device_id={"clip": across[m]}, device_id_type=MESH)
 
     def store(g):
-        return pltpu.make_async_copy(out_s.at[g % 2], out_hbm.at[0, pl.ds(g * GROUP, GROUP)], out_sems.at[g % 2])
+        return Several(
+            pltpu.make_async_copy(out_s.at[g % 2, j], out_hbm.at[0, lane_of(g, j)], out_sems.at[g % 2, j])
+            for j in range(GROUP)
+        )
 
     for start, count in cuts:
         raw_copy(tok_hbm, start, count).wait()
@@ -368,16 +387,19 @@
         raw_copy(cot_hbm, start, count).start()
     pl.semaphore_wait(barrier, len(others) + len(masks))
 
-    def start_tokens(pair, carry):
-        for l in (2 * pair, 2 * pair + 1):
-            xhat, _ = normalise(tok_s[l].astype(F32))
-            gl_s[l] = (xhat * pre_gain + pre_bias).astype(BF16)
-        for l in (2 * pair, 2 * pair + 1):
-            pl.when(has_up(l))(lambda: rising(l).start())
-            pl.when(has_low(l))(lambda: falling(l).start())
+    def start_tokens(block, carry):
+        for l in range(WRAP):
+            xhat, _ = normalise(tok_s[WRAP * block + l].astype(F32))
+            gl_s[WRAP * block + l] = (xhat * pre_gain + pre_bias).astype(BF16)
+        for g in range(2):
+            for j in range(GROUP):
+                k = WRAP * block + lane_of(g, j)
+                inner_low, inner_up = lane_of(g, j) != 0, lane_of(g, j) != WRAP - 1
+                pl.when(tm < last if not inner_low else tm >= 0)(lambda: rising(k - step_up).start())
+                pl.when(tm > 0 if not inner_up else tm >= 0)(lambda: falling(k + step_down).start())
         return carry
 
-    lax.fori_loop(0, lanes // 2, start_tokens, 0)
+    lax.fori_loop(0, lanes // WRAP, start_tokens, 0)
     for start, count in cuts:
         raw_copy(cot_hbm, start, count).wait()
         cot_s[:, start : start + count, :] = jnp.transpose(raw_s[start : start + count], (1, 0, 2))
@@ -428,12 +450,12 @@
                 sums.step(a, n)
 
     def group(index, carry):
-        base = index * GROUP
         slot = index % 2
+        mine = [lane_of(index, j) for j in range(GROUP)]
         pl.when(index >= 2)(lambda: store(index - 2).wait())
 
         def arrive(j, carry):
-            l = base + j
+            l = lane_of(index, j)
             pl.when(has_low(l))(lambda: copy(gl_s.at[l], low_s.at[l], send_up.at[l], recv_low.at[l], lower).wait_recv())
             pl.when(has_up(l))(lambda: copy(gl_s.at[l], up_s.at[l], send_down.at[l], recv_up.at[l], higher).wait_recv())
             return carry
@@ -452,7 +474,7 @@
             return jnp.concatenate([value, zero_half] if h % 2 == 0 else [zero_half, value], 0)
 
         def project(j, s):
-            n1 = (low_s, gl_s, up_s)[s][base + j]
+            n1 = (low_s, gl_s, up_s)[s][mine[j]]
             n1_s[slot, s, rows_of(j), :] = n1
             kv = dot(n1, w_project_ref[:, f:])
             k = kv[:, :f].astype(BF16)
@@ -470,7 +492,7 @@
             return [dot(k_s[s, j, :, pair_of(h)], qz) for s in range(3)]
 
         def attend(j, h, scores):
-            low_ok, up_ok = joined(base + j)
+            low_ok, up_ok = joined(mine[j])
             low_far, up_far = jnp.where(low_ok, 0.0, FAR), jnp.where(up_ok, 0.0, FAR)
             tops = [jnp.max(x, 0, keepdims=True) for x in scores]
             top = jnp.maximum(jnp.maximum(tops[0] - low_far, tops[2] - up_far), tops[1])
@@ -501,10 +523,10 @@
             attend(j, h, scores)
             if h == heads - 1:
                 att_s[rows_of(j), :] = attt_s[j].T
-                res_s[rows_of(j), :] = tok_s[base + j].astype(F32)
+                res_s[rows_of(j), :] = tok_s[mine[j]].astype(F32)
 
         def sent(j, carry):
-            l = base + j
+            l = lane_of(index, j)
             pl.when(has_up(l))(lambda: rising(l).wait_send())
             pl.when(has_low(l))(lambda: falling(l).wait_send())
             return carry
@@ -516,8 +538,8 @@
         xhat2, rate2 = normalise(residual)
         n2_s[...] = (xhat2 * mid_gain + mid_bias).astype(BF16)
         for j in range(GROUP):
-            full = full_lane(base + j)
-            g = cot_s[base + j]
+            full = full_lane(mine[j])
+            g = cot_s[mine[j]]
             dao_s[pl.ds(j * pad, spatial), :] = jnp.where(full, g.astype(F32), 0.0).astype(BF16)
 
         wide = 256
@@ -532,7 +554,7 @@
             a_upb[:, cols] += column_sum(gh)
             return carry
 
-        before, _, _ = project_back(1 - slot, jnp.maximum(base - GROUP, 0))
+        before, _, _ = project_back(1 - slot, jnp.maximum(index - 1, 0))
         chunks = hidden // wide
         for c in range(chunks):
             mlp(c, 0)
@@ -544,16 +566,16 @@
         grad_n2 = dot(gh_s[...], w_up_ref[...], NT)
         in_last(index, (1, 0), (2, 0))
         for j in range(GROUP):
-            full = full_lane(base + j)
-            mine = total_out[j * pad : j * pad + spatial]
-            out_s[slot, j] = jnp.where(full, mine, tok_s[base + j].astype(F32)).astype(BF16)
+            full = full_lane(mine[j])
+            rows_out = total_out[j * pad : j * pad + spatial]
+            out_s[slot, j] = jnp.where(full, rows_out, tok_s[mine[j]].astype(F32)).astype(BF16)
         store(index).start()
         g = dao_s[...].astype(F32)
         xhat2, rate2 = normalise(res_s[...])
         dres = g + norm_back(grad_n2, xhat2, rate2, mid_gain)
         for j in range(GROUP):
-            straight = jnp.where(full_lane(base + j), 0.0, cot_s[base + j].astype(F32))
-            own_s[base + j] = (dres[j * pad : j * pad + spatial] + straight).astype(BF16)
+            straight = jnp.where(full_lane(mine[j]), 0.0, cot_s[mine[j]].astype(F32))
+            own_s[mine[j]] = (dres[j * pad : j * pad + spatial] + straight).astype(BF16)
         dao = dres.astype(BF16)
         dao_s[...] = dao
         a_small[3:4, :] += column_sum(dao.astype(F32))
@@ -573,19 +595,19 @@
             return dh, delta, [dot(v_s[s, j, :, pair_of(h)], dz) for s in range(3)]
 
         def attend_back(j, h, dh, delta, grad_probs):
-            mine = mine_of(h)
-            qh = qt_s[j, mine, :]
+            place = mine_of(h)
+            qh = qt_s[j, place, :]
             probs = [p_s[j, h, s] for s in range(3)]
             for s in range(3):
-                dt_s[4 + s, mine, :] = dot(dh, probs[s], NT).astype(BF16)
+                dt_s[4 + s, place, :] = dot(dh, probs[s], NT).astype(BF16)
             ds = [(probs[s].astype(F32) * (grad_probs[s] - delta)).astype(BF16) for s in range(3)]
             for s in range(3):
-                dt_s[1 + s, mine, :] = dot(qh, ds[s], NT).astype(BF16)
+                dt_s[1 + s, place, :] = dot(qh, ds[s], NT).astype(BF16)
             grad_q = None
             for s in range(3):
-                got = dot(kt_s[s, j, mine, :], ds[s])
+                got = dot(kt_s[s, j, place, :], ds[s])
                 grad_q = got if grad_q is None else grad_q + got
-            dt_s[0, mine, :] = (grad_q * HEAD_DIM ** (-0.5)).astype(BF16)
+            dt_s[0, place, :] = (grad_q * HEAD_DIM ** (-0.5)).astype(BF16)
 
         dts = [start_back(j) for j in range(GROUP)]
         later = prepare(0, 0, dts[0])
@@ -603,10 +625,10 @@
                     dkv_s[slot, s, rows_of(j), f:] = dt_s[4 + s].T
 
         in_last(index, (1, 2), (2, 2))
-        pl.when(jnp.logical_and(index > 0, index < groups - LATE + 1))(lambda: give_back(base - GROUP))
+        pl.when(jnp.logical_and(index > 0, index < groups - LATE + 1))(lambda: give_back(index - 1))
         return carry
 
-    def project_back(side, base):
+    def project_back(side, g):
         def weights_q():
             dq = dq_s[side]
             a_w[:, :f] += dot(n1_s[side, 1], dq, TN)
@@ -623,14 +645,14 @@
                 grad += dot(dq_s[side, rows_of(j), :], w_project_ref[:, :f], NT)
             a_small[0:1, :] += column_sum(grad * n1_s[side, s, rows_of(j), :].astype(F32))
             a_small[1:2, :] += column_sum(grad)
-            (gl_s, low_s, up_s)[s][base + j] = grad.astype(BF16)
+            (gl_s, low_s, up_s)[s][lane_of(g, j)] = grad.astype(BF16)
 
         rows_work = [functools.partial(rows_back, j, s) for j in range(GROUP) for s in range(3)]
         return [weights_q] + rows_work[:3] + [weights_kv] + rows_work[3:], [weights_q, weights_kv], rows_work
 
-    def give_back(base):
+    def give_back(g):
         def one(j, carry):
-            l = base + j
+            l = lane_of(g, j)
             pl.when(has_low(l))(lambda: returning_low(l).start())
             pl.when(has_up(l))(lambda: returning_up(l).start())
             return carry
@@ -638,20 +660,22 @@
         lax.fori_loop(0, GROUP, one, 0)
 
     lax.fori_loop(0, lanes // GROUP, group, 0)
-    _, final_weights, final_rows = project_back((lanes // GROUP - 1) % 2, lanes - GROUP)
+    _, final_weights, final_rows = project_back((lanes // GROUP - 1) % 2, lanes // GROUP - 1)
     for work in final_weights:
         work()
 
     def hand_over(pair):
-        place = pl.ds(2 * pair, 2)
-        return pltpu.make_async_copy(own_s.at[place], grad_hbm.at[0, place], own_sems.at[pair])
+        return Several(
+            pltpu.make_async_copy(own_s.at[l], grad_hbm.at[0, l], own_sems.at[l])
+            for l in (lane_of(pair, 0), lane_of(pair, 1))
+        )
 
     def handed_over(pair, carry):
         hand_over(pair).wait()
         return carry
 
     def conclude(pair, carry):
-        for l in (2 * pair, 2 * pair + 1):
+        for l in (lane_of(pair, 0), lane_of(pair, 1)):
 
             @pl.when(has_up(l))
             def _(l=l):
@@ -663,7 +687,7 @@
                 returning_low(l).wait_send()
                 copy(up_s.at[l], below_s.at[l], send_gu.at[l], recv_below.at[l], lower).wait_recv()
 
-        for l in (2 * pair, 2 * pair + 1):
+        for l in (lane_of(pair, 0), lane_of(pair, 1)):
             grad = low_s[l].astype(F32) + above_s[l].astype(F32) + below_s[l].astype(F32)
             xhat, rate = normalise(tok_s[l].astype(F32))
             own_s[l] = (norm_back(grad, xhat, rate, pre_gain) + own_s[l].astype(F32)).astype(BF16)
@@ -685,7 +709,7 @@
                 work()
         elif what[0] == "give":
             for i in range(LATE, 0, -1):
-                give_back(lanes - i * GROUP)
+                give_back(lanes // GROUP - i)
         elif what[0] == "trade":
             sums.trade(what[1], what[2])
         else:
@@ -794,7 +818,9 @@
         lane(rows, f), lane(GROUP, f, spatial), pltpu.VMEM((rows, f), F32), lane(rows, f),
         lane(rows, hidden), lane(rows, hidden), lane(rows, f),
         lane(2, rows, f), lane(2, 3, rows, 2 * f), lane(7, f, spatial),
-    ] + [dma] * 8 + [pltpu.SemaphoreType.DMA((n,)) for n in (3, 4, 2, lanes // 2)]
+    ] + [dma] * 8 + [pltpu.SemaphoreType.DMA((n,)) for n in (3, 4)] + [
+        pltpu.SemaphoreType.DMA((2, GROUP)), pltpu.SemaphoreType.DMA((lanes,))
+    ]
     sems = pltpu.SemaphoreType.DMA((96,))
     scratch += [
         lane(f, hidden), lane(3, f // 2, hidden), lane(3, f // 4, hidden),

time: 233 us -> 231 us (level)
  Pallas kernels: 232 us -> 229 us
    pallas_call x1, Pallas kernels: 224 us -> 221 us  [layer_call(): pl.pallas_call(functools.partial(layer_kernel, lanes, spatial, f, hidden,...]
where the time goes in v8:
time: 231 us; the launch traced here: 230 us
  Pallas kernels  229 us (99%)
    pallas_call x1, Pallas kernels, layer_call(): pl.pallas_call(functools.partial(layer_kernel, lanes, spatial, f, hidden,...  221 us
    pallas_call x1, Pallas kernels, body(): pl.pallas_call(finish_kernel, in_specs=[hbm] * 3 + [vmem], out_specs=[hbm...  8.03 us

profile of v8, /device:TPU:0, one launch (start us, length us, event | category | flops | bytes accessed | tf_op | source)
XLA Modules:
  0.0 230.1 jit_solution(16607518159316363495)
XLA Ops:
  0.7 221.2 %layer.1 = (bf16[1,16,196,384]{3,2,1,0:T(8,128)(2,1)}, bf16[1,16,196,384]{3,2,1,0:T(8,128)(2,1)}, bf16[3,384,1536]{2,1,0:T(8,128)(2,1)}, f32[16,384]{1,0:T(8,128)}) custom-call(s32[16]{0:T(128)} %frames_ref.1, bf16[1,196,16,384]{3,2,1,0:T(8,128)(2,1)} %bitcast.4, bf16[1,196,16,384]{3,2,1,0:T(8,128)(2,1)} %bitcast.5, bf16[384]{0:T(512)(128)(2,1)} %pre_gain_ref.1, ...), custom_call_target="tpu_custom_call" | custom-call | flops 99999997952 | bytes 40000000 | tf_op jit(solution)/shard_map/layer/pallas_call | solution.py:830
  221.9 8.0 %finish.1 = (bf16[1,196,16,384]{3,2,1,0:T(8,128)(2,1)}, bf16[1,196,16,384]{3,2,1,0:T(8,128)(2,1)}, f32[384,1152]{1,0:T(8,128)}, f32[384,384]{1,0:T(8,128)}, f32[...) custom-call(bf16[1,16,196,384]{3,2,1,0:T(8,128)(2,1)} %get-tuple-ele, ...), custom_call_target="tpu_custom_call" | custom-call | tf_op jit(solution)/shard_map/finish/pallas_call | solution.py:863

commit v9 on v8

--- a/solution.py
+++ b/solution.py
@@ -315,7 +315,9 @@
     query_bias, value_bias = row(query_bias_ref), row(value_bias_ref)
 
     def lane_of(g, j):
-        return 4 * (g // 2) + (1 - g % 2) * 3 * j + g % 2 * (1 + j)
+        four, blocks = g // 2, lanes // 4
+        inner = (g + (four + blocks - 1) // blocks) % 2
+        return 4 * four + (1 - inner) * 3 * j + inner * (1 + j)
 
     def full_lane(l):
         return frames_ref[l] > 0
@@ -387,11 +389,11 @@
         raw_copy(cot_hbm, start, count).start()
     pl.semaphore_wait(barrier, len(others) + len(masks))
 
-    def start_tokens(block, carry):
+    def start_tokens(block, carry, order=(1, 0)):
         for l in range(WRAP):
             xhat, _ = normalise(tok_s[WRAP * block + l].astype(F32))
             gl_s[WRAP * block + l] = (xhat * pre_gain + pre_bias).astype(BF16)
-        for g in range(2):
+        for g in order:
             for j in range(GROUP):
                 k = WRAP * block + lane_of(g, j)
                 inner_low, inner_up = lane_of(g, j) != 0, lane_of(g, j) != WRAP - 1
@@ -399,7 +401,8 @@
                 pl.when(tm > 0 if not inner_up else tm >= 0)(lambda: falling(k + step_down).start())
         return carry
 
-    lax.fori_loop(0, lanes // WRAP, start_tokens, 0)
+    start_tokens(0, 0, (0, 1))
+    lax.fori_loop(1, lanes // WRAP, start_tokens, 0)
     for start, count in cuts:
         raw_copy(cot_hbm, start, count).wait()
         cot_s[:, start : start + count, :] = jnp.transpose(raw_s[start : start + count], (1, 0, 2))
@@ -525,14 +528,7 @@
                 att_s[rows_of(j), :] = attt_s[j].T
                 res_s[rows_of(j), :] = tok_s[mine[j]].astype(F32)
 
-        def sent(j, carry):
-            l = lane_of(index, j)
-            pl.when(has_up(l))(lambda: rising(l).wait_send())
-            pl.when(has_low(l))(lambda: falling(l).wait_send())
-            return carry
-
-        lax.fori_loop(0, GROUP, sent, 0)
-
+        pl.when(index > 0)(lambda: sent(index - 1))
         residual = res_s[...] + dot(att_s[...], w_out_ref[...]) + out_bias
         res_s[...] = residual
         xhat2, rate2 = normalise(residual)
@@ -554,7 +550,7 @@
             a_upb[:, cols] += column_sum(gh)
             return carry
 
-        before, _, _ = project_back(1 - slot, jnp.maximum(index - 1, 0))
+        before, _, _ = project_back(1 - slot, jnp.maximum(index - 1, 0), index > 0)
         chunks = hidden // wide
         for c in range(chunks):
             mlp(c, 0)
@@ -628,7 +624,16 @@
         pl.when(jnp.logical_and(index > 0, index < groups - LATE + 1))(lambda: give_back(index - 1))
         return carry
 
-    def project_back(side, g):
+    def sent(g):
+        def one(j, carry):
+            l = lane_of(g, j)
+            pl.when(has_up(l))(lambda: rising(l).wait_send())
+            pl.when(has_low(l))(lambda: falling(l).wait_send())
+            return carry
+
+        lax.fori_loop(0, GROUP, one, 0)
+
+    def project_back(side, g, real=True):
         def weights_q():
             dq = dq_s[side]
             a_w[:, :f] += dot(n1_s[side, 1], dq, TN)
@@ -645,7 +650,10 @@
                 grad += dot(dq_s[side, rows_of(j), :], w_project_ref[:, :f], NT)
             a_small[0:1, :] += column_sum(grad * n1_s[side, s, rows_of(j), :].astype(F32))
             a_small[1:2, :] += column_sum(grad)
-            (gl_s, low_s, up_s)[s][lane_of(g, j)] = grad.astype(BF16)
+            place = lane_of(g, j)
+            if s == 0:
+                place = jnp.where(real, place, lanes + j)
+            (gl_s, low_s, up_s)[s][place] = grad.astype(BF16)
 
         rows_work = [functools.partial(rows_back, j, s) for j in range(GROUP) for s in range(3)]
         return [weights_q] + rows_work[:3] + [weights_kv] + rows_work[3:], [weights_q, weights_kv], rows_work
@@ -663,6 +671,7 @@
     _, final_weights, final_rows = project_back((lanes // GROUP - 1) % 2, lanes // GROUP - 1)
     for work in final_weights:
         work()
+    sent(groups - 1)
 
     def hand_over(pair):
         return Several(
@@ -808,7 +817,7 @@
     lane = lambda *s: pltpu.VMEM(s, BF16)
     dma = pltpu.SemaphoreType.DMA((lanes,))
     scratch = sums + [
-        lane(lanes, spatial, f), lane(lanes, spatial, f), lane(lanes, spatial, f), lane(lanes, spatial, f),
+        lane(lanes, spatial, f), lane(lanes, spatial, f), lane(lanes + GROUP, spatial, f), lane(lanes, spatial, f),
         lane(lanes, spatial, f),
         lane(lanes, spatial, f), lane(spatial, lanes, f), lane(lanes, spatial, f), lane(lanes, spatial, f), lane(2, GROUP, spatial, f),
         lane(f, 3 * f), lane(f, f), lane(f, hidden), lane(hidden, f),

time: 231 us -> 233 us (level)
  Pallas kernels: 229 us -> 232 us
    pallas_call x1, Pallas kernels: 221 us -> 224 us  [layer_call(): pl.pallas_call(functools.partial(layer_kernel, lanes, spatial, f, hidden,...]
where the time goes in v9:
time: 233 us
  Pallas kernels  232 us (100%)
    pallas_call x1, Pallas kernels, layer_call(): pl.pallas_call(functools.partial(layer_kernel, lanes, spatial, f, hidden,...  224 us
    pallas_call x1, Pallas kernels, body(): pl.pallas_call(finish_kernel, in_specs=[hbm] * 3 + [vmem], out_specs=[hbm...  8.03 us

profile of v9, /device:TPU:0, one launch (start us, length us, event | category | flops | bytes accessed | tf_op | source)
XLA Modules:
  0.0 232.9 jit_solution(16250106322707629989)
XLA Ops:
  0.7 224.0 %layer.1 = (bf16[1,16,196,384]{3,2,1,0:T(8,128)(2,1)}, bf16[1,16,196,384]{3,2,1,0:T(8,128)(2,1)}, bf16[3,384,1536]{2,1,0:T(8,128)(2,1)}, f32[16,384]{1,0:T(8,128)}) custom-call(s32[16]{0:T(128)} %frames_ref.1, bf16[1,196,16,384]{3,2,1,0:T(8,128)(2,1)} %bitcast.4, bf16[1,196,16,384]{3,2,1,0:T(8,128)(2,1)} %bitcast.5, bf16[384]{0:T(512)(128)(2,1)} %pre_gain_ref.1, ...), custom_call_target="tpu_custom_call" | custom-call | flops 99999997952 | bytes 40000000 | tf_op jit(solution)/shard_map/layer/pallas_call | solution.py:839
  224.7 8.0 %finish.1 = (bf16[1,196,16,384]{3,2,1,0:T(8,128)(2,1)}, bf16[1,196,16,384]{3,2,1,0:T(8,128)(2,1)}, f32[384,1152]{1,0:T(8,128)}, f32[384,384]{1,0:T(8,128)}, f32[...) custom-call(bf16[1,16,196,384]{3,2,1,0:T(8,128)(2,1)} %get-tuple-ele, ...), custom_call_target="tpu_custom_call" | custom-call | tf_op jit(solution)/shard_map/finish/pallas_call | solution.py:872
